TPU v7x, 32 devices: a whole 2x2x4 slice. The times are simulated.
32 devices in a mesh: rows: 32 (over z, y, x, core), cols: 1.
Axes of the slice: x: 2, y: 2, z: 4, core: 2. Of those that a mesh axis runs over, the one named last changes fastest.
Arguments:
- slab: bfloat16 [4096, 4096], P('rows', 'cols'), may hold values from -6 to 6
- cross: bfloat16 [4096, 128], P('rows', 'cols'), may hold values from 0 to 6, as said below
- obs_index: int32 [128], replicated, may hold values from 0 to 4095, as said below
- noise: float32 [128], replicated, may hold values from 0.25 to 2
Outputs:
- posterior: bfloat16 [4096, 4096], P('rows', 'cols')
Inputs may be any that keep to these rules, and one draw needn't show every extreme that they name: `obs_index`: the 128 segments are distinct. Split the segments into blocks of 128 in order: a quarter of the blocks hold exactly 12 inspected segments, a quarter hold 4, the rest none. `cross`: innovation is positive definite.
All inputs are finite; a program needn't handle non-finite values.
Results may differ from a plain program's by a relative error of at most 0.0099.
Values may be sent and summed in bfloat16 or wider, within the bound.
No kernel may reach another device: no remote copies, remote signals or barrier semaphores. Data moves between devices by JAX's collectives and lax.ppermute only.
A program may use at most 64 MiB of HBM per device.

v0:
```python
import jax
import jax.numpy as jnp
from jax import lax
from jax.sharding import PartitionSpec as P

CAP = 12


def solve_gain(factor, right_side):
    forward = lax.linalg.triangular_solve(factor, right_side, left_side=True, lower=True)
    return lax.linalg.triangular_solve(
        factor, forward, left_side=True, lower=True, transpose_a=True
    )


def make_factor(picked_half, noise):
    picked = lax.all_gather(picked_half, "cols", axis=1, tiled=True).astype(jnp.float32)
    innovation = 0.5 * (picked + picked.T) + jnp.diag(noise)
    return jnp.linalg.cholesky(innovation)


def body(slab, cross, obs_index, noise):
    row_count = slab.shape[0]
    groups = lax.axis_size("rows")
    owners = obs_index // row_count
    local_row = obs_index % row_count
    owner_hit = (owners[:, None] == jnp.arange(groups, dtype=jnp.int32)[None, :]).astype(jnp.int32)
    before = jnp.cumsum(owner_hit, axis=0) - owner_hit
    slot_rank = jnp.sum(before * owner_hit, axis=1)
    mine = owners == lax.axis_index("rows")
    slot_hit = (
        mine[:, None] & (slot_rank[:, None] == jnp.arange(CAP, dtype=jnp.int32)[None, :])
    ).astype(jnp.bfloat16)
    row_hit = (local_row[:, None] == jnp.arange(row_count, dtype=jnp.int32)[None, :]).astype(
        jnp.bfloat16
    )
    selector = jnp.dot(slot_hit.T, row_hit, preferred_element_type=jnp.float32).astype(jnp.bfloat16)
    packed_cross = jnp.dot(selector, cross, preferred_element_type=jnp.float32).astype(jnp.bfloat16)
    packed_slab = jnp.dot(selector, slab, preferred_element_type=jnp.float32).astype(jnp.bfloat16)
    placed = owners * CAP + slot_rank
    all_cross, all_slab = (
        lax.all_gather(packed_cross, "rows", axis=0, tiled=True),
        lax.all_gather(packed_slab, "rows", axis=0, tiled=True),
    )
    factor = make_factor(all_cross[placed], noise)
    observed = all_slab[placed].astype(jnp.float32)
    gain = solve_gain(factor, observed).astype(jnp.bfloat16)
    update = jnp.dot(
        lax.all_gather(cross, "cols", axis=1, tiled=True), gain, preferred_element_type=jnp.float32
    )
    return (slab.astype(jnp.float32) - update).astype(jnp.bfloat16)


def solution(mesh):
    return jax.shard_map(
        body,
        mesh=mesh,
        in_specs=(P("rows", "cols"), P("rows", "cols"), P(), P()),
        out_specs=P("rows", "cols"),
        check_vma=False,
    )
```

profile of v0, /device:TPU:0, one launch (start us, length us, event | category | flops | bytes accessed | tf_op | source)
XLA Modules:
  0.0 98.9 jit_solution(18207353720528968413)
XLA Ops:
  6.5 0.0 copy-start
  6.5 0.0 all-gather.4.cloned.1.call-start
  6.5 0.8 and_select_fusion
  7.3 0.7 broadcast_compare_fusion
  8.0 0.1 fusion.9
  8.1 0.2 reduce_window_sum.11
  8.2 0.2 select_reduce_fusion.1
  8.4 0.3 convolution_convert_fusion.3
  8.7 2.2 %fusion.2 = bf16[1,12,4096]{2,1,0:T(8,128)(2,1)} fusion(bf16[12,128]{1,0:T(8,128)(2,1)S(1)} %convolution_convert_fusion.3, bf16[128,4096]{1,0:T(8,128)(2,1)} %param.4), kind=kOutput, calls=%fused_computation.7 | convolution fusion | flops 12632064 | bytes 1149952 | tf_op jit(solution)/shard_map/dot_general | solution.py:39
  10.8 0.0 all-gather.4.cloned.1.call-update
  10.8 0.0 copy-done.2
  10.9 1.3 %copy.13 = bf16[128,4096]{0,1:T(8,128)(2,1)} copy(bf16[128,4096]{1,0:T(8,128)(2,1)S(1)} %copy-done.2) | data formatting | bytes 2097152 | tf_op args[0]
  12.2 0.0 copy-done
  12.2 0.1 fusion.3
  12.3 43.6 %all-gather = bf16[32,12,128]{2,1,0:T(8,128)(2,1)S(1)} all-gather(bf16[1,12,128]{2,1,0:T(8,128)(2,1)S(1)} %fusion.3), channel_id=1, replica_groups=mesh['rows'=32,'cols'=1] {'rows'}, dimensions={0}, use_global_device_ids=true | all-gather | bytes 101376 | tf_op jit(solution)/shard_map/all_gather | solution.py:42
  55.9 0.7 gather_fusion
  56.7 0.1 copy.14
  56.8 0.1 copy.15
  56.9 0.0 copy-done.3
  56.9 0.1 add_multiply_fusion
  57.0 11.7 %cholesky.16 = f32[128,128]{1,0:T(8,128)S(1)} custom-call(f32[128,128]{1,0:T(8,128)S(1)} %add_multiply_fusion), custom_call_target="Cholesky" | custom-call | tf_op jit(solution)/shard_map/jit(cholesky)/cholesky | solution.py:19
  68.7 0.7 compare_reduce_fusion
  69.4 0.6 fusion.4
  70.1 9.8 %custom-call.8 = f32[1,128,128]{1,2,0:T(8,128)S(1)} custom-call(f32[1,128,128]{2,1,0:T(8,128)S(1)} %fusion.4), custom_call_target="InvertDiagBlocksLowerTriangular" | custom-call | tf_op jit(solution)/shard_map/triangular_solve | solution.py:11
  79.9 0.0 all-gather.4.cloned.1.call-done
  79.9 4.0 %reshape.37 = bf16[384,4096]{1,0:T(8,128)(2,1)S(1)} reshape(bf16[32,12,4096]{2,1,0:T(8,128)(2,1)} %all-gather.4.cloned.1.call-done) | data formatting | bytes 6291456
  83.9 2.2 %gather_fusion.1 = bf16[128,4096]{1,0:T(8,128)(2,1)} fusion(bf16[384,4096]{1,0:T(8,128)(2,1)S(1)} %reshape.37, s32[1024]{0:T(1024)S(1)} %pad_clamp_fusion), kind=kCustom, calls=%fused_computation.1 | custom fusion | bytes 2097664 | tf_op jit(solution)/shard_map/gather | solution.py:46
  86.0 2.3 %fusion.6 = f32[128,4096]{1,0:T(8,128)S(1)} fusion(bf16[128,4096]{1,0:T(8,128)(2,1)} %gather_fusion.1, f32[1,128,128]{1,2,0:T(8,128)S(1)} %custom-call.8), kind=kOutput, calls=%fused_computation.14 | convolution fusion | flops 805306368 | bytes 3211264 | tf_op jit(solution)/shard_map/triangular_solve | solution.py:10
  88.3 0.0 copy-start.1
  88.3 1.9 %convolution_convert_fusion = bf16[128,4096]{1,0:T(8,128)(2,1)S(1)} fusion(f32[128,4096]{1,0:T(8,128)S(1)} %fusion.6, f32[1,128,128]{1,2,0:T(8,128)S(1)} %custom-call.8), kind=kOutput, calls=%fused_computation.5 | convolution fusion | flops 805830656 | bytes 3211264 | tf_op jit(solution)/shard_map/triangular_solve | solution.py:11
  90.2 0.5 fusion.1
  90.7 1.3 %copy.16 = bf16[128,4096]{1,0:T(8,128)(2,1)} copy(bf16[128,4096]{0,1:T(8,128)(2,1)S(1)} %fusion.1) | data formatting | bytes 2097152 | tf_op jit(solution)/shard_map/convert_element_type | solution.py:51
  (7 shorter events, 0.1 us)
Async XLA Ops:
  6.5 5.7 %copy-start = (bf16[128,128]{1,0:T(8,128)(2,1)S(1)}, bf16[128,128]{1,0:T(8,128)(2,1)}, u32[]{:S(2)}) copy-start(bf16[128,128]{1,0:T(8,128)(2,1)} %param.5) | copy-start | bytes 98308
  6.5 4.3 %copy-start.2 = (bf16[128,4096]{1,0:T(8,128)(2,1)S(1)}, bf16[128,4096]{1,0:T(8,128)(2,1)}, u32[]{:S(2)}) copy-start(bf16[128,4096]{1,0:T(8,128)(2,1)} %param.4) | copy-start | bytes 3145732
  6.5 73.4 %all-gather.4.cloned.1.call-start = ((), (), s32[]{:S(2)}) async-start(), calls=%async_computation | async-start | bytes 4325376 | tf_op jit(solution)/shard_map/all_gather | solution.py:43
  8.7 48.2 %copy-start.3 = (f32[128]{0:T(128)S(1)}, f32[128]{0:T(128)}, u32[]{:S(2)}) copy-start(f32[128]{0:T(128)} %param.7) | copy-start | bytes 1540
  88.3 1.9 %copy-start.1 = (bf16[128,4096]{0,1:T(8,128)(2,1)S(1)}, bf16[128,4096]{0,1:T(8,128)(2,1)}, u32[]{:S(2)}) copy-start(bf16[128,4096]{0,1:T(8,128)(2,1)} %copy.13) | copy-start | bytes 3145732
Sparse Core Ops, SparseCore 0:
  11.0 65.2 all-gather.3
where the time goes:
time: 99.2 us; the launch traced here: 98.9 us
  blocking collectives  43.6 us (44%)
  other arithmetic  24.8 us (25%)
  between operations  13.5 us (14%)
  local copies, waits for them, and re-layouts  9.76 us (10%)
  matrix products  7.17 us (7%)
    all_gather x1, blocking collectives, body(): lax.all_gather(packed_cross, 'rows', axis=0, tiled=True)  43.6 us
    another operation x3, other arithmetic, make_factor(): return jnp.linalg.cholesky(innovation)  12.4 us
    another operation x2, other arithmetic, solve_gain(): lax.linalg.triangular_solve(factor, forward, left_side=True, lower=True,...  10.5 us
    unnamed x11, local copies, waits for them, and re-layouts  5.35 us
    another operation x1, matrix products, solve_gain(): lax.linalg.triangular_solve(factor, right_side, left_side=True, lower=True)  2.26 us
    gather x1, local copies, waits for them, and re-layouts, body(): observed = all_slab[placed].astype(jnp.float32)  2.16 us
    dot_general x1, matrix products, body(): jnp.dot(selector, slab, preferred_element_type=jnp.float32)  2.15 us
  transfers between devices with their start and end apart: 1, of which 0 were waited for; matrix products, arithmetic and copies ran while one was open for 26% of the time, Pallas kernels for 0%

commit v1 on v0

--- a/solution.py
+++ b/solution.py
@@ -1,9 +1,20 @@
+import functools
+
 import jax
 import jax.numpy as jnp
 from jax import lax
+from jax.experimental import pallas as pl
+from jax.experimental.pallas import tpu as pltpu
 from jax.sharding import PartitionSpec as P
 
 CAP = 12
+SLOTS = 16
+PLANE = 8
+VMEM = pl.BlockSpec(memory_space=pltpu.VMEM)
+
+
+def dot32(a, b):
+    return jnp.dot(a, b, preferred_element_type=jnp.float32)
 
 
 def solve_gain(factor, right_side):
@@ -19,7 +30,7 @@
     return jnp.linalg.cholesky(innovation)
 
 
-def body(slab, cross, obs_index, noise):
+def general_body(slab, cross, obs_index, noise):
     row_count = slab.shape[0]
     groups = lax.axis_size("rows")
     owners = obs_index // row_count
@@ -34,9 +45,9 @@
     row_hit = (local_row[:, None] == jnp.arange(row_count, dtype=jnp.int32)[None, :]).astype(
         jnp.bfloat16
     )
-    selector = jnp.dot(slot_hit.T, row_hit, preferred_element_type=jnp.float32).astype(jnp.bfloat16)
-    packed_cross = jnp.dot(selector, cross, preferred_element_type=jnp.float32).astype(jnp.bfloat16)
-    packed_slab = jnp.dot(selector, slab, preferred_element_type=jnp.float32).astype(jnp.bfloat16)
+    selector = dot32(slot_hit.T, row_hit).astype(jnp.bfloat16)
+    packed_cross = dot32(selector, cross).astype(jnp.bfloat16)
+    packed_slab = dot32(selector, slab).astype(jnp.bfloat16)
     placed = owners * CAP + slot_rank
     all_cross, all_slab = (
         lax.all_gather(packed_cross, "rows", axis=0, tiled=True),
@@ -45,15 +56,238 @@
     factor = make_factor(all_cross[placed], noise)
     observed = all_slab[placed].astype(jnp.float32)
     gain = solve_gain(factor, observed).astype(jnp.bfloat16)
-    update = jnp.dot(
-        lax.all_gather(cross, "cols", axis=1, tiled=True), gain, preferred_element_type=jnp.float32
-    )
+    update = dot32(lax.all_gather(cross, "cols", axis=1, tiled=True), gain)
     return (slab.astype(jnp.float32) - update).astype(jnp.bfloat16)
 
 
+def spread_index(obs_ref, rows):
+    count = obs_ref.shape[1]
+    along = jnp.broadcast_to(obs_ref[...], (count, count))
+    down = along.astype(jnp.float32).T.astype(jnp.int32)
+    earlier_row = lax.broadcasted_iota(jnp.int32, (count, count), 0)
+    earlier_col = lax.broadcasted_iota(jnp.int32, (count, count), 1)
+    same = along // rows == down // rows
+    rank_along = jnp.sum(
+        jnp.where(same & (earlier_row < earlier_col), 1.0, 0.0), axis=0, keepdims=True
+    ).astype(jnp.int32)
+    rank_down = jnp.sum(
+        jnp.where(same & (earlier_col < earlier_row), 1.0, 0.0), axis=1, keepdims=True
+    ).astype(jnp.int32)
+    return along, down, rank_along, rank_down
+
+
+def pick_kernel(groups, width, obs_ref, slab_ref, cross_ref, out_ref):
+    rows, count = slab_ref.shape[0], obs_ref.shape[1]
+    me = lax.axis_index("rows")
+    along, down, rank, _ = spread_index(obs_ref, rows)
+    picks = 4 * SLOTS
+    slot = lax.broadcasted_iota(jnp.int32, (picks, count), 0)
+    within, part = slot % SLOTS, slot // SLOTS
+    wanted = jnp.where(
+        part == 0,
+        jnp.where(within < CAP, within, -1),
+        jnp.where(within >= CAP, 4 * (part - 1) + within - CAP, -1),
+    )
+    mine = (along[:1] // rows) == me
+    hit = jnp.where(mine & (rank == wanted), 1.0, 0.0).astype(jnp.bfloat16)
+    local = lax.broadcasted_iota(jnp.int32, (count, rows), 1) == down[:, :rows] % rows
+    selector = dot32(hit, jnp.where(local, 1.0, 0.0).astype(jnp.bfloat16)).astype(jnp.bfloat16)
+    cross_part = dot32(selector[:SLOTS], cross_ref[...]).astype(jnp.bfloat16)
+    lanes = width // 4
+    for group in range(PLANE):
+        got = dot32(selector, slab_ref[:, group * width : (group + 1) * width])
+        tail = got[:, 3 * lanes :]
+        block = jnp.concatenate(
+            [
+                (
+                    got[:SLOTS, t * lanes : (t + 1) * lanes]
+                    + tail[(t + 1) * SLOTS : (t + 2) * SLOTS]
+                ).astype(jnp.bfloat16)
+                for t in range(3)
+            ]
+            + [cross_part],
+            axis=1,
+        )
+        for level in range(groups // PLANE):
+            at = (level * PLANE + group) * SLOTS
+            out_ref[at : at + SLOTS, :] = block
+
+
+def compact_kernel(rows, obs_ref, noise_ref, got_ref, a_ref, b_ref, inn_ref):
+    count, slots = obs_ref.shape[1], got_ref.shape[0]
+    lanes = got_ref.shape[1] // 4
+    _, down, _, rank = spread_index(obs_ref, rows)
+    owner = down[:, :1] // rows
+    lane = lax.broadcasted_iota(jnp.int32, (count, slots), 1)
+    within = lane % SLOTS
+    owned = owner == lane // SLOTS
+
+    def one_hot(hit):
+        return jnp.where(owned & hit, 1.0, 0.0).astype(jnp.bfloat16)
+
+    head = dot32(one_hot(rank == within), got_ref[...])
+    tail = jnp.zeros((count, lanes), jnp.float32)
+    for t in range(3):
+        hit = one_hot((within >= CAP) & (rank == within + (4 * t - CAP)))
+        tail += dot32(hit, got_ref[:, t * lanes : (t + 1) * lanes])
+    a_ref[...] = head[:, : 2 * lanes].astype(jnp.bfloat16)
+    b_ref[:, :lanes] = head[:, 2 * lanes : 3 * lanes].astype(jnp.bfloat16)
+    b_ref[:, lanes:] = tail.astype(jnp.bfloat16)
+    picked = head[:, 3 * lanes :]
+    diagonal = lax.broadcasted_iota(jnp.int32, (count, count), 0) == lax.broadcasted_iota(
+        jnp.int32, (count, count), 1
+    )
+    inn_ref[...] = 0.5 * (picked + picked.T) + jnp.where(diagonal, noise_ref[...], 0.0)
+
+
+def invert_kernel(inn_ref, out_ref):
+    size = inn_ref.shape[0]
+    step, panels = 8, size // 8
+    full = (step, size)
+    m = [inn_ref[i * step : (i + 1) * step, :] for i in range(panels)]
+    sub = lax.broadcasted_iota(jnp.int32, full, 0)
+    lane = lax.broadcasted_iota(jnp.int32, full, 1)
+    for p in range(panels):
+        at = p * step
+        on = lane == sub + at
+        row = m[p]
+        spread = [jnp.broadcast_to(row[:, at + k : at + k + 1], full) for k in range(step)]
+        e = {}
+        for i in range(step):
+            for k in range(i + 1):
+                e[i, k] = jnp.broadcast_to(spread[k][i : i + 1, :], full)
+        get = lambda i, k: e[max(i, k), min(i, k)]
+        for k in range(step):
+            d = 1.0 / e[k, k]
+            col = {i: get(i, k) for i in range(step) if i != k}
+            scaled = {i: v * d for i, v in col.items()}
+            for i in range(step):
+                for j in range(i + 1):
+                    if i != k and j != k:
+                        e[i, j] = e[i, j] - scaled[i] * col[j]
+            for i, v in scaled.items():
+                e[max(i, k), min(i, k)] = v
+            e[k, k] = -d
+        less = row - jnp.where(on, 1.0, 0.0)
+        rows_b = [jnp.broadcast_to(less[k : k + 1, :], full) for k in range(step)]
+        q = []
+        for i in range(step):
+            terms = [get(i, k) * rows_b[k] for k in range(step)]
+            while len(terms) > 1:
+                terms = [x + y for x, y in zip(terms[::2], terms[1::2])]
+            q.append(terms[0])
+        for i in range(panels):
+            base = less if i == p else m[i]
+            cols = (
+                [jnp.broadcast_to(base[:, at + k : at + k + 1], full) for k in range(step)]
+            )
+            terms = [cols[k] * q[k] for k in range(step)]
+            while len(terms) > 1:
+                terms = [x + y for x, y in zip(terms[::2], terms[1::2])]
+            m[i] = m[i] + terms[0]
+            if i == p:
+                m[i] = m[i] - jnp.where(on, 2.0, 0.0)
+    for i in range(0, panels, 2):
+        x = -jnp.concatenate([m[i], m[i + 1]], axis=0)
+        for part in range(3):
+            piece = x.astype(jnp.bfloat16)
+            out_ref[i * step : (i + 2) * step, part * size : (part + 1) * size] = piece
+            x = x - piece.astype(jnp.float32)
+
+
+def update_kernel(width, inverse_ref, cross_ref, slab_ref, *refs):
+    pieces, out_ref, held, sem = refs[:8], refs[8], refs[9], refs[10]
+    me = lax.axis_index("rows")
+    half = width // 2
+    inverse, cross = inverse_ref[...], cross_ref[...]
+    size = inverse.shape[0]
+    y, x, core = 4, 2, 1
+    flips = ((0, y), (x, x + y), (0, x), (y, x + y))
+    copies = []
+    for other in range(2):
+        for which in range(4):
+            for k in range(2):
+                owner = ((me % PLANE) ^ flips[which][k]) ^ (core * other)
+                at = owner * width + (which // 2) * half
+                at = pl.multiple_of(at, half)
+                obs = pieces[other * 4 + which][k]
+                gain = sum(
+                    dot32(inverse[:, t * size : (t + 1) * size], obs) for t in range(3)
+                ).astype(jnp.bfloat16)
+                new = slab_ref[:, pl.ds(at, half)].astype(jnp.float32) - dot32(cross, gain)
+                index = len(copies)
+                held[index] = new.astype(jnp.bfloat16)
+                copy = pltpu.make_async_copy(
+                    held.at[index], out_ref.at[:, pl.ds(at, half)], sem.at[index]
+                )
+                copy.start()
+                copies.append(copy)
+    for copy in copies:
+        copy.wait()
+
+
+def plane_body(slab, cross, obs_index, noise):
+    groups = lax.axis_size("rows")
+    rows, columns = slab.shape
+    count = cross.shape[1]
+    width = columns // PLANE
+    half = width // 2
+    obs = obs_index.reshape(1, count)
+    picked = pl.pallas_call(
+        functools.partial(pick_kernel, groups, width),
+        out_shape=jax.ShapeDtypeStruct((groups * SLOTS, 3 * width // 4 + count), jnp.bfloat16),
+        in_specs=[VMEM] * 3,
+        out_specs=VMEM,
+        name="pick",
+    )(obs, slab, cross)
+    got = lax.all_to_all(
+        picked.reshape(groups, SLOTS, -1), "rows", split_axis=0, concat_axis=0, tiled=True
+    ).reshape(groups * SLOTS, -1)
+    block = jax.ShapeDtypeStruct((count, half), jnp.bfloat16)
+    a0, b0, innovation = pl.pallas_call(
+        functools.partial(compact_kernel, rows),
+        out_shape=(block, block, jax.ShapeDtypeStruct((count, count), jnp.float32)),
+        in_specs=[VMEM] * 3,
+        out_specs=(VMEM,) * 3,
+        name="compact",
+    )(obs, noise.reshape(1, count), got)
+    inverse = pl.pallas_call(
+        invert_kernel,
+        out_shape=jax.ShapeDtypeStruct((count, 3 * count), jnp.bfloat16),
+        in_specs=[VMEM],
+        out_specs=VMEM,
+        cost_estimate=pl.CostEstimate(
+            flops=2 * count**3, bytes_accessed=4 * count * count, transcendentals=count
+        ),
+        name="invert",
+    )(innovation)
+
+    def swap(value, bit):
+        return lax.ppermute(value, "rows", [(i, i ^ bit) for i in range(groups)])
+
+    y, x, core = 4, 2, 1
+    a1, b1 = swap(a0, y), swap(b0, x)
+    a01, b01 = jnp.stack([a0, a1]), jnp.stack([b0, b1])
+    a23, b23 = swap(a01, x), swap(b01, y)
+    own = (a01, a23, b01, b23)
+    other = tuple(swap(v, core) for v in own)
+    return pl.pallas_call(
+        functools.partial(update_kernel, width),
+        out_shape=jax.ShapeDtypeStruct(slab.shape, jnp.bfloat16),
+        in_specs=[VMEM] * 11,
+        out_specs=pl.BlockSpec(memory_space=pl.ANY),
+        scratch_shapes=[
+            pltpu.VMEM((16, rows, half), jnp.bfloat16),
+            pltpu.SemaphoreType.DMA((16,)),
+        ],
+        name="update",
+    )(inverse, cross, slab, *own, *other)
+
+
 def solution(mesh):
+    plane = mesh.shape["cols"] == 1 and mesh.shape["rows"] == 4 * PLANE
     return jax.shard_map(
-        body,
+        plane_body if plane else general_body,
         mesh=mesh,
         in_specs=(P("rows", "cols"), P("rows", "cols"), P(), P()),
         out_specs=P("rows", "cols"),

time: 99.2 us -> 54.3 us (0.55)
  other arithmetic: 24.8 us -> 0.9 us
  blocking collectives: 43.6 us -> 23 us
  Pallas kernels: 0 us -> 17.7 us
  between operations: 13.5 us -> 0.1 us
  local copies, waits for them, and re-layouts: 9.76 us -> 1.37 us
  matrix products: 7.17 us -> 0 us
  starting transfers between devices: 0.01 us -> 5.47 us
  waiting for transfers between devices: 0.04 us -> 5.35 us
    all_gather x1 -> x0, blocking collectives: 43.6 us -> none  [body(): lax.all_gather(packed_cross, 'rows', axis=0, tiled=True)]
    all_to_all x0 -> x1, blocking collectives: none -> 23 us  [plane_body(): lax.all_to_all(picked.reshape(groups, SLOTS, -1), 'rows', split_axis=0, c...]
    another operation x6 -> x2, other arithmetic: 23 us -> 0.9 us  [plane_body(): a01, b01 = (jnp.stack([a0, a1]), jnp.stack([b0, b1]))]
    pallas_call x0 -> x4, Pallas kernels: none -> 17.7 us  [the longest x1 6.56 us: plane_body(): pl.pallas_call(functools.partial(update_kernel, width), out_shape=jax.Sha...]
    ppermute x0 -> x8, starting transfers between devices: none -> 5.47 us  [swap(): return lax.ppermute(value, 'rows', [(i, i ^ bit) for i in range(groups)])]
    ppermute x0 -> x8, waiting for transfers between devices: none -> 5.35 us  [swap(): return lax.ppermute(value, 'rows', [(i, i ^ bit) for i in range(groups)])]
    another operation x2 -> x0, matrix products: 4.16 us -> none  [the longest x1 2.26 us: solve_gain(): lax.linalg.triangular_solve(factor, right_side, left_side=True, lower=True)]
    unnamed x11 -> x18, local copies, waits for them, and re-layouts: 5.35 us -> 1.37 us
  transfers between devices with their start and end apart: 1 -> 8, of which waited for: 0 -> 3; matrix products, arithmetic and copies ran while one was open for 26% -> 2% of each run, Pallas kernels for 0% -> 12%
where the time goes in v1:
time: 54.3 us; the launch traced here: 53.9 us
  blocking collectives  23 us (42%)
  Pallas kernels  17.7 us (33%)
  starting transfers between devices  5.47 us (10%)
  waiting for transfers between devices  5.35 us (10%)
  local copies, waits for them, and re-layouts  1.37 us (3%)
  other arithmetic  0.9 us (2%)
    all_to_all x1, blocking collectives, plane_body(): lax.all_to_all(picked.reshape(groups, SLOTS, -1), 'rows', split_axis=0, c...  23 us
    pallas_call x1, Pallas kernels, plane_body(): pl.pallas_call(functools.partial(update_kernel, width), out_shape=jax.Sha...  6.56 us
    pallas_call x1, Pallas kernels, plane_body(): pl.pallas_call(invert_kernel, out_shape=jax.ShapeDtypeStruct((count, 3 *...  6.32 us
    ppermute x8, starting transfers between devices, swap(): return lax.ppermute(value, 'rows', [(i, i ^ bit) for i in range(groups)])  5.47 us
    ppermute x8, waiting for transfers between devices, swap(): return lax.ppermute(value, 'rows', [(i, i ^ bit) for i in range(groups)])  5.35 us
    pallas_call x1, Pallas kernels, plane_body(): pl.pallas_call(functools.partial(pick_kernel, groups, width), out_shape=j...  2.59 us
    pallas_call x1, Pallas kernels, plane_body(): pl.pallas_call(functools.partial(compact_kernel, rows), out_shape=(block,...  2.27 us
    unnamed x18, local copies, waits for them, and re-layouts  1.37 us
  transfers between devices with their start and end apart: 8, of which 3 were waited for; matrix products, arithmetic and copies ran while one was open for 2% of the time, Pallas kernels for 12%

profile of v1, /device:TPU:0, one launch (start us, length us, event | category | flops | bytes accessed | tf_op | source)
XLA Modules:
  0.0 53.9 jit_solution(17214305000405748313)
XLA Ops:
  0.0 2.6 %pick.1 = bf16[512,512]{1,0:T(8,128)(2,1)} custom-call(s32[1,128]{1,0:T(1,128)} %bitcast.14, bf16[128,4096]{1,0:T(8,128)(2,1)} %slab_ref.3, bf16[128,128]{1,0:T(8,128)(2,1)} %cross_ref.3), custom_call_target="tpu_custom_call" | custom-call | tf_op jit(solution)/shard_map/pick/pallas_call | solution.py:236
  2.6 23.0 %all_to_all.5 = bf16[32,16,512]{2,1,0:T(8,128)(2,1)} all-to-all(bf16[32,16,512]{2,1,0:T(8,128)(2,1)} %bitcast.9), channel_id=1, replica_groups=mesh['rows'=32,'cols'=1] {'rows'}, dimensions={0} | all-to-all | bytes 1048576 | tf_op jit(solution)/shard_map/all_to_all | solution.py:243
  25.5 2.3 %compact.1 = (bf16[128,256]{1,0:T(8,128)(2,1)}, bf16[128,256]{1,0:T(8,128)(2,1)}, f32[128,128]{1,0:T(8,128)}) custom-call(s32[1,128]{1,0:T(1,128)} %bitcast.15, f32[1,128]{1,0:T(1,128)} %bitcast.16, bf16[512,512]{1,0:T(8,128)(2,1)} %bitcast.8), custom_call_target="tpu_custom_call" | custom-call | tf_op jit(solution)/shard_map/compact/pallas_call | solution.py:247
  27.8 1.0 %collective-permute-start.2 = (bf16[128,256]{1,0:T(8,128)(2,1)}, bf16[128,256]{1,0:T(8,128)(2,1)S(1)}, u32[]{:S(2)}, u32[]{:S(2)}) collective-permute-start(bf16[128,256]{1,0:T(8,128)(2,1)} %get-tuple-element.10), channel_id=1, source_target_pairs={{0,2},{1,3},{2,0},{3,1},{4,6},{5,7},{6,4},{7,5},{8,10},{9,11},{10,... | collective-permute-start | bytes 196616 | tf_op jit(solution)/shard_map/ppermute | solution.py:266
  28.8 1.5 %collective-permute-start = (bf16[128,256]{1,0:T(8,128)(2,1)}, bf16[128,256]{1,0:T(8,128)(2,1)S(1)}, u32[]{:S(2)}, u32[]{:S(2)}) collective-permute-start(bf16[128,256]{1,0:T(8,128)(2,1)} %get-tuple-element.9), channel_id=1, source_target_pairs={{0,4},{1,5},{2,6},{3,7},{4,0},{5,1},{6,2},{7,3},{8,12},{9,13},{10,... | collective-permute-start | bytes 196616 | tf_op jit(solution)/shard_map/ppermute | solution.py:266
  30.2 2.1 %collective-permute-done.2 = bf16[128,256]{1,0:T(8,128)(2,1)S(1)} collective-permute-done((bf16[128,256]{1,0:T(8,128)(2,1)}, bf16[128,256]{1,0:T(8,128)(2,1)S(1)}, u32[]{:S(2)}, u32[]{:S(2)}) %collective-permute-start.2) | collective-permute-done | bytes 65568 | tf_op jit(solution)/shard_map/ppermute | solution.py:266
  32.3 0.9 %pad_maximum_fusion.1.refs_2_ = bf16[2,128,256]{2,1,0:T(8,128)(2,1)S(1)} fusion(bf16[1,128,256]{2,1,0:T(8,128)(2,1)S(1)} %bitcast.13, bf16[1,128,256]{2,1,0:T(8,128)(2,1)} %bitcast.11), kind=kLoop, calls=%fused_computation.1 | loop fusion | flops 65536 | bytes 262144 | tf_op jit(solution)/shard_map/stack | solution.py:270
  33.2 0.0 copy-start
  33.2 1.3 %collective-permute-start.3 = (bf16[2,128,256]{2,1,0:T(8,128)(2,1)S(1)}, bf16[2,128,256]{2,1,0:T(8,128)(2,1)S(1)}, u32[]{:S(2)}, u32[]{:S(2)}) collective-permute-start(bf16[2,128,256]{2,1,0:T(8,128)(2,1)S(1)} %pad_maximum_fusion.1.refs_2_), channel_id=1, source_target_pairs={{0,4},{1,5},{2,6},{3,7},{4,0},{5,1},{6,2},{7,3},{8,12},{9,13},{10,... | collective-permute-start | bytes 393224 | tf_op jit(solution)/shard_map/ppermute | solution.py:266
  34.5 0.0 collective-permute-done
  34.5 0.0 copy-done.8
  34.5 0.0 copy-start.1
  34.5 1.2 %collective-permute-start.1 = (bf16[2,128,256]{2,1,0:T(8,128)(2,1)S(1)}, bf16[2,128,256]{2,1,0:T(8,128)(2,1)S(1)}, u32[]{:S(2)}, u32[]{:S(2)}) collective-permute-start(bf16[2,128,256]{2,1,0:T(8,128)(2,1)S(1)} %pad_maximum_fusion.refs_0_), channel_id=1, source_target_pairs={{0,2},{1,3},{2,0},{3,1},{4,6},{5,7},{6,4},{7,5},{8,10},{9,11},{10,... | collective-permute-start | bytes 393224 | tf_op jit(solution)/shard_map/ppermute | solution.py:266
  35.8 0.0 copy-done
  35.8 0.0 collective-permute-start.6
  35.8 0.5 collective-permute-start.4
  36.3 1.9 %collective-permute-done.3.refs_3_ = bf16[2,128,256]{2,1,0:T(8,128)(2,1)S(1)} collective-permute-done((bf16[2,128,256]{2,1,0:T(8,128)(2,1)S(1)}, bf16[2,128,256]{2,1,0:T(8,128)(2,1)S(1)}, u32[]{:S(2)}, u32[]{:S(2)}) %collective-permute-start.3) | collective-permute-done | bytes 131104 | tf_op jit(solution)/shard_map/ppermute | solution.py:266
  38.2 0.0 collective-permute-start.7
  38.2 1.3 %collective-permute-done.1.refs_1_ = bf16[2,128,256]{2,1,0:T(8,128)(2,1)S(1)} collective-permute-done((bf16[2,128,256]{2,1,0:T(8,128)(2,1)S(1)}, bf16[2,128,256]{2,1,0:T(8,128)(2,1)S(1)}, u32[]{:S(2)}, u32[]{:S(2)}) %collective-permute-start.1) | collective-permute-done | bytes 131104 | tf_op jit(solution)/shard_map/ppermute | solution.py:266
  39.6 0.0 collective-permute-start.5
  39.6 6.3 %invert.1.inverse_ref = bf16[128,384]{1,0:T(8,128)(2,1)} custom-call(f32[128,128]{1,0:T(8,128)} %get-tuple-element.8.inn_ref), custom_call_target="tpu_custom_call" | custom-call | flops 4194304 | bytes 65536 | tf_op jit(solution)/shard_map/invert/pallas_call | solution.py:254
  45.9 0.0 collective-permute-done.6.refs_6_
  45.9 0.0 collective-permute-done.4.refs_4_
  45.9 0.0 copy-start.5
  45.9 0.0 collective-permute-done.7.refs_7_
  45.9 0.0 copy-start.6
  45.9 0.0 collective-permute-done.5.refs_5_
  46.0 0.6 %copy-done.4 = bf16[2,128,256]{2,1,0:T(8,128)(2,1)} copy-done((bf16[2,128,256]{2,1,0:T(8,128)(2,1)}, bf16[2,128,256]{2,1,0:T(8,128)(2,1)S(1)}, u32[]{:S(2)}) %copy-start.4) | copy-done | bytes 131096
  46.5 0.1 copy-done.5
  46.6 0.1 copy-done.6
  46.7 0.6 %copy-done.7 = bf16[2,128,256]{2,1,0:T(8,128)(2,1)} copy-done((bf16[2,128,256]{2,1,0:T(8,128)(2,1)}, bf16[2,128,256]{2,1,0:T(8,128)(2,1)S(1)}, u32[]{:S(2)}) %copy-start.7) | copy-done | bytes 131096
  47.3 6.6 %update.1 = bf16[128,4096]{1,0:T(8,128)(2,1)} custom-call(bf16[128,384]{1,0:T(8,128)(2,1)} %invert.1.inverse_ref, bf16[128,128]{1,0:T(8,128)(2,1)} %cross_ref.3, bf16[128,4096]{1,0:T(8,128)(2,1)} %slab_ref.3, bf16[2,128,256]{2,1,0:T(8,128)(2,1)} %copy-done.1, bf16[2,128,256]{2,1,0:T(8,128)(2,1)} %copy-done.3, bf16[2,128,256]{2,1,0:T(8,128)(2,1)} %copy-done, ...), custom_call_target="tpu_custom_call" | custom-call | tf_op jit(solution)/shard_map/update/pallas_call | solution.py:274
  (9 shorter events, 0.0 us)
Async XLA Ops:
  27.8 4.5 %collective-permute-start.2 = (bf16[128,256]{1,0:T(8,128)(2,1)}, bf16[128,256]{1,0:T(8,128)(2,1)S(1)}, u32[]{:S(2)}, u32[]{:S(2)}) collective-permute-start(bf16[128,256]{1,0:T(8,128)(2,1)} %get-tuple-element.10), channel_id=1, source_target_pairs={{0,2},{1,3},{2,0},{3,1},{4,6},{5,7},{6,4},{7,5},{8,10},{9,11},{10,... | collective-permute-start | bytes 196616 | tf_op jit(solution)/shard_map/ppermute | solution.py:266
  28.8 5.7 %collective-permute-start = (bf16[128,256]{1,0:T(8,128)(2,1)}, bf16[128,256]{1,0:T(8,128)(2,1)S(1)}, u32[]{:S(2)}, u32[]{:S(2)}) collective-permute-start(bf16[128,256]{1,0:T(8,128)(2,1)} %get-tuple-element.9), channel_id=1, source_target_pairs={{0,4},{1,5},{2,6},{3,7},{4,0},{5,1},{6,2},{7,3},{8,12},{9,13},{10,... | collective-permute-start | bytes 196616 | tf_op jit(solution)/shard_map/ppermute | solution.py:266
  32.3 2.2 %copy-start.8 = (bf16[128,256]{1,0:T(8,128)(2,1)S(1)}, bf16[128,256]{1,0:T(8,128)(2,1)}, u32[]{:S(2)}) copy-start(bf16[128,256]{1,0:T(8,128)(2,1)} %get-tuple-element.9) | copy-start | bytes 196612
  33.2 2.6 %copy-start = (bf16[2,128,256]{2,1,0:T(8,128)(2,1)}, bf16[2,128,256]{2,1,0:T(8,128)(2,1)S(1)}, u32[]{:S(2)}) copy-start(bf16[2,128,256]{2,1,0:T(8,128)(2,1)S(1)} %pad_maximum_fusion.1.refs_2_) | copy-start | bytes 393220
  33.2 5.0 %collective-permute-start.3 = (bf16[2,128,256]{2,1,0:T(8,128)(2,1)S(1)}, bf16[2,128,256]{2,1,0:T(8,128)(2,1)S(1)}, u32[]{:S(2)}, u32[]{:S(2)}) collective-permute-start(bf16[2,128,256]{2,1,0:T(8,128)(2,1)S(1)} %pad_maximum_fusion.1.refs_2_), channel_id=1, source_target_pairs={{0,4},{1,5},{2,6},{3,7},{4,0},{5,1},{6,2},{7,3},{8,12},{9,13},{10,... | collective-permute-start | bytes 393224 | tf_op jit(solution)/shard_map/ppermute | solution.py:266
  34.5 11.4 %copy-start.1 = (bf16[2,128,256]{2,1,0:T(8,128)(2,1)}, bf16[2,128,256]{2,1,0:T(8,128)(2,1)S(1)}, u32[]{:S(2)}) copy-start(bf16[2,128,256]{2,1,0:T(8,128)(2,1)S(1)} %pad_maximum_fusion.refs_0_) | copy-start | bytes 393220
  34.5 5.0 %collective-permute-start.1 = (bf16[2,128,256]{2,1,0:T(8,128)(2,1)S(1)}, bf16[2,128,256]{2,1,0:T(8,128)(2,1)S(1)}, u32[]{:S(2)}, u32[]{:S(2)}) collective-permute-start(bf16[2,128,256]{2,1,0:T(8,128)(2,1)S(1)} %pad_maximum_fusion.refs_0_), channel_id=1, source_target_pairs={{0,2},{1,3},{2,0},{3,1},{4,6},{5,7},{6,4},{7,5},{8,10},{9,11},{10,... | collective-permute-start | bytes 393224 | tf_op jit(solution)/shard_map/ppermute | solution.py:266
  35.8 10.1 %collective-permute-start.6 = (bf16[2,128,256]{2,1,0:T(8,128)(2,1)S(1)}, bf16[2,128,256]{2,1,0:T(8,128)(2,1)S(1)}, u32[]{:S(2)}, u32[]{:S(2)}) collective-permute-start(bf16[2,128,256]{2,1,0:T(8,128)(2,1)S(1)} %pad_maximum_fusion.1.refs_2_), channel_id=1, source_target_pairs={{0,1},{1,0},{2,3},{3,2},{4,5},{5,4},{6,7},{7,6},{8,9},{9,8},{10,11... | collective-permute-start | bytes 393224 | tf_op jit(solution)/shard_map/ppermute | solution.py:266
  35.8 10.1 %collective-permute-start.4 = (bf16[2,128,256]{2,1,0:T(8,128)(2,1)S(1)}, bf16[2,128,256]{2,1,0:T(8,128)(2,1)S(1)}, u32[]{:S(2)}, u32[]{:S(2)}) collective-permute-start(bf16[2,128,256]{2,1,0:T(8,128)(2,1)S(1)} %pad_maximum_fusion.refs_0_), channel_id=1, source_target_pairs={{0,1},{1,0},{2,3},{3,2},{4,5},{5,4},{6,7},{7,6},{8,9},{9,8},{10,11... | collective-permute-start | bytes 393224 | tf_op jit(solution)/shard_map/ppermute | solution.py:266
  38.2 7.7 %copy-start.2 = (bf16[2,128,256]{2,1,0:T(8,128)(2,1)}, bf16[2,128,256]{2,1,0:T(8,128)(2,1)S(1)}, u32[]{:S(2)}) copy-start(bf16[2,128,256]{2,1,0:T(8,128)(2,1)S(1)} %collective-permute-done.3.refs_3_) | copy-start | bytes 393220
  38.2 7.7 %collective-permute-start.7 = (bf16[2,128,256]{2,1,0:T(8,128)(2,1)S(1)}, bf16[2,128,256]{2,1,0:T(8,128)(2,1)S(1)}, u32[]{:S(2)}, u32[]{:S(2)}) collective-permute-start(bf16[2,128,256]{2,1,0:T(8,128)(2,1)S(1)} %collective-permute-done.3.refs_3_), channel_id=1, source_target_pairs={{0,1},{1,0},{2,3},{3,2},{4,5},{5,4},{6,7},{7,6},{8,9},{9,8},{10,11... | collective-permute-start | bytes 393224 | tf_op jit(solution)/shard_map/ppermute | solution.py:266
  39.6 6.4 %copy-start.3 = (bf16[2,128,256]{2,1,0:T(8,128)(2,1)}, bf16[2,128,256]{2,1,0:T(8,128)(2,1)S(1)}, u32[]{:S(2)}) copy-start(bf16[2,128,256]{2,1,0:T(8,128)(2,1)S(1)} %collective-permute-done.1.refs_1_) | copy-start | bytes 393220
  39.6 6.4 %collective-permute-start.5 = (bf16[2,128,256]{2,1,0:T(8,128)(2,1)S(1)}, bf16[2,128,256]{2,1,0:T(8,128)(2,1)S(1)}, u32[]{:S(2)}, u32[]{:S(2)}) collective-permute-start(bf16[2,128,256]{2,1,0:T(8,128)(2,1)S(1)} %collective-permute-done.1.refs_1_), channel_id=1, source_target_pairs={{0,1},{1,0},{2,3},{3,2},{4,5},{5,4},{6,7},{7,6},{8,9},{9,8},{10,11... | collective-permute-start | bytes 393224 | tf_op jit(solution)/shard_map/ppermute | solution.py:266
  45.9 0.6 %copy-start.4 = (bf16[2,128,256]{2,1,0:T(8,128)(2,1)}, bf16[2,128,256]{2,1,0:T(8,128)(2,1)S(1)}, u32[]{:S(2)}) copy-start(bf16[2,128,256]{2,1,0:T(8,128)(2,1)S(1)} %collective-permute-done.6.refs_6_) | copy-start | bytes 393220
  45.9 0.7 %copy-start.5 = (bf16[2,128,256]{2,1,0:T(8,128)(2,1)}, bf16[2,128,256]{2,1,0:T(8,128)(2,1)S(1)}, u32[]{:S(2)}) copy-start(bf16[2,128,256]{2,1,0:T(8,128)(2,1)S(1)} %collective-permute-done.4.refs_4_) | copy-start | bytes 393220
  45.9 0.7 %copy-start.6 = (bf16[2,128,256]{2,1,0:T(8,128)(2,1)}, bf16[2,128,256]{2,1,0:T(8,128)(2,1)S(1)}, u32[]{:S(2)}) copy-start(bf16[2,128,256]{2,1,0:T(8,128)(2,1)S(1)} %collective-permute-done.7.refs_7_) | copy-start | bytes 393220
  46.7 0.7 %copy-start.7 = (bf16[2,128,256]{2,1,0:T(8,128)(2,1)}, bf16[2,128,256]{2,1,0:T(8,128)(2,1)S(1)}, u32[]{:S(2)}) copy-start(bf16[2,128,256]{2,1,0:T(8,128)(2,1)S(1)} %collective-permute-done.5.refs_5_) | copy-start | bytes 393220

commit v2 on v1

--- a/solution.py
+++ b/solution.py
@@ -10,7 +10,14 @@
 CAP = 12
 SLOTS = 16
 PLANE = 8
+PARTS = 3
 VMEM = pl.BlockSpec(memory_space=pltpu.VMEM)
+HBM = pl.BlockSpec(memory_space=pltpu.HBM)
+MIB = 1 << 20
+
+
+def room(mib):
+    return pltpu.CompilerParams(vmem_limit_bytes=mib * MIB)
 
 
 def dot32(a, b):
@@ -76,9 +83,22 @@
     return along, down, rank_along, rank_down
 
 
-def pick_kernel(groups, width, obs_ref, slab_ref, cross_ref, out_ref):
-    rows, count = slab_ref.shape[0], obs_ref.shape[1]
+def pick_kernel(groups, width, obs_hbm, slab_hbm, cross_hbm, out_ref, obs_ref, slab, cross, sem):
+    rows, count = slab.shape[0], obs_ref.shape[1]
+
+    def fetch(source, target, index):
+        copy = pltpu.make_async_copy(source, target, sem.at[index])
+        copy.start()
+        return copy
+
+    def columns(ref, group):
+        return ref.at[:, group * width : (group + 1) * width]
+
+    got_obs = fetch(obs_hbm, obs_ref, PLANE)
+    got_slab = [fetch(columns(slab_hbm, g), columns(slab, g), g) for g in range(PLANE)]
+    got_cross = fetch(cross_hbm, cross, PLANE + 1)
     me = lax.axis_index("rows")
+    got_obs.wait()
     along, down, rank, _ = spread_index(obs_ref, rows)
     picks = 4 * SLOTS
     slot = lax.broadcasted_iota(jnp.int32, (picks, count), 0)
@@ -92,10 +112,12 @@
     hit = jnp.where(mine & (rank == wanted), 1.0, 0.0).astype(jnp.bfloat16)
     local = lax.broadcasted_iota(jnp.int32, (count, rows), 1) == down[:, :rows] % rows
     selector = dot32(hit, jnp.where(local, 1.0, 0.0).astype(jnp.bfloat16)).astype(jnp.bfloat16)
-    cross_part = dot32(selector[:SLOTS], cross_ref[...]).astype(jnp.bfloat16)
+    got_cross.wait()
+    cross_part = dot32(selector[:SLOTS], cross[...]).astype(jnp.bfloat16)
     lanes = width // 4
     for group in range(PLANE):
-        got = dot32(selector, slab_ref[:, group * width : (group + 1) * width])
+        got_slab[group].wait()
+        got = dot32(selector, slab[:, group * width : (group + 1) * width])
         tail = got[:, 3 * lanes :]
         block = jnp.concatenate(
             [
@@ -113,31 +135,39 @@
             out_ref[at : at + SLOTS, :] = block
 
 
-def compact_kernel(rows, obs_ref, noise_ref, got_ref, a_ref, b_ref, inn_ref):
-    count, slots = obs_ref.shape[1], got_ref.shape[0]
-    lanes = got_ref.shape[1] // 4
+def order_kernel(rows, obs_ref, noise_ref, order_ref, diagonal_ref):
+    count, slots = obs_ref.shape[1], order_ref.shape[1]
     _, down, _, rank = spread_index(obs_ref, rows)
     owner = down[:, :1] // rows
     lane = lax.broadcasted_iota(jnp.int32, (count, slots), 1)
     within = lane % SLOTS
     owned = owner == lane // SLOTS
-
-    def one_hot(hit):
-        return jnp.where(owned & hit, 1.0, 0.0).astype(jnp.bfloat16)
-
-    head = dot32(one_hot(rank == within), got_ref[...])
+    for t in range(4):
+        hit = (
+            rank == within
+            if t == 0
+            else (within >= CAP) & (rank == within + (4 * (t - 1) - CAP))
+        )
+        order_ref[t * count : (t + 1) * count, :] = jnp.where(owned & hit, 1.0, 0.0).astype(
+            jnp.bfloat16
+        )
+    square = (count, count)
+    on = lax.broadcasted_iota(jnp.int32, square, 0) == lax.broadcasted_iota(jnp.int32, square, 1)
+    diagonal_ref[...] = jnp.where(on, noise_ref[...], 0.0)
+
+
+def compact_kernel(order_ref, diagonal_ref, got_ref, observed_ref, inn_ref):
+    count = diagonal_ref.shape[0]
+    lanes = got_ref.shape[1] // 4
+    head = dot32(order_ref[:count, :], got_ref[...])
     tail = jnp.zeros((count, lanes), jnp.float32)
     for t in range(3):
-        hit = one_hot((within >= CAP) & (rank == within + (4 * t - CAP)))
+        hit = order_ref[(t + 1) * count : (t + 2) * count, :]
         tail += dot32(hit, got_ref[:, t * lanes : (t + 1) * lanes])
-    a_ref[...] = head[:, : 2 * lanes].astype(jnp.bfloat16)
-    b_ref[:, :lanes] = head[:, 2 * lanes : 3 * lanes].astype(jnp.bfloat16)
-    b_ref[:, lanes:] = tail.astype(jnp.bfloat16)
+    observed_ref[:, : 3 * lanes] = head[:, : 3 * lanes].astype(jnp.bfloat16)
+    observed_ref[:, 3 * lanes :] = tail.astype(jnp.bfloat16)
     picked = head[:, 3 * lanes :]
-    diagonal = lax.broadcasted_iota(jnp.int32, (count, count), 0) == lax.broadcasted_iota(
-        jnp.int32, (count, count), 1
-    )
-    inn_ref[...] = 0.5 * (picked + picked.T) + jnp.where(diagonal, noise_ref[...], 0.0)
+    inn_ref[...] = 0.5 * (picked + picked.T) + diagonal_ref[...]
 
 
 def invert_kernel(inn_ref, out_ref):
@@ -189,39 +219,30 @@
                 m[i] = m[i] - jnp.where(on, 2.0, 0.0)
     for i in range(0, panels, 2):
         x = -jnp.concatenate([m[i], m[i + 1]], axis=0)
-        for part in range(3):
+        for part in range(PARTS):
             piece = x.astype(jnp.bfloat16)
-            out_ref[i * step : (i + 2) * step, part * size : (part + 1) * size] = piece
+            at = part * size + i * step
+            out_ref[at : at + 2 * step, :] = piece
             x = x - piece.astype(jnp.float32)
 
 
-def update_kernel(width, inverse_ref, cross_ref, slab_ref, *refs):
-    pieces, out_ref, held, sem = refs[:8], refs[8], refs[9], refs[10]
-    me = lax.axis_index("rows")
-    half = width // 2
+def update_kernel(width, flips, inverse_ref, cross_ref, slab_ref, *refs):
+    pieces, (out_ref, held, sem) = refs[: len(flips)], refs[-3:]
+    place = lax.axis_index("rows") % PLANE
     inverse, cross = inverse_ref[...], cross_ref[...]
-    size = inverse.shape[0]
-    y, x, core = 4, 2, 1
-    flips = ((0, y), (x, x + y), (0, x), (y, x + y))
+    size = cross.shape[1]
     copies = []
-    for other in range(2):
-        for which in range(4):
-            for k in range(2):
-                owner = ((me % PLANE) ^ flips[which][k]) ^ (core * other)
-                at = owner * width + (which // 2) * half
-                at = pl.multiple_of(at, half)
-                obs = pieces[other * 4 + which][k]
-                gain = sum(
-                    dot32(inverse[:, t * size : (t + 1) * size], obs) for t in range(3)
-                ).astype(jnp.bfloat16)
-                new = slab_ref[:, pl.ds(at, half)].astype(jnp.float32) - dot32(cross, gain)
-                index = len(copies)
-                held[index] = new.astype(jnp.bfloat16)
-                copy = pltpu.make_async_copy(
-                    held.at[index], out_ref.at[:, pl.ds(at, half)], sem.at[index]
-                )
-                copy.start()
-                copies.append(copy)
+    for index, flip in enumerate(flips):
+        at = pl.multiple_of((place ^ flip) * width, width)
+        parts = dot32(inverse, pieces[index][...])
+        gain = sum(parts[t * size : (t + 1) * size] for t in range(PARTS)).astype(jnp.bfloat16)
+        new = slab_ref[:, pl.ds(at, width)].astype(jnp.float32) - dot32(cross, gain)
+        held[index] = new.astype(jnp.bfloat16)
+        copies.append(
+            pltpu.make_async_copy(held.at[index], out_ref.at[:, pl.ds(at, width)], sem.at[index])
+        )
+    for copy in copies:
+        copy.start()
     for copy in copies:
         copy.wait()
 
@@ -231,57 +252,91 @@
     rows, columns = slab.shape
     count = cross.shape[1]
     width = columns // PLANE
-    half = width // 2
     obs = obs_index.reshape(1, count)
     picked = pl.pallas_call(
         functools.partial(pick_kernel, groups, width),
         out_shape=jax.ShapeDtypeStruct((groups * SLOTS, 3 * width // 4 + count), jnp.bfloat16),
-        in_specs=[VMEM] * 3,
+        in_specs=[HBM] * 3,
         out_specs=VMEM,
+        scratch_shapes=[
+            pltpu.VMEM((1, count), jnp.int32),
+            pltpu.VMEM(slab.shape, jnp.bfloat16),
+            pltpu.VMEM(cross.shape, jnp.bfloat16),
+            pltpu.SemaphoreType.DMA((PLANE + 2,)),
+        ],
+        compiler_params=room(56),
         name="pick",
     )(obs, slab, cross)
+    order, diagonal = pl.pallas_call(
+        functools.partial(order_kernel, rows),
+        out_shape=(
+            jax.ShapeDtypeStruct((4 * count, groups * SLOTS), jnp.bfloat16),
+            jax.ShapeDtypeStruct((count, count), jnp.float32),
+        ),
+        in_specs=[VMEM] * 2,
+        out_specs=(VMEM,) * 2,
+        cost_estimate=pl.CostEstimate(
+            flops=1000 * count**3, bytes_accessed=4 * count * count, transcendentals=0
+        ),
+        compiler_params=room(8),
+        name="order",
+    )(obs, noise.reshape(1, count))
     got = lax.all_to_all(
         picked.reshape(groups, SLOTS, -1), "rows", split_axis=0, concat_axis=0, tiled=True
     ).reshape(groups * SLOTS, -1)
-    block = jax.ShapeDtypeStruct((count, half), jnp.bfloat16)
-    a0, b0, innovation = pl.pallas_call(
-        functools.partial(compact_kernel, rows),
-        out_shape=(block, block, jax.ShapeDtypeStruct((count, count), jnp.float32)),
+    observed, innovation = pl.pallas_call(
+        compact_kernel,
+        out_shape=(
+            jax.ShapeDtypeStruct((count, width), jnp.bfloat16),
+            jax.ShapeDtypeStruct((count, count), jnp.float32),
+        ),
         in_specs=[VMEM] * 3,
-        out_specs=(VMEM,) * 3,
+        out_specs=(VMEM,) * 2,
+        compiler_params=room(8),
         name="compact",
-    )(obs, noise.reshape(1, count), got)
+    )(order, diagonal, got)
     inverse = pl.pallas_call(
         invert_kernel,
-        out_shape=jax.ShapeDtypeStruct((count, 3 * count), jnp.bfloat16),
+        out_shape=jax.ShapeDtypeStruct((PARTS * count, count), jnp.bfloat16),
         in_specs=[VMEM],
         out_specs=VMEM,
         cost_estimate=pl.CostEstimate(
-            flops=2 * count**3, bytes_accessed=4 * count * count, transcendentals=count
+            flops=3000 * count**3, bytes_accessed=4 * count * count, transcendentals=count
         ),
+        compiler_params=room(4),
         name="invert",
     )(innovation)
 
     def swap(value, bit):
         return lax.ppermute(value, "rows", [(i, i ^ bit) for i in range(groups)])
 
+    def update(inverse, flips, pieces, before):
+        more = () if before is None else (before,)
+        return pl.pallas_call(
+            functools.partial(update_kernel, width, flips),
+            out_shape=jax.ShapeDtypeStruct(slab.shape, jnp.bfloat16),
+            in_specs=[VMEM] * (3 + len(pieces)) + [HBM] * len(more),
+            out_specs=HBM,
+            scratch_shapes=[
+                pltpu.VMEM((len(flips), rows, width), jnp.bfloat16),
+                pltpu.SemaphoreType.DMA((len(flips),)),
+            ],
+            input_output_aliases={3 + len(pieces): 0} if more else {},
+            compiler_params=room(8),
+            name="update",
+        )(inverse, cross, slab, *pieces, *more)
+
     y, x, core = 4, 2, 1
-    a1, b1 = swap(a0, y), swap(b0, x)
-    a01, b01 = jnp.stack([a0, a1]), jnp.stack([b0, b1])
-    a23, b23 = swap(a01, x), swap(b01, y)
-    own = (a01, a23, b01, b23)
-    other = tuple(swap(v, core) for v in own)
-    return pl.pallas_call(
-        functools.partial(update_kernel, width),
-        out_shape=jax.ShapeDtypeStruct(slab.shape, jnp.bfloat16),
-        in_specs=[VMEM] * 11,
-        out_specs=pl.BlockSpec(memory_space=pl.ANY),
-        scratch_shapes=[
-            pltpu.VMEM((16, rows, half), jnp.bfloat16),
-            pltpu.SemaphoreType.DMA((16,)),
-        ],
-        name="update",
-    )(inverse, cross, slab, *own, *other)
+    by = {0: observed}
+    for flip in (x + y, x, y, core):
+        by[flip] = swap(observed, flip)
+    arrived, inverse = lax.optimization_barrier(([by[f] for f in (x, y, x + y)], inverse))
+    for flip, piece in zip((x, y, x + y), arrived):
+        by[flip] = piece
+        by[flip + core] = swap(piece, core)
+    early, late = (0, core, x, y, x + y), (x + core, y + core, x + y + core)
+    half = update(inverse, early, [by[f] for f in early], None)
+    return update(inverse, late, [by[f] for f in late], half)
 
 
 def solution(mesh):

time: 54.3 us -> 41.3 us (0.76)
  blocking collectives: 23 us -> 0 us
  waiting for transfers between devices: 5.35 us -> 15.7 us
  starting transfers between devices: 5.47 us -> 11.5 us
  Pallas kernels: 17.7 us -> 13.1 us
  other arithmetic: 0.9 us -> 0 us
  local copies, waits for them, and re-layouts: 1.37 us -> 0.67 us
    all_to_all x1 -> x0, blocking collectives: 23 us -> none  [plane_body(): lax.all_to_all(picked.reshape(groups, SLOTS, -1), 'rows', split_axis=0, c...]
    all_to_all x0 -> x1, waiting for transfers between devices: none -> 14.4 us  [plane_body(): lax.all_to_all(picked.reshape(groups, SLOTS, -1), 'rows', split_axis=0, c...]
    all_to_all x0 -> x1, starting transfers between devices: none -> 7.3 us  [plane_body(): lax.all_to_all(picked.reshape(groups, SLOTS, -1), 'rows', split_axis=0, c...]
    pallas_call x3 -> x5, Pallas kernels: 15.2 us -> 9.64 us  [the longest x1 4.79 us: plane_body(): pl.pallas_call(invert_kernel, out_shape=jax.ShapeDtypeStruct((PARTS * cou...]
    ppermute x8 -> x7, waiting for transfers between devices: 5.35 us -> 1.27 us  [swap(): return lax.ppermute(value, 'rows', [(i, i ^ bit) for i in range(groups)])]
    ppermute x8 -> x7, starting transfers between devices: 5.47 us -> 4.17 us  [swap(): return lax.ppermute(value, 'rows', [(i, i ^ bit) for i in range(groups)])]
    another operation x2 -> x0, other arithmetic: 0.9 us -> none  [plane_body(): a01, b01 = (jnp.stack([a0, a1]), jnp.stack([b0, b1]))]
    pallas_call x1, Pallas kernels: 2.59 us -> 3.42 us  [plane_body(): pl.pallas_call(functools.partial(pick_kernel, groups, width), out_shape=j...]
  transfers between devices with their start and end apart: 8 -> 8, of which waited for: 3 -> 2; matrix products, arithmetic and copies ran while one was open for 2% -> 0% of each run, Pallas kernels for 12% -> 19%
where the time goes in v2:
time: 41.3 us; the launch traced here: 41 us
  waiting for transfers between devices  15.7 us (38%)
  Pallas kernels  13.1 us (32%)
  starting transfers between devices  11.5 us (28%)
  local copies, waits for them, and re-layouts  0.67 us (2%)
    all_to_all x1, waiting for transfers between devices, plane_body(): lax.all_to_all(picked.reshape(groups, SLOTS, -1), 'rows', split_axis=0, c...  14.4 us
    all_to_all x1, starting transfers between devices, plane_body(): lax.all_to_all(picked.reshape(groups, SLOTS, -1), 'rows', split_axis=0, c...  7.3 us
    pallas_call x1, Pallas kernels, plane_body(): pl.pallas_call(invert_kernel, out_shape=jax.ShapeDtypeStruct((PARTS * cou...  4.79 us
    ppermute x7, starting transfers between devices, swap(): return lax.ppermute(value, 'rows', [(i, i ^ bit) for i in range(groups)])  4.17 us
    pallas_call x2, Pallas kernels, update(): pl.pallas_call(functools.partial(update_kernel, width, flips), out_shape=...  4.05 us
    pallas_call x1, Pallas kernels, plane_body(): pl.pallas_call(functools.partial(pick_kernel, groups, width), out_shape=j...  3.42 us
    ppermute x7, waiting for transfers between devices, swap(): return lax.ppermute(value, 'rows', [(i, i ^ bit) for i in range(groups)])  1.27 us
  transfers between devices with their start and end apart: 8, of which 2 were waited for; matrix products, arithmetic and copies ran while one was open for 0% of the time, Pallas kernels for 19%

profile of v2, /device:TPU:0, one launch (start us, length us, event | category | flops | bytes accessed | tf_op | source)
XLA Modules:
  0.0 41.0 jit_solution(5397852573063696507)
XLA Ops:
  0.0 3.4 %pick.1 = bf16[512,512]{1,0:T(8,128)(2,1)} custom-call(s32[1,128]{1,0:T(1,128)} %bitcast.5, bf16[128,4096]{1,0:T(8,128)(2,1)} %slab_ref.3, bf16[128,128]{1,0:T(8,128)(2,1)} %cross_ref.3), custom_call_target="tpu_custom_call" | custom-call | tf_op jit(solution)/shard_map/pick/pallas_call | solution.py:256
  3.4 7.3 %all-to-all-start = ((bf16[32,16,512]{2,1,0:T(8,128)(2,1)}), bf16[32,16,512]{2,1,0:T(8,128)(2,1)S(1)}, u32[]{:S(2)}, u32[]{:S(2)}) async-start(bf16[32,16,512]{2,1,0:T(8,128)(2,1)} %bitcast.8), calls=%async_computation | async-start | bytes 1048576 | tf_op jit(solution)/shard_map/all_to_all | solution.py:284
  10.7 0.0 copy-start.2
  10.8 0.0 copy-start.3
  10.8 0.6 %copy-done.2 = s32[128]{0:T(128)S(1)} copy-done((s32[128]{0:T(128)S(1)}, s32[128]{0:T(128)}, u32[]{:S(2)}) %copy-start.2) | copy-done | bytes 536
  11.4 0.0 copy-done.3
  11.4 0.5 %order.1 = (bf16[512,512]{1,0:T(8,128)(2,1)S(1)}, f32[128,128]{1,0:T(8,128)S(1)}) custom-call(s32[1,128]{1,0:T(1,128)S(1)} %bitcast.6, f32[1,128]{1,0:T(1,128)S(1)} %bitcast.7), custom_call_target="tpu_custom_call" | custom-call | flops 2097152000 | bytes 65536 | tf_op jit(solution)/shard_map/order/pallas_call | solution.py:270
  11.9 14.4 %all-to-all-done = bf16[32,16,512]{2,1,0:T(8,128)(2,1)S(1)} async-done(((bf16[32,16,512]{2,1,0:T(8,128)(2,1)}), bf16[32,16,512]{2,1,0:T(8,128)(2,1)S(1)}, u32[]{:S(2)}, u32[]{:S(2)}) %all-to-all-start) | async-done | bytes 524320 | tf_op jit(solution)/shard_map/all_to_all | solution.py:284
  26.3 0.3 compact.1
  26.6 0.1 collective-permute-start.6
  26.7 1.9 %collective-permute-start.2 = (bf16[128,512]{1,0:T(8,128)(2,1)S(1)}, bf16[128,512]{1,0:T(8,128)(2,1)S(1)}, u32[]{:S(2)}, u32[]{:S(2)}) collective-permute-start(bf16[128,512]{1,0:T(8,128)(2,1)S(1)} %get-tuple-element.15.refs_0_), channel_id=1, source_target_pairs={{0,6},{1,7},{2,4},{3,5},{4,2},{5,3},{6,0},{7,1},{8,14},{9,15},{10,... | collective-permute-start | bytes 393224 | tf_op jit(solution)/shard_map/ppermute | solution.py:311
  28.6 0.9 %collective-permute-start.1 = (bf16[128,512]{1,0:T(8,128)(2,1)S(1)}, bf16[128,512]{1,0:T(8,128)(2,1)S(1)}, u32[]{:S(2)}, u32[]{:S(2)}) collective-permute-start(bf16[128,512]{1,0:T(8,128)(2,1)S(1)} %get-tuple-element.15.refs_0_), channel_id=1, source_target_pairs={{0,4},{1,5},{2,6},{3,7},{4,0},{5,1},{6,2},{7,3},{8,12},{9,13},{10,... | collective-permute-start | bytes 393224 | tf_op jit(solution)/shard_map/ppermute | solution.py:311
  29.5 0.8 %collective-permute-start = (bf16[128,512]{1,0:T(8,128)(2,1)S(1)}, bf16[128,512]{1,0:T(8,128)(2,1)S(1)}, u32[]{:S(2)}, u32[]{:S(2)}) collective-permute-start(bf16[128,512]{1,0:T(8,128)(2,1)S(1)} %get-tuple-element.15.refs_0_), channel_id=1, source_target_pairs={{0,2},{1,3},{2,0},{3,1},{4,6},{5,7},{6,4},{7,5},{8,10},{9,11},{10,... | collective-permute-start | bytes 393224 | tf_op jit(solution)/shard_map/ppermute | solution.py:311
  30.3 0.0 copy-start
  30.3 0.0 copy-start.1
  30.3 4.8 %invert.1.inverse_ref = bf16[384,128]{1,0:T(8,128)(2,1)S(1)} custom-call(f32[128,128]{1,0:T(8,128)S(1)} %get-tuple-element.16.inn_ref), custom_call_target="tpu_custom_call" | custom-call | flops 6291456000 | bytes 65536 | tf_op jit(solution)/shard_map/invert/pallas_call | solution.py:298
  35.1 0.0 collective-permute-done.2.refs_4_
  35.1 1.3 %collective-permute-done.1.refs_3_ = bf16[128,512]{1,0:T(8,128)(2,1)S(1)} collective-permute-done((bf16[128,512]{1,0:T(8,128)(2,1)S(1)}, bf16[128,512]{1,0:T(8,128)(2,1)S(1)}, u32[]{:S(2)}, u32[]{:S(2)}) %collective-permute-start.1) | collective-permute-done | bytes 131104 | tf_op jit(solution)/shard_map/ppermute | solution.py:311
  36.3 0.0 collective-permute-done.refs_2_
  36.3 0.0 collective-permute-start.3
  36.4 0.5 %collective-permute-start.4 = (bf16[128,512]{1,0:T(8,128)(2,1)S(1)}, bf16[128,512]{1,0:T(8,128)(2,1)S(1)}, u32[]{:S(2)}, u32[]{:S(2)}) collective-permute-start(bf16[128,512]{1,0:T(8,128)(2,1)S(1)} %collective-permute-done.1.refs_3_), channel_id=1, source_target_pairs={{0,1},{1,0},{2,3},{3,2},{4,5},{5,4},{6,7},{7,6},{8,9},{9,8},{10,11... | collective-permute-start | bytes 393224 | tf_op jit(solution)/shard_map/ppermute | solution.py:311
  36.8 0.0 collective-permute-start.5
  36.9 0.0 collective-permute-done.6.refs_1_
  36.9 0.0 copy-done
  36.9 0.0 copy-done.1
  36.9 2.3 %update.2.refs_3_ = bf16[128,4096]{1,0:T(8,128)(2,1)} custom-call(bf16[384,128]{1,0:T(8,128)(2,1)S(1)} %invert.1.inverse_ref, bf16[128,128]{1,0:T(8,128)(2,1)S(1)} %copy-done.1, bf16[128,4096]{1,0:T(8,128)(2,1)S(1)} %copy-done, bf16[128,512]{1,0:T(8,128)(2,1)S(1)} %get-tuple-element.15.refs_0_, bf16[128,512]{1,0:T(8,128)(2,1)S(1)} %collective-permute-done.6.refs_1_, ...), custom_call_target="tpu_custom_call" | custom-call | tf_op jit(solution)/shard_map/update/pallas_call | solution.py:315
  39.2 0.0 collective-permute-done.3.refs_0_
  39.3 0.0 collective-permute-done.4.refs_1_
  39.3 0.0 collective-permute-done.5.refs_2_
  39.3 1.7 %update.3 = bf16[128,4096]{1,0:T(8,128)(2,1)} custom-call(bf16[384,128]{1,0:T(8,128)(2,1)S(1)} %invert.1.inverse_ref, bf16[128,128]{1,0:T(8,128)(2,1)S(1)} %copy-done.1, bf16[128,4096]{1,0:T(8,128)(2,1)S(1)} %copy-done, bf16[128,512]{1,0:T(8,128)(2,1)S(1)} %collective-permute-done.3.refs_0_, ...), custom_call_target="tpu_custom_call", output_to_operand_aliasing={{}: (6, {})} | custom-call | tf_op jit(solution)/shard_map/update/pallas_call | solution.py:315
Async XLA Ops:
  3.4 22.9 %all-to-all-start = ((bf16[32,16,512]{2,1,0:T(8,128)(2,1)}), bf16[32,16,512]{2,1,0:T(8,128)(2,1)S(1)}, u32[]{:S(2)}, u32[]{:S(2)}) async-start(bf16[32,16,512]{2,1,0:T(8,128)(2,1)} %bitcast.8), calls=%async_computation | async-start | bytes 1048576 | tf_op jit(solution)/shard_map/all_to_all | solution.py:284
  10.7 0.7 %copy-start.2 = (s32[128]{0:T(128)S(1)}, s32[128]{0:T(128)}, u32[]{:S(2)}) copy-start(s32[128]{0:T(128)} %param.6) | copy-start | bytes 1540
  10.8 0.7 %copy-start.3 = (f32[128]{0:T(128)S(1)}, f32[128]{0:T(128)}, u32[]{:S(2)}) copy-start(f32[128]{0:T(128)} %param.7) | copy-start | bytes 1540
  26.6 10.3 %collective-permute-start.6 = (bf16[128,512]{1,0:T(8,128)(2,1)S(1)}, bf16[128,512]{1,0:T(8,128)(2,1)S(1)}, u32[]{:S(2)}, u32[]{:S(2)}) collective-permute-start(bf16[128,512]{1,0:T(8,128)(2,1)S(1)} %get-tuple-element.15.refs_0_), channel_id=1, source_target_pairs={{0,1},{1,0},{2,3},{3,2},{4,5},{5,4},{6,7},{7,6},{8,9},{9,8},{10,11... | collective-permute-start | bytes 393224 | tf_op jit(solution)/shard_map/ppermute | solution.py:311
  26.7 8.4 %collective-permute-start.2 = (bf16[128,512]{1,0:T(8,128)(2,1)S(1)}, bf16[128,512]{1,0:T(8,128)(2,1)S(1)}, u32[]{:S(2)}, u32[]{:S(2)}) collective-permute-start(bf16[128,512]{1,0:T(8,128)(2,1)S(1)} %get-tuple-element.15.refs_0_), channel_id=1, source_target_pairs={{0,6},{1,7},{2,4},{3,5},{4,2},{5,3},{6,0},{7,1},{8,14},{9,15},{10,... | collective-permute-start | bytes 393224 | tf_op jit(solution)/shard_map/ppermute | solution.py:311
  28.6 7.7 %collective-permute-start.1 = (bf16[128,512]{1,0:T(8,128)(2,1)S(1)}, bf16[128,512]{1,0:T(8,128)(2,1)S(1)}, u32[]{:S(2)}, u32[]{:S(2)}) collective-permute-start(bf16[128,512]{1,0:T(8,128)(2,1)S(1)} %get-tuple-element.15.refs_0_), channel_id=1, source_target_pairs={{0,4},{1,5},{2,6},{3,7},{4,0},{5,1},{6,2},{7,3},{8,12},{9,13},{10,... | collective-permute-start | bytes 393224 | tf_op jit(solution)/shard_map/ppermute | solution.py:311
  29.5 6.9 %collective-permute-start = (bf16[128,512]{1,0:T(8,128)(2,1)S(1)}, bf16[128,512]{1,0:T(8,128)(2,1)S(1)}, u32[]{:S(2)}, u32[]{:S(2)}) collective-permute-start(bf16[128,512]{1,0:T(8,128)(2,1)S(1)} %get-tuple-element.15.refs_0_), channel_id=1, source_target_pairs={{0,2},{1,3},{2,0},{3,1},{4,6},{5,7},{6,4},{7,5},{8,10},{9,11},{10,... | collective-permute-start | bytes 393224 | tf_op jit(solution)/shard_map/ppermute | solution.py:311
  30.3 6.6 %copy-start = (bf16[128,4096]{1,0:T(8,128)(2,1)S(1)}, bf16[128,4096]{1,0:T(8,128)(2,1)}, u32[]{:S(2)}) copy-start(bf16[128,4096]{1,0:T(8,128)(2,1)} %slab_ref.3) | copy-start | bytes 3145732
  30.3 6.6 %copy-start.1 = (bf16[128,128]{1,0:T(8,128)(2,1)S(1)}, bf16[128,128]{1,0:T(8,128)(2,1)}, u32[]{:S(2)}) copy-start(bf16[128,128]{1,0:T(8,128)(2,1)} %cross_ref.3) | copy-start | bytes 98308
  36.3 2.9 %collective-permute-start.3 = (bf16[128,512]{1,0:T(8,128)(2,1)S(1)}, bf16[128,512]{1,0:T(8,128)(2,1)S(1)}, u32[]{:S(2)}, u32[]{:S(2)}) collective-permute-start(bf16[128,512]{1,0:T(8,128)(2,1)S(1)} %collective-permute-done.refs_2_), channel_id=1, source_target_pairs={{0,1},{1,0},{2,3},{3,2},{4,5},{5,4},{6,7},{7,6},{8,9},{9,8},{10,11... | collective-permute-start | bytes 393224 | tf_op jit(solution)/shard_map/ppermute | solution.py:311
  36.4 2.9 %collective-permute-start.4 = (bf16[128,512]{1,0:T(8,128)(2,1)S(1)}, bf16[128,512]{1,0:T(8,128)(2,1)S(1)}, u32[]{:S(2)}, u32[]{:S(2)}) collective-permute-start(bf16[128,512]{1,0:T(8,128)(2,1)S(1)} %collective-permute-done.1.refs_3_), channel_id=1, source_target_pairs={{0,1},{1,0},{2,3},{3,2},{4,5},{5,4},{6,7},{7,6},{8,9},{9,8},{10,11... | collective-permute-start | bytes 393224 | tf_op jit(solution)/shard_map/ppermute | solution.py:311
  36.8 2.4 %collective-permute-start.5 = (bf16[128,512]{1,0:T(8,128)(2,1)S(1)}, bf16[128,512]{1,0:T(8,128)(2,1)S(1)}, u32[]{:S(2)}, u32[]{:S(2)}) collective-permute-start(bf16[128,512]{1,0:T(8,128)(2,1)S(1)} %collective-permute-done.2.refs_4_), channel_id=1, source_target_pairs={{0,1},{1,0},{2,3},{3,2},{4,5},{5,4},{6,7},{7,6},{8,9},{9,8},{10,11... | collective-permute-start | bytes 393224 | tf_op jit(solution)/shard_map/ppermute | solution.py:311

commit v3 on v2

--- a/solution.py
+++ b/solution.py
@@ -83,20 +83,27 @@
     return along, down, rank_along, rank_down
 
 
-def pick_kernel(groups, width, obs_hbm, slab_hbm, cross_hbm, out_ref, obs_ref, slab, cross, sem):
+def column_group(device):
+    return (device % PLANE) ^ (6 * ((device // PLANE) % 2))
+
+
+def pick_kernel(
+    groups, width, obs_hbm, slab_hbm, cross_hbm, out_hbm, obs_ref, slab, cross, out, sem, out_sem
+):
     rows, count = slab.shape[0], obs_ref.shape[1]
+    half = slab.shape[1] // 2
 
     def fetch(source, target, index):
         copy = pltpu.make_async_copy(source, target, sem.at[index])
         copy.start()
         return copy
 
-    def columns(ref, group):
-        return ref.at[:, group * width : (group + 1) * width]
-
-    got_obs = fetch(obs_hbm, obs_ref, PLANE)
-    got_slab = [fetch(columns(slab_hbm, g), columns(slab, g), g) for g in range(PLANE)]
-    got_cross = fetch(cross_hbm, cross, PLANE + 1)
+    got_obs = fetch(obs_hbm, obs_ref, 0)
+    got_cross = fetch(cross_hbm, cross, 1)
+    got_slab = [
+        fetch(slab_hbm.at[:, i * half : (i + 1) * half], slab.at[:, i * half : (i + 1) * half], 2 + i)
+        for i in range(2)
+    ]
     me = lax.axis_index("rows")
     got_obs.wait()
     along, down, rank, _ = spread_index(obs_ref, rows)
@@ -115,11 +122,13 @@
     got_cross.wait()
     cross_part = dot32(selector[:SLOTS], cross[...]).astype(jnp.bfloat16)
     lanes = width // 4
+    sent = []
     for group in range(PLANE):
-        got_slab[group].wait()
+        if group % 4 == 0:
+            got_slab[group // 4].wait()
         got = dot32(selector, slab[:, group * width : (group + 1) * width])
         tail = got[:, 3 * lanes :]
-        block = jnp.concatenate(
+        out[group * SLOTS : (group + 1) * SLOTS, :] = jnp.concatenate(
             [
                 (
                     got[:SLOTS, t * lanes : (t + 1) * lanes]
@@ -130,9 +139,17 @@
             + [cross_part],
             axis=1,
         )
-        for level in range(groups // PLANE):
-            at = (level * PLANE + group) * SLOTS
-            out_ref[at : at + SLOTS, :] = block
+        if group % 2:
+            source = out.at[(group - 1) * SLOTS : (group + 1) * SLOTS]
+            for level in range(groups // PLANE):
+                to = (level * PLANE + column_group(level * PLANE + group - 1)) * SLOTS
+                copy = pltpu.make_async_copy(
+                    source, out_hbm.at[to : to + 2 * SLOTS], out_sem.at[len(sent)]
+                )
+                copy.start()
+                sent.append(copy)
+    for copy in sent:
+        copy.wait()
 
 
 def order_kernel(rows, obs_ref, noise_ref, order_ref, diagonal_ref):
@@ -170,14 +187,14 @@
     inn_ref[...] = 0.5 * (picked + picked.T) + diagonal_ref[...]
 
 
-def invert_kernel(inn_ref, out_ref):
+def invert_kernel(panel_range, inn_ref, out_ref):
     size = inn_ref.shape[0]
     step, panels = 8, size // 8
     full = (step, size)
     m = [inn_ref[i * step : (i + 1) * step, :] for i in range(panels)]
     sub = lax.broadcasted_iota(jnp.int32, full, 0)
     lane = lax.broadcasted_iota(jnp.int32, full, 1)
-    for p in range(panels):
+    for p in panel_range:
         at = p * step
         on = lane == sub + at
         row = m[p]
@@ -217,6 +234,10 @@
             m[i] = m[i] + terms[0]
             if i == p:
                 m[i] = m[i] - jnp.where(on, 2.0, 0.0)
+    if panel_range[-1] < panels - 1:
+        for i in range(panels):
+            out_ref[i * step : (i + 1) * step, :] = m[i]
+        return
     for i in range(0, panels, 2):
         x = -jnp.concatenate([m[i], m[i + 1]], axis=0)
         for part in range(PARTS):
@@ -228,21 +249,26 @@
 
 def update_kernel(width, flips, inverse_ref, cross_ref, slab_ref, *refs):
     pieces, (out_ref, held, sem) = refs[: len(flips)], refs[-3:]
-    place = lax.axis_index("rows") % PLANE
-    inverse, cross = inverse_ref[...], cross_ref[...]
+    place = column_group(lax.axis_index("rows"))
+    cross = cross_ref[...]
     size = cross.shape[1]
-    copies = []
+    inverse = jnp.concatenate(
+        [inverse_ref[t * size : (t + 1) * size] for t in range(PARTS)], axis=1
+    )
+    copies, gains = [], []
+    for piece in pieces:
+        gains.append(
+            dot32(inverse, jnp.concatenate([piece[...]] * PARTS, axis=0)).astype(jnp.bfloat16)
+        )
     for index, flip in enumerate(flips):
         at = pl.multiple_of((place ^ flip) * width, width)
-        parts = dot32(inverse, pieces[index][...])
-        gain = sum(parts[t * size : (t + 1) * size] for t in range(PARTS)).astype(jnp.bfloat16)
-        new = slab_ref[:, pl.ds(at, width)].astype(jnp.float32) - dot32(cross, gain)
+        new = slab_ref[:, pl.ds(at, width)].astype(jnp.float32) - dot32(cross, gains[index])
         held[index] = new.astype(jnp.bfloat16)
-        copies.append(
-            pltpu.make_async_copy(held.at[index], out_ref.at[:, pl.ds(at, width)], sem.at[index])
-        )
-    for copy in copies:
+        copy = pltpu.make_async_copy(
+            held.at[index], out_ref.at[:, pl.ds(at, width)], sem.at[index]
+        )
         copy.start()
+        copies.append(copy)
     for copy in copies:
         copy.wait()
 
@@ -257,12 +283,14 @@
         functools.partial(pick_kernel, groups, width),
         out_shape=jax.ShapeDtypeStruct((groups * SLOTS, 3 * width // 4 + count), jnp.bfloat16),
         in_specs=[HBM] * 3,
-        out_specs=VMEM,
+        out_specs=HBM,
         scratch_shapes=[
             pltpu.VMEM((1, count), jnp.int32),
             pltpu.VMEM(slab.shape, jnp.bfloat16),
             pltpu.VMEM(cross.shape, jnp.bfloat16),
-            pltpu.SemaphoreType.DMA((PLANE + 2,)),
+            pltpu.VMEM((PLANE * SLOTS, 3 * width // 4 + count), jnp.bfloat16),
+            pltpu.SemaphoreType.DMA((4,)),
+            pltpu.SemaphoreType.DMA((groups // 2,)),
         ],
         compiler_params=room(56),
         name="pick",
@@ -295,17 +323,18 @@
         compiler_params=room(8),
         name="compact",
     )(order, diagonal, got)
-    inverse = pl.pallas_call(
-        invert_kernel,
-        out_shape=jax.ShapeDtypeStruct((PARTS * count, count), jnp.bfloat16),
-        in_specs=[VMEM],
-        out_specs=VMEM,
-        cost_estimate=pl.CostEstimate(
-            flops=3000 * count**3, bytes_accessed=4 * count * count, transcendentals=count
-        ),
-        compiler_params=room(4),
-        name="invert",
-    )(innovation)
+    def invert(panel_range, value, out_shape):
+        return pl.pallas_call(
+            functools.partial(invert_kernel, panel_range),
+            out_shape=out_shape,
+            in_specs=[VMEM],
+            out_specs=VMEM,
+            cost_estimate=pl.CostEstimate(
+                flops=1500 * count**3, bytes_accessed=4 * count * count, transcendentals=count
+            ),
+            compiler_params=room(4),
+            name="invert",
+        )(value)
 
     def swap(value, bit):
         return lax.ppermute(value, "rows", [(i, i ^ bit) for i in range(groups)])
@@ -322,21 +351,25 @@
                 pltpu.SemaphoreType.DMA((len(flips),)),
             ],
             input_output_aliases={3 + len(pieces): 0} if more else {},
-            compiler_params=room(8),
+            compiler_params=room(12),
             name="update",
         )(inverse, cross, slab, *pieces, *more)
 
-    y, x, core = 4, 2, 1
-    by = {0: observed}
-    for flip in (x + y, x, y, core):
-        by[flip] = swap(observed, flip)
-    arrived, inverse = lax.optimization_barrier(([by[f] for f in (x, y, x + y)], inverse))
-    for flip, piece in zip((x, y, x + y), arrived):
-        by[flip] = piece
-        by[flip + core] = swap(piece, core)
-    early, late = (0, core, x, y, x + y), (x + core, y + core, x + y + core)
-    half = update(inverse, early, [by[f] for f in early], None)
-    return update(inverse, late, [by[f] for f in late], half)
+    panels = count // 8
+    by = {0: observed, 1: swap(observed, 1)}
+    by.update({group: swap(observed, bit) for bit, group in ((2, 2), (4, 4), (8, 6))})
+    midway = invert(range(panels // 2), innovation, innovation)
+    arrived, midway = lax.optimization_barrier(([by[g] for g in (2, 4, 6)], midway))
+    for group, piece in zip((2, 4, 6), arrived):
+        by[group] = piece
+        by[group + 1] = swap(piece, 1)
+    inverse = invert(
+        range(panels // 2, panels),
+        midway,
+        jax.ShapeDtypeStruct((PARTS * count, count), jnp.bfloat16),
+    )
+    flips = tuple(range(PLANE))
+    return update(inverse, flips, [by[f] for f in flips], None)
 
 
 def solution(mesh):

time: 41.3 us -> 38.2 us (0.925)
  Pallas kernels: 13.1 us -> 9.81 us
  waiting for transfers between devices: 15.7 us -> 16.8 us
  starting transfers between devices: 11.5 us -> 10.6 us
    pallas_call x2 -> x1, Pallas kernels: 4.05 us -> 1.79 us  [update(): pl.pallas_call(functools.partial(update_kernel, width, flips), out_shape=...]
    ppermute x7, waiting for transfers between devices: 1.27 us -> 2.38 us  [swap(): return lax.ppermute(value, 'rows', [(i, i ^ bit) for i in range(groups)])]
    pallas_call x1, Pallas kernels: 3.42 us -> 2.35 us  [plane_body(): pl.pallas_call(functools.partial(pick_kernel, groups, width), out_shape=j...]
    ppermute x7, starting transfers between devices: 4.17 us -> 3.26 us  [swap(): return lax.ppermute(value, 'rows', [(i, i ^ bit) for i in range(groups)])]
    pallas_call x1 -> x2, Pallas kernels: 4.79 us -> 4.86 us  [invert(): pl.pallas_call(functools.partial(invert_kernel, panel_range), out_shape=o...]
  transfers between devices with their start and end apart: 8 -> 8, of which waited for: 2 -> 4; matrix products, arithmetic and copies ran while one was open for 0% -> 0% of each run, Pallas kernels for 19% -> 14%
where the time goes in v3:
time: 38.2 us; the launch traced here: 37.9 us
  waiting for transfers between devices  16.8 us (44%)
  starting transfers between devices  10.6 us (28%)
  Pallas kernels  9.81 us (26%)
  local copies, waits for them, and re-layouts  0.67 us (2%)
    all_to_all x1, waiting for transfers between devices, plane_body(): lax.all_to_all(picked.reshape(groups, SLOTS, -1), 'rows', split_axis=0, c...  14.4 us
    all_to_all x1, starting transfers between devices, plane_body(): lax.all_to_all(picked.reshape(groups, SLOTS, -1), 'rows', split_axis=0, c...  7.3 us
    pallas_call x2, Pallas kernels, invert(): pl.pallas_call(functools.partial(invert_kernel, panel_range), out_shape=o...  4.86 us
    ppermute x7, starting transfers between devices, swap(): return lax.ppermute(value, 'rows', [(i, i ^ bit) for i in range(groups)])  3.26 us
    ppermute x7, waiting for transfers between devices, swap(): return lax.ppermute(value, 'rows', [(i, i ^ bit) for i in range(groups)])  2.38 us
    pallas_call x1, Pallas kernels, plane_body(): pl.pallas_call(functools.partial(pick_kernel, groups, width), out_shape=j...  2.35 us
    pallas_call x1, Pallas kernels, update(): pl.pallas_call(functools.partial(update_kernel, width, flips), out_shape=...  1.79 us
  transfers between devices with their start and end apart: 8, of which 4 were waited for; matrix products, arithmetic and copies ran while one was open for 0% of the time, Pallas kernels for 14%

profile of v3, /device:TPU:0, one launch (start us, length us, event | category | flops | bytes accessed | tf_op | source)
XLA Modules:
  0.0 37.9 jit_solution(14556554862402182556)
XLA Ops:
  0.0 2.3 %pick.1 = bf16[512,512]{1,0:T(8,128)(2,1)} custom-call(s32[1,128]{1,0:T(1,128)} %bitcast.5, bf16[128,4096]{1,0:T(8,128)(2,1)} %slab_ref.1, bf16[128,128]{1,0:T(8,128)(2,1)} %cross_ref.1), custom_call_target="tpu_custom_call" | custom-call | tf_op jit(solution)/shard_map/pick/pallas_call | solution.py:282
  2.4 7.3 %all-to-all-start = ((bf16[32,16,512]{2,1,0:T(8,128)(2,1)}), bf16[32,16,512]{2,1,0:T(8,128)(2,1)S(1)}, u32[]{:S(2)}, u32[]{:S(2)}) async-start(bf16[32,16,512]{2,1,0:T(8,128)(2,1)} %bitcast.8), calls=%async_computation | async-start | bytes 1048576 | tf_op jit(solution)/shard_map/all_to_all | solution.py:312
  9.7 0.0 copy-start.2
  9.7 0.0 copy-start.3
  9.7 0.6 %copy-done.2 = s32[128]{0:T(128)S(1)} copy-done((s32[128]{0:T(128)S(1)}, s32[128]{0:T(128)}, u32[]{:S(2)}) %copy-start.2) | copy-done | bytes 536
  10.3 0.0 copy-done.3
  10.3 0.5 %order.1 = (bf16[512,512]{1,0:T(8,128)(2,1)S(1)}, f32[128,128]{1,0:T(8,128)S(1)}) custom-call(s32[1,128]{1,0:T(1,128)S(1)} %bitcast.6, f32[1,128]{1,0:T(1,128)S(1)} %bitcast.7), custom_call_target="tpu_custom_call" | custom-call | flops 2097152000 | bytes 65536 | tf_op jit(solution)/shard_map/order/pallas_call | solution.py:298
  10.8 14.4 %all-to-all-done = bf16[32,16,512]{2,1,0:T(8,128)(2,1)S(1)} async-done(((bf16[32,16,512]{2,1,0:T(8,128)(2,1)}), bf16[32,16,512]{2,1,0:T(8,128)(2,1)S(1)}, u32[]{:S(2)}, u32[]{:S(2)}) %all-to-all-start) | async-done | bytes 524320 | tf_op jit(solution)/shard_map/all_to_all | solution.py:312
  25.2 0.3 compact.1
  25.6 0.1 collective-permute-start.3
  25.6 1.3 %collective-permute-start.2 = (bf16[128,512]{1,0:T(8,128)(2,1)S(1)}, bf16[128,512]{1,0:T(8,128)(2,1)S(1)}, u32[]{:S(2)}, u32[]{:S(2)}) collective-permute-start(bf16[128,512]{1,0:T(8,128)(2,1)S(1)} %get-tuple-element.15.refs_0_), channel_id=1, source_target_pairs={{0,8},{1,9},{2,10},{3,11},{4,12},{5,13},{6,14},{7,15},{8,0},{9,1},... | collective-permute-start | bytes 393224 | tf_op jit(solution)/shard_map/ppermute | solution.py:340
  27.0 0.8 %collective-permute-start.1 = (bf16[128,512]{1,0:T(8,128)(2,1)S(1)}, bf16[128,512]{1,0:T(8,128)(2,1)S(1)}, u32[]{:S(2)}, u32[]{:S(2)}) collective-permute-start(bf16[128,512]{1,0:T(8,128)(2,1)S(1)} %get-tuple-element.15.refs_0_), channel_id=1, source_target_pairs={{0,4},{1,5},{2,6},{3,7},{4,0},{5,1},{6,2},{7,3},{8,12},{9,13},{10,... | collective-permute-start | bytes 393224 | tf_op jit(solution)/shard_map/ppermute | solution.py:340
  27.7 0.6 %collective-permute-start = (bf16[128,512]{1,0:T(8,128)(2,1)S(1)}, bf16[128,512]{1,0:T(8,128)(2,1)S(1)}, u32[]{:S(2)}, u32[]{:S(2)}) collective-permute-start(bf16[128,512]{1,0:T(8,128)(2,1)S(1)} %get-tuple-element.15.refs_0_), channel_id=1, source_target_pairs={{0,2},{1,3},{2,0},{3,1},{4,6},{5,7},{6,4},{7,5},{8,10},{9,11},{10,... | collective-permute-start | bytes 393224 | tf_op jit(solution)/shard_map/ppermute | solution.py:340
  28.3 2.3 %invert.2.inn_ref = f32[128,128]{1,0:T(8,128)S(1)} custom-call(f32[128,128]{1,0:T(8,128)S(1)} %get-tuple-element.16.inn_ref), custom_call_target="tpu_custom_call" | custom-call | flops 3145728000 | bytes 65536 | tf_op jit(solution)/shard_map/invert/pallas_call | solution.py:327
  30.6 0.0 copy-start
  30.6 0.0 copy-start.1
  30.7 0.9 %collective-permute-done.2.refs_6_ = bf16[128,512]{1,0:T(8,128)(2,1)S(1)} collective-permute-done((bf16[128,512]{1,0:T(8,128)(2,1)S(1)}, bf16[128,512]{1,0:T(8,128)(2,1)S(1)}, u32[]{:S(2)}, u32[]{:S(2)}) %collective-permute-start.2) | collective-permute-done | bytes 131104 | tf_op jit(solution)/shard_map/ppermute | solution.py:340
  31.5 1.0 %collective-permute-done.1.refs_4_ = bf16[128,512]{1,0:T(8,128)(2,1)S(1)} collective-permute-done((bf16[128,512]{1,0:T(8,128)(2,1)S(1)}, bf16[128,512]{1,0:T(8,128)(2,1)S(1)}, u32[]{:S(2)}, u32[]{:S(2)}) %collective-permute-start.1) | collective-permute-done | bytes 131104 | tf_op jit(solution)/shard_map/ppermute | solution.py:340
  32.5 0.5 %collective-permute-done.refs_2_ = bf16[128,512]{1,0:T(8,128)(2,1)S(1)} collective-permute-done((bf16[128,512]{1,0:T(8,128)(2,1)S(1)}, bf16[128,512]{1,0:T(8,128)(2,1)S(1)}, u32[]{:S(2)}, u32[]{:S(2)}) %collective-permute-start) | collective-permute-done | bytes 131104 | tf_op jit(solution)/shard_map/ppermute | solution.py:340
  33.0 0.0 collective-permute-start.4
  33.0 0.5 %collective-permute-start.5 = (bf16[128,512]{1,0:T(8,128)(2,1)S(1)}, bf16[128,512]{1,0:T(8,128)(2,1)S(1)}, u32[]{:S(2)}, u32[]{:S(2)}) collective-permute-start(bf16[128,512]{1,0:T(8,128)(2,1)S(1)} %collective-permute-done.1.refs_4_), channel_id=1, source_target_pairs={{0,1},{1,0},{2,3},{3,2},{4,5},{5,4},{6,7},{7,6},{8,9},{9,8},{10,11... | collective-permute-start | bytes 393224 | tf_op jit(solution)/shard_map/ppermute | solution.py:340
  33.5 0.0 collective-permute-start.6
  33.5 2.5 %invert.3.inverse_ref = bf16[384,128]{1,0:T(8,128)(2,1)S(1)} custom-call(f32[128,128]{1,0:T(8,128)S(1)} %invert.2.inn_ref), custom_call_target="tpu_custom_call" | custom-call | flops 3145728000 | bytes 65536 | tf_op jit(solution)/shard_map/invert/pallas_call | solution.py:327
  36.1 0.0 collective-permute-done.3.refs_1_
  36.1 0.0 collective-permute-done.4.refs_3_
  36.1 0.0 collective-permute-done.5.refs_5_
  36.1 0.0 collective-permute-done.6.refs_7_
  36.1 0.0 copy-done
  36.1 0.0 copy-done.1
  36.1 1.8 %update.1 = bf16[128,4096]{1,0:T(8,128)(2,1)} custom-call(bf16[384,128]{1,0:T(8,128)(2,1)S(1)} %invert.3.inverse_ref, bf16[128,128]{1,0:T(8,128)(2,1)S(1)} %copy-done.1, bf16[128,4096]{1,0:T(8,128)(2,1)S(1)} %copy-done, bf16[128,512]{1,0:T(8,128)(2,1)S(1)} %get-tuple-element.15.refs_0_, bf16[128,512]{1,0:T(8,128)(2,1)S(1)} %collective-permute-done.3.refs_1_, ...), custom_call_target="tpu_custom_call" | custom-call | tf_op jit(solution)/shard_map/update/pallas_call | solution.py:344
Async XLA Ops:
  2.4 22.9 %all-to-all-start = ((bf16[32,16,512]{2,1,0:T(8,128)(2,1)}), bf16[32,16,512]{2,1,0:T(8,128)(2,1)S(1)}, u32[]{:S(2)}, u32[]{:S(2)}) async-start(bf16[32,16,512]{2,1,0:T(8,128)(2,1)} %bitcast.8), calls=%async_computation | async-start | bytes 1048576 | tf_op jit(solution)/shard_map/all_to_all | solution.py:312
  9.7 0.7 %copy-start.2 = (s32[128]{0:T(128)S(1)}, s32[128]{0:T(128)}, u32[]{:S(2)}) copy-start(s32[128]{0:T(128)} %param.6) | copy-start | bytes 1540
  9.7 0.7 %copy-start.3 = (f32[128]{0:T(128)S(1)}, f32[128]{0:T(128)}, u32[]{:S(2)}) copy-start(f32[128]{0:T(128)} %param.7) | copy-start | bytes 1540
  25.6 10.5 %collective-permute-start.3 = (bf16[128,512]{1,0:T(8,128)(2,1)S(1)}, bf16[128,512]{1,0:T(8,128)(2,1)S(1)}, u32[]{:S(2)}, u32[]{:S(2)}) collective-permute-start(bf16[128,512]{1,0:T(8,128)(2,1)S(1)} %get-tuple-element.15.refs_0_), channel_id=1, source_target_pairs={{0,1},{1,0},{2,3},{3,2},{4,5},{5,4},{6,7},{7,6},{8,9},{9,8},{10,11... | collective-permute-start | bytes 393224 | tf_op jit(solution)/shard_map/ppermute | solution.py:340
  25.6 5.9 %collective-permute-start.2 = (bf16[128,512]{1,0:T(8,128)(2,1)S(1)}, bf16[128,512]{1,0:T(8,128)(2,1)S(1)}, u32[]{:S(2)}, u32[]{:S(2)}) collective-permute-start(bf16[128,512]{1,0:T(8,128)(2,1)S(1)} %get-tuple-element.15.refs_0_), channel_id=1, source_target_pairs={{0,8},{1,9},{2,10},{3,11},{4,12},{5,13},{6,14},{7,15},{8,0},{9,1},... | collective-permute-start | bytes 393224 | tf_op jit(solution)/shard_map/ppermute | solution.py:340
  27.0 5.6 %collective-permute-start.1 = (bf16[128,512]{1,0:T(8,128)(2,1)S(1)}, bf16[128,512]{1,0:T(8,128)(2,1)S(1)}, u32[]{:S(2)}, u32[]{:S(2)}) collective-permute-start(bf16[128,512]{1,0:T(8,128)(2,1)S(1)} %get-tuple-element.15.refs_0_), channel_id=1, source_target_pairs={{0,4},{1,5},{2,6},{3,7},{4,0},{5,1},{6,2},{7,3},{8,12},{9,13},{10,... | collective-permute-start | bytes 393224 | tf_op jit(solution)/shard_map/ppermute | solution.py:340
  27.7 5.3 %collective-permute-start = (bf16[128,512]{1,0:T(8,128)(2,1)S(1)}, bf16[128,512]{1,0:T(8,128)(2,1)S(1)}, u32[]{:S(2)}, u32[]{:S(2)}) collective-permute-start(bf16[128,512]{1,0:T(8,128)(2,1)S(1)} %get-tuple-element.15.refs_0_), channel_id=1, source_target_pairs={{0,2},{1,3},{2,0},{3,1},{4,6},{5,7},{6,4},{7,5},{8,10},{9,11},{10,... | collective-permute-start | bytes 393224 | tf_op jit(solution)/shard_map/ppermute | solution.py:340
  30.6 5.5 %copy-start = (bf16[128,4096]{1,0:T(8,128)(2,1)S(1)}, bf16[128,4096]{1,0:T(8,128)(2,1)}, u32[]{:S(2)}) copy-start(bf16[128,4096]{1,0:T(8,128)(2,1)} %slab_ref.1) | copy-start | bytes 3145732
  30.6 5.5 %copy-start.1 = (bf16[128,128]{1,0:T(8,128)(2,1)S(1)}, bf16[128,128]{1,0:T(8,128)(2,1)}, u32[]{:S(2)}) copy-start(bf16[128,128]{1,0:T(8,128)(2,1)} %cross_ref.1) | copy-start | bytes 98308
  33.0 3.1 %collective-permute-start.4 = (bf16[128,512]{1,0:T(8,128)(2,1)S(1)}, bf16[128,512]{1,0:T(8,128)(2,1)S(1)}, u32[]{:S(2)}, u32[]{:S(2)}) collective-permute-start(bf16[128,512]{1,0:T(8,128)(2,1)S(1)} %collective-permute-done.refs_2_), channel_id=1, source_target_pairs={{0,1},{1,0},{2,3},{3,2},{4,5},{5,4},{6,7},{7,6},{8,9},{9,8},{10,11... | collective-permute-start | bytes 393224 | tf_op jit(solution)/shard_map/ppermute | solution.py:340
  33.0 3.1 %collective-permute-start.5 = (bf16[128,512]{1,0:T(8,128)(2,1)S(1)}, bf16[128,512]{1,0:T(8,128)(2,1)S(1)}, u32[]{:S(2)}, u32[]{:S(2)}) collective-permute-start(bf16[128,512]{1,0:T(8,128)(2,1)S(1)} %collective-permute-done.1.refs_4_), channel_id=1, source_target_pairs={{0,1},{1,0},{2,3},{3,2},{4,5},{5,4},{6,7},{7,6},{8,9},{9,8},{10,11... | collective-permute-start | bytes 393224 | tf_op jit(solution)/shard_map/ppermute | solution.py:340
  33.5 2.6 %collective-permute-start.6 = (bf16[128,512]{1,0:T(8,128)(2,1)S(1)}, bf16[128,512]{1,0:T(8,128)(2,1)S(1)}, u32[]{:S(2)}, u32[]{:S(2)}) collective-permute-start(bf16[128,512]{1,0:T(8,128)(2,1)S(1)} %collective-permute-done.2.refs_6_), channel_id=1, source_target_pairs={{0,1},{1,0},{2,3},{3,2},{4,5},{5,4},{6,7},{7,6},{8,9},{9,8},{10,11... | collective-permute-start | bytes 393224 | tf_op jit(solution)/shard_map/ppermute | solution.py:340

commit v4 on v3

--- a/solution.py
+++ b/solution.py
@@ -88,7 +88,7 @@
 
 
 def pick_kernel(
-    groups, width, obs_hbm, slab_hbm, cross_hbm, out_hbm, obs_ref, slab, cross, out, sem, out_sem
+    groups, width, obs_hbm, slab_hbm, cross_hbm, out_hbm, picked_hbm, obs_ref, slab, cross, out, picked, sem, out_sem
 ):
     rows, count = slab.shape[0], obs_ref.shape[1]
     half = slab.shape[1] // 2
@@ -120,9 +120,10 @@
     local = lax.broadcasted_iota(jnp.int32, (count, rows), 1) == down[:, :rows] % rows
     selector = dot32(hit, jnp.where(local, 1.0, 0.0).astype(jnp.bfloat16)).astype(jnp.bfloat16)
     got_cross.wait()
-    cross_part = dot32(selector[:SLOTS], cross[...]).astype(jnp.bfloat16)
+    picked[...] = dot32(selector[:SLOTS], cross[...]).astype(jnp.bfloat16)
     lanes = width // 4
-    sent = []
+    sent = [pltpu.make_async_copy(picked, picked_hbm, out_sem.at[0])]
+    sent[0].start()
     for group in range(PLANE):
         if group % 4 == 0:
             got_slab[group // 4].wait()
@@ -135,8 +136,7 @@
                     + tail[(t + 1) * SLOTS : (t + 2) * SLOTS]
                 ).astype(jnp.bfloat16)
                 for t in range(3)
-            ]
-            + [cross_part],
+            ],
             axis=1,
         )
         if group % 2:
@@ -152,43 +152,54 @@
         copy.wait()
 
 
-def order_kernel(rows, obs_ref, noise_ref, order_ref, diagonal_ref):
+def order_kernel(rows, obs_ref, noise_ref, order_ref, cross_order_ref, diagonal_ref):
     count, slots = obs_ref.shape[1], order_ref.shape[1]
     _, down, _, rank = spread_index(obs_ref, rows)
     owner = down[:, :1] // rows
     lane = lax.broadcasted_iota(jnp.int32, (count, slots), 1)
-    within = lane % SLOTS
-    owned = owner == lane // SLOTS
-    for t in range(4):
-        hit = (
-            rank == within
-            if t == 0
-            else (within >= CAP) & (rank == within + (4 * (t - 1) - CAP))
-        )
-        order_ref[t * count : (t + 1) * count, :] = jnp.where(owned & hit, 1.0, 0.0).astype(
-            jnp.bfloat16
-        )
+    within, device = lane % SLOTS, lane // SLOTS
+
+    def one_hot(hit):
+        return jnp.where(hit, 1.0, 0.0).astype(jnp.bfloat16)
+
+    owned = owner == device
+    order_ref[:count, :] = one_hot(owned & (rank == within))
+    for t in range(3):
+        hit = (within >= CAP) & (rank == within + (4 * t - CAP))
+        order_ref[(t + 1) * count : (t + 2) * count, :] = one_hot(owned & hit)
+    apart = owner ^ lax.axis_index("rows")
+    cross_order_ref[...] = one_hot((apart == device) & (rank == within))
     square = (count, count)
     on = lax.broadcasted_iota(jnp.int32, square, 0) == lax.broadcasted_iota(jnp.int32, square, 1)
     diagonal_ref[...] = jnp.where(on, noise_ref[...], 0.0)
 
 
-def compact_kernel(order_ref, diagonal_ref, got_ref, observed_ref, inn_ref):
-    count = diagonal_ref.shape[0]
-    lanes = got_ref.shape[1] // 4
+def compact_kernel(order_ref, got_ref, observed_ref):
+    count = observed_ref.shape[0]
+    lanes = got_ref.shape[1] // 3
     head = dot32(order_ref[:count, :], got_ref[...])
     tail = jnp.zeros((count, lanes), jnp.float32)
     for t in range(3):
         hit = order_ref[(t + 1) * count : (t + 2) * count, :]
         tail += dot32(hit, got_ref[:, t * lanes : (t + 1) * lanes])
-    observed_ref[:, : 3 * lanes] = head[:, : 3 * lanes].astype(jnp.bfloat16)
+    observed_ref[:, : 3 * lanes] = head.astype(jnp.bfloat16)
     observed_ref[:, 3 * lanes :] = tail.astype(jnp.bfloat16)
-    picked = head[:, 3 * lanes :]
-    inn_ref[...] = 0.5 * (picked + picked.T) + diagonal_ref[...]
-
-
-def invert_kernel(panel_range, inn_ref, out_ref):
+
+
+def innovation_of(order_ref, diagonal_ref, *pieces):
+    span = pieces[0].shape[0]
+    picked = sum(
+        dot32(order_ref[:, i * span : (i + 1) * span], piece[...])
+        for i, piece in enumerate(pieces)
+    )
+    return 0.5 * (picked + picked.T) + diagonal_ref[...]
+
+
+def invert_kernel(panel_range, *refs):
+    sources, out_ref = refs[:-2], refs[-2]
+    inn_ref = refs[-1]
     size = inn_ref.shape[0]
+    inn_ref[...] = innovation_of(*sources) if len(sources) > 1 else sources[0][...]
     step, panels = 8, size // 8
     full = (step, size)
     m = [inn_ref[i * step : (i + 1) * step, :] for i in range(panels)]
@@ -279,65 +290,74 @@
     count = cross.shape[1]
     width = columns // PLANE
     obs = obs_index.reshape(1, count)
-    picked = pl.pallas_call(
+    packed, picked = pl.pallas_call(
         functools.partial(pick_kernel, groups, width),
-        out_shape=jax.ShapeDtypeStruct((groups * SLOTS, 3 * width // 4 + count), jnp.bfloat16),
+        out_shape=(
+            jax.ShapeDtypeStruct((groups * SLOTS, 3 * width // 4), jnp.bfloat16),
+            jax.ShapeDtypeStruct((SLOTS, count), jnp.bfloat16),
+        ),
         in_specs=[HBM] * 3,
-        out_specs=HBM,
+        out_specs=(HBM, HBM),
         scratch_shapes=[
             pltpu.VMEM((1, count), jnp.int32),
             pltpu.VMEM(slab.shape, jnp.bfloat16),
             pltpu.VMEM(cross.shape, jnp.bfloat16),
-            pltpu.VMEM((PLANE * SLOTS, 3 * width // 4 + count), jnp.bfloat16),
+            pltpu.VMEM((PLANE * SLOTS, 3 * width // 4), jnp.bfloat16),
+            pltpu.VMEM((SLOTS, count), jnp.bfloat16),
             pltpu.SemaphoreType.DMA((4,)),
-            pltpu.SemaphoreType.DMA((groups // 2,)),
+            pltpu.SemaphoreType.DMA((1 + groups // 2,)),
         ],
         compiler_params=room(56),
         name="pick",
     )(obs, slab, cross)
-    order, diagonal = pl.pallas_call(
+    order, cross_order, diagonal = pl.pallas_call(
         functools.partial(order_kernel, rows),
         out_shape=(
             jax.ShapeDtypeStruct((4 * count, groups * SLOTS), jnp.bfloat16),
+            jax.ShapeDtypeStruct((count, groups * SLOTS), jnp.bfloat16),
             jax.ShapeDtypeStruct((count, count), jnp.float32),
         ),
         in_specs=[VMEM] * 2,
-        out_specs=(VMEM,) * 2,
+        out_specs=(VMEM,) * 3,
         cost_estimate=pl.CostEstimate(
             flops=1000 * count**3, bytes_accessed=4 * count * count, transcendentals=0
         ),
         compiler_params=room(8),
         name="order",
     )(obs, noise.reshape(1, count))
+
+    def swap(value, bit):
+        return lax.ppermute(value, "rows", [(i, i ^ bit) for i in range(groups)])
+
     got = lax.all_to_all(
-        picked.reshape(groups, SLOTS, -1), "rows", split_axis=0, concat_axis=0, tiled=True
+        packed.reshape(groups, SLOTS, -1), "rows", split_axis=0, concat_axis=0, tiled=True
     ).reshape(groups * SLOTS, -1)
-    observed, innovation = pl.pallas_call(
+    chip = jnp.concatenate([picked, swap(picked, 1)])
+    plane = jnp.concatenate([chip] + [swap(chip, bits) for bits in (2, 4, 6)])
+    levels = [plane] + [swap(plane, bits) for bits in range(PLANE, groups, PLANE)]
+    observed = pl.pallas_call(
         compact_kernel,
-        out_shape=(
-            jax.ShapeDtypeStruct((count, width), jnp.bfloat16),
-            jax.ShapeDtypeStruct((count, count), jnp.float32),
-        ),
-        in_specs=[VMEM] * 3,
-        out_specs=(VMEM,) * 2,
+        out_shape=jax.ShapeDtypeStruct((count, width), jnp.bfloat16),
+        in_specs=[VMEM] * 2,
+        out_specs=VMEM,
         compiler_params=room(8),
         name="compact",
-    )(order, diagonal, got)
-    def invert(panel_range, value, out_shape):
+    )(order, got)
+    def invert(panel_range, sources, out_shape):
         return pl.pallas_call(
             functools.partial(invert_kernel, panel_range),
             out_shape=out_shape,
-            in_specs=[VMEM],
+            in_specs=[VMEM] * len(sources),
             out_specs=VMEM,
+            scratch_shapes=[pltpu.VMEM((count, count), jnp.float32)],
             cost_estimate=pl.CostEstimate(
-                flops=1500 * count**3, bytes_accessed=4 * count * count, transcendentals=count
+                flops=200 * len(panel_range) * count**3,
+                bytes_accessed=4 * count * count,
+                transcendentals=count,
             ),
             compiler_params=room(4),
             name="invert",
-        )(value)
-
-    def swap(value, bit):
-        return lax.ppermute(value, "rows", [(i, i ^ bit) for i in range(groups)])
+        )(*sources)
 
     def update(inverse, flips, pieces, before):
         more = () if before is None else (before,)
@@ -355,18 +375,20 @@
             name="update",
         )(inverse, cross, slab, *pieces, *more)
 
-    panels = count // 8
     by = {0: observed, 1: swap(observed, 1)}
     by.update({group: swap(observed, bit) for bit, group in ((2, 2), (4, 4), (8, 6))})
-    midway = invert(range(panels // 2), innovation, innovation)
+    panels, early = count // 8, 3 * count // 32
+    midway = invert(
+        range(early),
+        (cross_order, diagonal, *levels),
+        jax.ShapeDtypeStruct((count, count), jnp.float32),
+    )
     arrived, midway = lax.optimization_barrier(([by[g] for g in (2, 4, 6)], midway))
     for group, piece in zip((2, 4, 6), arrived):
         by[group] = piece
         by[group + 1] = swap(piece, 1)
     inverse = invert(
-        range(panels // 2, panels),
-        midway,
-        jax.ShapeDtypeStruct((PARTS * count, count), jnp.bfloat16),
+        range(early, panels), (midway,), jax.ShapeDtypeStruct((PARTS * count, count), jnp.bfloat16)
     )
     flips = tuple(range(PLANE))
     return update(inverse, flips, [by[f] for f in flips], None)

time: 38.2 us -> 35.3 us (0.924)
  waiting for transfers between devices: 16.8 us -> 4.98 us
  starting transfers between devices: 10.6 us -> 19.6 us
  local copies, waits for them, and re-layouts: 0.67 us -> 0.06 us
  Pallas kernels: 9.81 us -> 10.2 us
    all_to_all x1, waiting for transfers between devices: 14.4 us -> 0.65 us  [plane_body(): lax.all_to_all(packed.reshape(groups, SLOTS, -1), 'rows', split_axis=0, c...]
    ppermute x7 -> x14, starting transfers between devices: 3.26 us -> 12.3 us  [swap(): return lax.ppermute(value, 'rows', [(i, i ^ bit) for i in range(groups)])]
    ppermute x7 -> x14, waiting for transfers between devices: 2.38 us -> 4.33 us  [swap(): return lax.ppermute(value, 'rows', [(i, i ^ bit) for i in range(groups)])]
    unnamed x8 -> x13, local copies, waits for them, and re-layouts: 0.67 us -> 0.04 us
  transfers between devices with their start and end apart: 8 -> 15, of which waited for: 4 -> 4; matrix products, arithmetic and copies ran while one was open for 0% -> 0% of each run, Pallas kernels for 14% -> 17%
where the time goes in v4:
time: 35.3 us; the launch traced here: 35 us
  starting transfers between devices  19.6 us (56%)
  Pallas kernels  10.2 us (29%)
  waiting for transfers between devices  4.98 us (14%)
    ppermute x14, starting transfers between devices, swap(): return lax.ppermute(value, 'rows', [(i, i ^ bit) for i in range(groups)])  12.3 us
    all_to_all x1, starting transfers between devices, plane_body(): lax.all_to_all(packed.reshape(groups, SLOTS, -1), 'rows', split_axis=0, c...  7.3 us
    pallas_call x2, Pallas kernels, invert(): pl.pallas_call(functools.partial(invert_kernel, panel_range), out_shape=o...  5.18 us
    ppermute x14, waiting for transfers between devices, swap(): return lax.ppermute(value, 'rows', [(i, i ^ bit) for i in range(groups)])  4.33 us
    pallas_call x1, Pallas kernels, plane_body(): pl.pallas_call(functools.partial(pick_kernel, groups, width), out_shape=(...  2.34 us
    pallas_call x1, Pallas kernels, update(): pl.pallas_call(functools.partial(update_kernel, width, flips), out_shape=...  1.78 us
  transfers between devices with their start and end apart: 15, of which 4 were waited for; matrix products, arithmetic and copies ran while one was open for 0% of the time, Pallas kernels for 17%

profile of v4, /device:TPU:0, one launch (start us, length us, event | category | flops | bytes accessed | tf_op | source)
XLA Modules:
  0.0 35.0 jit_solution(11177708486406591013)
XLA Ops:
  0.0 2.3 %pick.1 = (bf16[512,384]{1,0:T(8,128)(2,1)}, bf16[16,128]{1,0:T(8,128)(2,1)}) custom-call(s32[1,128]{1,0:T(1,128)} %bitcast.5, bf16[128,4096]{1,0:T(8,128)(2,1)} %slab_ref.1, bf16[128,128]{1,0:T(8,128)(2,1)} %cross_ref.1), custom_call_target="tpu_custom_call" | custom-call | tf_op jit(solution)/shard_map/pick/pallas_call | solution.py:293
  2.4 7.3 %all-to-all-start = ((bf16[32,16,384]{2,1,0:T(8,128)(2,1)}), bf16[32,16,384]{2,1,0:T(8,128)(2,1)S(1)}, u32[]{:S(2)}, u32[]{:S(2)}) async-start(bf16[32,16,384]{2,1,0:T(8,128)(2,1)} %bitcast.8), calls=%async_computation | async-start | bytes 786432 | tf_op jit(solution)/shard_map/all_to_all | solution.py:332
  9.7 0.3 collective-permute-start.3
  10.0 0.9 %collective-permute-done.3 = bf16[16,128]{1,0:T(8,128)(2,1)S(1)} collective-permute-done((bf16[16,128]{1,0:T(8,128)(2,1)S(1)}, bf16[16,128]{1,0:T(8,128)(2,1)S(1)}, u32[]{:S(2)}, u32[]{:S(2)}) %collective-permute-start.3) | collective-permute-done | bytes 4128 | tf_op jit(solution)/shard_map/ppermute | solution.py:330
  10.9 1.8 %collective-permute-start.4 = (bf16[32,128]{1,0:T(8,128)(2,1)S(1)}, bf16[32,128]{1,0:T(8,128)(2,1)S(1)}, u32[]{:S(2)}, u32[]{:S(2)}) collective-permute-start(bf16[32,128]{1,0:T(8,128)(2,1)S(1)} %get-tuple-element.23), channel_id=1, source_target_pairs={{0,2},{1,3},{2,0},{3,1},{4,6},{5,7},{6,4},{7,5},{8,10},{9,11},{10,... | collective-permute-start | bytes 24584 | tf_op jit(solution)/shard_map/ppermute | solution.py:330
  12.7 1.5 %collective-permute-start.6 = (bf16[32,128]{1,0:T(8,128)(2,1)S(1)}, bf16[32,128]{1,0:T(8,128)(2,1)S(1)}, u32[]{:S(2)}, u32[]{:S(2)}) collective-permute-start(bf16[32,128]{1,0:T(8,128)(2,1)S(1)} %get-tuple-element.23), channel_id=1, source_target_pairs={{0,6},{1,7},{2,4},{3,5},{4,2},{5,3},{6,0},{7,1},{8,14},{9,15},{10,... | collective-permute-start | bytes 24584 | tf_op jit(solution)/shard_map/ppermute | solution.py:330
  14.1 0.3 collective-permute-start.5
  14.4 0.2 collective-permute-done.4
  14.6 3.2 %collective-permute-done.5 = bf16[32,128]{1,0:T(8,128)(2,1)S(1)} collective-permute-done((bf16[32,128]{1,0:T(8,128)(2,1)S(1)}, bf16[32,128]{1,0:T(8,128)(2,1)S(1)}, u32[]{:S(2)}, u32[]{:S(2)}) %collective-permute-start.5) | collective-permute-done | bytes 8224 | tf_op jit(solution)/shard_map/ppermute | solution.py:330
  17.8 0.0 collective-permute-done.6
  17.8 0.0 copy-start.3
  17.8 3.5 %collective-permute-start.9 = (bf16[128,128]{1,0:T(8,128)(2,1)S(1)}, bf16[128,128]{1,0:T(8,128)(2,1)S(1)}, u32[]{:S(2)}, u32[]{:S(2)}) collective-permute-start(bf16[128,128]{1,0:T(8,128)(2,1)S(1)} %constant_dynamic-update-slice_fusion.2.refs_2_), channel_id=1, source_target_pairs={{0,24},{1,25},{2,26},{3,27},{4,28},{5,29},{6,30},{7,31},{8,16},{9,... | collective-permute-start | bytes 98312 | tf_op jit(solution)/shard_map/ppermute | solution.py:330
  21.3 0.0 collective-permute-start.8
  21.3 1.0 %collective-permute-start.7 = (bf16[128,128]{1,0:T(8,128)(2,1)S(1)}, bf16[128,128]{1,0:T(8,128)(2,1)S(1)}, u32[]{:S(2)}, u32[]{:S(2)}) collective-permute-start(bf16[128,128]{1,0:T(8,128)(2,1)S(1)} %constant_dynamic-update-slice_fusion.2.refs_2_), channel_id=1, source_target_pairs={{0,8},{1,9},{2,10},{3,11},{4,12},{5,13},{6,14},{7,15},{8,0},{9,1},... | collective-permute-start | bytes 98312 | tf_op jit(solution)/shard_map/ppermute | solution.py:330
  22.3 0.6 %order.1 = (bf16[512,512]{1,0:T(8,128)(2,1)S(1)}, bf16[128,512]{1,0:T(8,128)(2,1)S(1)}, f32[128,128]{1,0:T(8,128)S(1)}) custom-call(s32[1,128]{1,0:T(1,128)S(1)} %bitcast.6, f32[1,128]{1,0:T(1,128)S(1)} %bitcast.7), custom_call_target="tpu_custom_call" | custom-call | flops 2097152000 | bytes 65536 | tf_op jit(solution)/shard_map/order/pallas_call | solution.py:313
  22.9 0.7 %all-to-all-done = bf16[32,16,384]{2,1,0:T(8,128)(2,1)S(1)} async-done(((bf16[32,16,384]{2,1,0:T(8,128)(2,1)}), bf16[32,16,384]{2,1,0:T(8,128)(2,1)S(1)}, u32[]{:S(2)}, u32[]{:S(2)}) %all-to-all-start) | async-done | bytes 393248 | tf_op jit(solution)/shard_map/all_to_all | solution.py:332
  23.5 0.3 compact.1.refs_0_
  23.9 1.2 %collective-permute-start.2 = (bf16[128,512]{1,0:T(8,128)(2,1)S(1)}, bf16[128,512]{1,0:T(8,128)(2,1)S(1)}, u32[]{:S(2)}, u32[]{:S(2)}) collective-permute-start(bf16[128,512]{1,0:T(8,128)(2,1)S(1)} %compact.1.refs_0_), channel_id=1, source_target_pairs={{0,8},{1,9},{2,10},{3,11},{4,12},{5,13},{6,14},{7,15},{8,0},{9,1},... | collective-permute-start | bytes 393224 | tf_op jit(solution)/shard_map/ppermute | solution.py:330
  25.0 0.4 %collective-permute-start.1 = (bf16[128,512]{1,0:T(8,128)(2,1)S(1)}, bf16[128,512]{1,0:T(8,128)(2,1)S(1)}, u32[]{:S(2)}, u32[]{:S(2)}) collective-permute-start(bf16[128,512]{1,0:T(8,128)(2,1)S(1)} %compact.1.refs_0_), channel_id=1, source_target_pairs={{0,4},{1,5},{2,6},{3,7},{4,0},{5,1},{6,2},{7,3},{8,12},{9,13},{10,... | collective-permute-start | bytes 393224 | tf_op jit(solution)/shard_map/ppermute | solution.py:330
  25.5 0.0 collective-permute-done.9.refs_5_
  25.5 1.3 %collective-permute-start = (bf16[128,512]{1,0:T(8,128)(2,1)S(1)}, bf16[128,512]{1,0:T(8,128)(2,1)S(1)}, u32[]{:S(2)}, u32[]{:S(2)}) collective-permute-start(bf16[128,512]{1,0:T(8,128)(2,1)S(1)} %compact.1.refs_0_), channel_id=1, source_target_pairs={{0,2},{1,3},{2,0},{3,1},{4,6},{5,7},{6,4},{7,5},{8,10},{9,11},{10,... | collective-permute-start | bytes 393224 | tf_op jit(solution)/shard_map/ppermute | solution.py:330
  26.8 3.8 %invert.2.refs_0_ = f32[128,128]{1,0:T(8,128)S(1)} custom-call(bf16[128,512]{1,0:T(8,128)(2,1)S(1)} %get-tuple-element.16.refs_0_, f32[128,128]{1,0:T(8,128)S(1)} %get-tuple-element.17.refs_1_, bf16[128,128]{1,0:T(8,128)(2,1)S(1)} %constant_dynamic-update-slice_fusion.2.refs_2_, bf16[128,128]{1,0:T(8,128)(2,1)S(1)} %collective-permute-done.7.refs_3_, ...), custom_call_target="tpu_custom_call" | custom-call | flops 5033164800 | bytes 65536 | tf_op jit(solution)/shard_map/invert/pallas_call | solution.py:347
  30.6 0.0 copy-start
  30.7 0.0 copy-start.1
  30.7 0.1 collective-permute-start.10
  30.8 0.0 collective-permute-done.1.refs_4_
  30.8 0.5 %collective-permute-start.11 = (bf16[128,512]{1,0:T(8,128)(2,1)S(1)}, bf16[128,512]{1,0:T(8,128)(2,1)S(1)}, u32[]{:S(2)}, u32[]{:S(2)}) collective-permute-start(bf16[128,512]{1,0:T(8,128)(2,1)S(1)} %collective-permute-done.refs_2_), channel_id=1, source_target_pairs={{0,1},{1,0},{2,3},{3,2},{4,5},{5,4},{6,7},{7,6},{8,9},{9,8},{10,11... | collective-permute-start | bytes 393224 | tf_op jit(solution)/shard_map/ppermute | solution.py:330
  31.3 0.1 collective-permute-start.12
  31.4 0.4 %collective-permute-start.13 = (bf16[128,512]{1,0:T(8,128)(2,1)S(1)}, bf16[128,512]{1,0:T(8,128)(2,1)S(1)}, u32[]{:S(2)}, u32[]{:S(2)}) collective-permute-start(bf16[128,512]{1,0:T(8,128)(2,1)S(1)} %collective-permute-done.2.refs_6_), channel_id=1, source_target_pairs={{0,1},{1,0},{2,3},{3,2},{4,5},{5,4},{6,7},{7,6},{8,9},{9,8},{10,11... | collective-permute-start | bytes 393224 | tf_op jit(solution)/shard_map/ppermute | solution.py:330
  31.8 1.4 %invert.3.inverse_ref = bf16[384,128]{1,0:T(8,128)(2,1)S(1)} custom-call(f32[128,128]{1,0:T(8,128)S(1)} %invert.2.refs_0_), custom_call_target="tpu_custom_call" | custom-call | flops 1677721600 | bytes 65536 | tf_op jit(solution)/shard_map/invert/pallas_call | solution.py:347
  33.2 0.0 collective-permute-done.10.refs_1_
  33.3 1.8 %update.1 = bf16[128,4096]{1,0:T(8,128)(2,1)} custom-call(bf16[384,128]{1,0:T(8,128)(2,1)S(1)} %invert.3.inverse_ref, bf16[128,128]{1,0:T(8,128)(2,1)S(1)} %copy-done.1, bf16[128,4096]{1,0:T(8,128)(2,1)S(1)} %copy-done, bf16[128,512]{1,0:T(8,128)(2,1)S(1)} %compact.1.refs_0_, bf16[128,512]{1,0:T(8,128)(2,1)S(1)} %collective-permute-done.10.refs_1_, ...), custom_call_target="tpu_custom_call" | custom-call | tf_op jit(solution)/shard_map/update/pallas_call | solution.py:364
  (19 shorter events, 0.1 us)
Async XLA Ops:
  2.3 7.3 %copy-start.4 = (bf16[16,128]{1,0:T(8,128)(2,1)S(1)}, bf16[16,128]{1,0:T(8,128)(2,1)}, u32[]{:S(2)}) copy-start(bf16[16,128]{1,0:T(8,128)(2,1)} %get-tuple-element.18) | copy-start | bytes 12292
  2.4 21.2 %all-to-all-start = ((bf16[32,16,384]{2,1,0:T(8,128)(2,1)}), bf16[32,16,384]{2,1,0:T(8,128)(2,1)S(1)}, u32[]{:S(2)}, u32[]{:S(2)}) async-start(bf16[32,16,384]{2,1,0:T(8,128)(2,1)} %bitcast.8), calls=%async_computation | async-start | bytes 786432 | tf_op jit(solution)/shard_map/all_to_all | solution.py:332
  9.7 1.2 %collective-permute-start.3 = (bf16[16,128]{1,0:T(8,128)(2,1)S(1)}, bf16[16,128]{1,0:T(8,128)(2,1)S(1)}, u32[]{:S(2)}, u32[]{:S(2)}) collective-permute-start(bf16[16,128]{1,0:T(8,128)(2,1)S(1)} %copy-done.4), channel_id=1, source_target_pairs={{0,1},{1,0},{2,3},{3,2},{4,5},{5,4},{6,7},{7,6},{8,9},{9,8},{10,11... | collective-permute-start | bytes 12296 | tf_op jit(solution)/shard_map/ppermute | solution.py:330
  10.9 3.7 %collective-permute-start.4 = (bf16[32,128]{1,0:T(8,128)(2,1)S(1)}, bf16[32,128]{1,0:T(8,128)(2,1)S(1)}, u32[]{:S(2)}, u32[]{:S(2)}) collective-permute-start(bf16[32,128]{1,0:T(8,128)(2,1)S(1)} %get-tuple-element.23), channel_id=1, source_target_pairs={{0,2},{1,3},{2,0},{3,1},{4,6},{5,7},{6,4},{7,5},{8,10},{9,11},{10,... | collective-permute-start | bytes 24584 | tf_op jit(solution)/shard_map/ppermute | solution.py:330
  12.7 5.1 %collective-permute-start.6 = (bf16[32,128]{1,0:T(8,128)(2,1)S(1)}, bf16[32,128]{1,0:T(8,128)(2,1)S(1)}, u32[]{:S(2)}, u32[]{:S(2)}) collective-permute-start(bf16[32,128]{1,0:T(8,128)(2,1)S(1)} %get-tuple-element.23), channel_id=1, source_target_pairs={{0,6},{1,7},{2,4},{3,5},{4,2},{5,3},{6,0},{7,1},{8,14},{9,15},{10,... | collective-permute-start | bytes 24584 | tf_op jit(solution)/shard_map/ppermute | solution.py:330
  14.1 3.7 %collective-permute-start.5 = (bf16[32,128]{1,0:T(8,128)(2,1)S(1)}, bf16[32,128]{1,0:T(8,128)(2,1)S(1)}, u32[]{:S(2)}, u32[]{:S(2)}) collective-permute-start(bf16[32,128]{1,0:T(8,128)(2,1)S(1)} %get-tuple-element.23), channel_id=1, source_target_pairs={{0,4},{1,5},{2,6},{3,7},{4,0},{5,1},{6,2},{7,3},{8,12},{9,13},{10,... | collective-permute-start | bytes 24584 | tf_op jit(solution)/shard_map/ppermute | solution.py:330
  17.8 4.5 %copy-start.2 = (s32[128]{0:T(128)S(1)}, s32[128]{0:T(128)}, u32[]{:S(2)}) copy-start(s32[128]{0:T(128)} %param.6) | copy-start | bytes 1540
  17.8 4.5 %copy-start.3 = (f32[128]{0:T(128)S(1)}, f32[128]{0:T(128)}, u32[]{:S(2)}) copy-start(f32[128]{0:T(128)} %param.7) | copy-start | bytes 1540
  17.8 7.6 %collective-permute-start.9 = (bf16[128,128]{1,0:T(8,128)(2,1)S(1)}, bf16[128,128]{1,0:T(8,128)(2,1)S(1)}, u32[]{:S(2)}, u32[]{:S(2)}) collective-permute-start(bf16[128,128]{1,0:T(8,128)(2,1)S(1)} %constant_dynamic-update-slice_fusion.2.refs_2_), channel_id=1, source_target_pairs={{0,24},{1,25},{2,26},{3,27},{4,28},{5,29},{6,30},{7,31},{8,16},{9,... | collective-permute-start | bytes 98312 | tf_op jit(solution)/shard_map/ppermute | solution.py:330
  21.3 5.5 %collective-permute-start.8 = (bf16[128,128]{1,0:T(8,128)(2,1)S(1)}, bf16[128,128]{1,0:T(8,128)(2,1)S(1)}, u32[]{:S(2)}, u32[]{:S(2)}) collective-permute-start(bf16[128,128]{1,0:T(8,128)(2,1)S(1)} %constant_dynamic-update-slice_fusion.2.refs_2_), channel_id=1, source_target_pairs={{0,16},{1,17},{2,18},{3,19},{4,20},{5,21},{6,22},{7,23},{8,24},{9,... | collective-permute-start | bytes 98312 | tf_op jit(solution)/shard_map/ppermute | solution.py:330
  21.3 5.5 %collective-permute-start.7 = (bf16[128,128]{1,0:T(8,128)(2,1)S(1)}, bf16[128,128]{1,0:T(8,128)(2,1)S(1)}, u32[]{:S(2)}, u32[]{:S(2)}) collective-permute-start(bf16[128,128]{1,0:T(8,128)(2,1)S(1)} %constant_dynamic-update-slice_fusion.2.refs_2_), channel_id=1, source_target_pairs={{0,8},{1,9},{2,10},{3,11},{4,12},{5,13},{6,14},{7,15},{8,0},{9,1},... | collective-permute-start | bytes 98312 | tf_op jit(solution)/shard_map/ppermute | solution.py:330
  23.9 6.9 %collective-permute-start.2 = (bf16[128,512]{1,0:T(8,128)(2,1)S(1)}, bf16[128,512]{1,0:T(8,128)(2,1)S(1)}, u32[]{:S(2)}, u32[]{:S(2)}) collective-permute-start(bf16[128,512]{1,0:T(8,128)(2,1)S(1)} %compact.1.refs_0_), channel_id=1, source_target_pairs={{0,8},{1,9},{2,10},{3,11},{4,12},{5,13},{6,14},{7,15},{8,0},{9,1},... | collective-permute-start | bytes 393224 | tf_op jit(solution)/shard_map/ppermute | solution.py:330
  25.0 5.7 %collective-permute-start.1 = (bf16[128,512]{1,0:T(8,128)(2,1)S(1)}, bf16[128,512]{1,0:T(8,128)(2,1)S(1)}, u32[]{:S(2)}, u32[]{:S(2)}) collective-permute-start(bf16[128,512]{1,0:T(8,128)(2,1)S(1)} %compact.1.refs_0_), channel_id=1, source_target_pairs={{0,4},{1,5},{2,6},{3,7},{4,0},{5,1},{6,2},{7,3},{8,12},{9,13},{10,... | collective-permute-start | bytes 393224 | tf_op jit(solution)/shard_map/ppermute | solution.py:330
  25.5 5.3 %collective-permute-start = (bf16[128,512]{1,0:T(8,128)(2,1)S(1)}, bf16[128,512]{1,0:T(8,128)(2,1)S(1)}, u32[]{:S(2)}, u32[]{:S(2)}) collective-permute-start(bf16[128,512]{1,0:T(8,128)(2,1)S(1)} %compact.1.refs_0_), channel_id=1, source_target_pairs={{0,2},{1,3},{2,0},{3,1},{4,6},{5,7},{6,4},{7,5},{8,10},{9,11},{10,... | collective-permute-start | bytes 393224 | tf_op jit(solution)/shard_map/ppermute | solution.py:330
  30.6 2.6 %copy-start = (bf16[128,4096]{1,0:T(8,128)(2,1)S(1)}, bf16[128,4096]{1,0:T(8,128)(2,1)}, u32[]{:S(2)}) copy-start(bf16[128,4096]{1,0:T(8,128)(2,1)} %slab_ref.1) | copy-start | bytes 3145732
  30.7 2.6 %copy-start.1 = (bf16[128,128]{1,0:T(8,128)(2,1)S(1)}, bf16[128,128]{1,0:T(8,128)(2,1)}, u32[]{:S(2)}) copy-start(bf16[128,128]{1,0:T(8,128)(2,1)} %cross_ref.1) | copy-start | bytes 98308
  30.7 2.5 %collective-permute-start.10 = (bf16[128,512]{1,0:T(8,128)(2,1)S(1)}, bf16[128,512]{1,0:T(8,128)(2,1)S(1)}, u32[]{:S(2)}, u32[]{:S(2)}) collective-permute-start(bf16[128,512]{1,0:T(8,128)(2,1)S(1)} %compact.1.refs_0_), channel_id=1, source_target_pairs={{0,1},{1,0},{2,3},{3,2},{4,5},{5,4},{6,7},{7,6},{8,9},{9,8},{10,11... | collective-permute-start | bytes 393224 | tf_op jit(solution)/shard_map/ppermute | solution.py:330
  30.8 2.4 %collective-permute-start.11 = (bf16[128,512]{1,0:T(8,128)(2,1)S(1)}, bf16[128,512]{1,0:T(8,128)(2,1)S(1)}, u32[]{:S(2)}, u32[]{:S(2)}) collective-permute-start(bf16[128,512]{1,0:T(8,128)(2,1)S(1)} %collective-permute-done.refs_2_), channel_id=1, source_target_pairs={{0,1},{1,0},{2,3},{3,2},{4,5},{5,4},{6,7},{7,6},{8,9},{9,8},{10,11... | collective-permute-start | bytes 393224 | tf_op jit(solution)/shard_map/ppermute | solution.py:330
  31.3 1.9 %collective-permute-start.12 = (bf16[128,512]{1,0:T(8,128)(2,1)S(1)}, bf16[128,512]{1,0:T(8,128)(2,1)S(1)}, u32[]{:S(2)}, u32[]{:S(2)}) collective-permute-start(bf16[128,512]{1,0:T(8,128)(2,1)S(1)} %collective-permute-done.1.refs_4_), channel_id=1, source_target_pairs={{0,1},{1,0},{2,3},{3,2},{4,5},{5,4},{6,7},{7,6},{8,9},{9,8},{10,11... | collective-permute-start | bytes 393224 | tf_op jit(solution)/shard_map/ppermute | solution.py:330
  31.4 1.8 %collective-permute-start.13 = (bf16[128,512]{1,0:T(8,128)(2,1)S(1)}, bf16[128,512]{1,0:T(8,128)(2,1)S(1)}, u32[]{:S(2)}, u32[]{:S(2)}) collective-permute-start(bf16[128,512]{1,0:T(8,128)(2,1)S(1)} %collective-permute-done.2.refs_6_), channel_id=1, source_target_pairs={{0,1},{1,0},{2,3},{3,2},{4,5},{5,4},{6,7},{7,6},{8,9},{9,8},{10,11... | collective-permute-start | bytes 393224 | tf_op jit(solution)/shard_map/ppermute | solution.py:330

commit v5 on v4

--- a/solution.py
+++ b/solution.py
@@ -195,67 +195,103 @@
     return 0.5 * (picked + picked.T) + diagonal_ref[...]
 
 
-def invert_kernel(panel_range, *refs):
-    sources, out_ref = refs[:-2], refs[-2]
-    inn_ref = refs[-1]
-    size = inn_ref.shape[0]
-    inn_ref[...] = innovation_of(*sources) if len(sources) > 1 else sources[0][...]
-    step, panels = 8, size // 8
-    full = (step, size)
-    m = [inn_ref[i * step : (i + 1) * step, :] for i in range(panels)]
+def tree_sum(terms):
+    while len(terms) > 1:
+        terms = [x + y for x, y in zip(terms[::2], terms[1::2])]
+    return terms[0]
+
+
+def sweep(e, step):
+    def at(i, k):
+        return max(i, k), min(i, k)
+
+    for k in range(0, step, 2):
+        a, b, c = e[k, k], e[k + 1, k], e[k + 1, k + 1]
+        over = 1.0 / (a * c - b * b)
+        pa, pb, pc = c * over, -b * over, a * over
+        others = [i for i in range(step) if i not in (k, k + 1)]
+        u = {i: e[at(i, k)] for i in others}
+        v = {i: e[at(i, k + 1)] for i in others}
+        su = {i: u[i] * pa + v[i] * pb for i in others}
+        sv = {i: u[i] * pb + v[i] * pc for i in others}
+        for i in others:
+            for j in others:
+                if j <= i:
+                    e[i, j] = e[i, j] - (su[i] * u[j] + sv[i] * v[j])
+        for i in others:
+            e[at(i, k)], e[at(i, k + 1)] = su[i], sv[i]
+        e[k, k], e[k + 1, k], e[k + 1, k + 1] = -pa, -pb, -pc
+
+
+def invert_kernel(panel_range, sources, *refs):
+    inputs, outputs, (spread_ref,) = refs[:sources], refs[sources:-1], refs[-1:]
+    step = 8
+    first, stop = panel_range[0], panel_range[-1] + 1
+    if first == 0:
+        inn = innovation_of(*inputs)
+        state_ref, solved_ref = outputs
+        size = inn.shape[0]
+        state_ref[...] = inn
+        given = state_ref
+    else:
+        given, solved_before = inputs
+        out_ref, state_ref, solved_ref = outputs
+        size = given.shape[0]
+        done = first * step
+        state_ref[:done, :] = given[:done, :]
+        solved_ref[:done, :] = solved_before[:done, :]
+    full, panels = (step, size), size // step
+    m = {i: given[i * step : (i + 1) * step, :] for i in range(first, panels)}
     sub = lax.broadcasted_iota(jnp.int32, full, 0)
     lane = lax.broadcasted_iota(jnp.int32, full, 1)
     for p in panel_range:
-        at = p * step
-        on = lane == sub + at
+        at, base = p * step, (p % 2) * (step + 1)
         row = m[p]
-        spread = [jnp.broadcast_to(row[:, at + k : at + k + 1], full) for k in range(step)]
-        e = {}
-        for i in range(step):
-            for k in range(i + 1):
-                e[i, k] = jnp.broadcast_to(spread[k][i : i + 1, :], full)
-        get = lambda i, k: e[max(i, k), min(i, k)]
         for k in range(step):
-            d = 1.0 / e[k, k]
-            col = {i: get(i, k) for i in range(step) if i != k}
-            scaled = {i: v * d for i, v in col.items()}
-            for i in range(step):
-                for j in range(i + 1):
-                    if i != k and j != k:
-                        e[i, j] = e[i, j] - scaled[i] * col[j]
-            for i, v in scaled.items():
-                e[max(i, k), min(i, k)] = v
-            e[k, k] = -d
-        less = row - jnp.where(on, 1.0, 0.0)
-        rows_b = [jnp.broadcast_to(less[k : k + 1, :], full) for k in range(step)]
-        q = []
-        for i in range(step):
-            terms = [get(i, k) * rows_b[k] for k in range(step)]
-            while len(terms) > 1:
-                terms = [x + y for x, y in zip(terms[::2], terms[1::2])]
-            q.append(terms[0])
-        for i in range(panels):
-            base = less if i == p else m[i]
-            cols = (
-                [jnp.broadcast_to(base[:, at + k : at + k + 1], full) for k in range(step)]
-            )
-            terms = [cols[k] * q[k] for k in range(step)]
-            while len(terms) > 1:
-                terms = [x + y for x, y in zip(terms[::2], terms[1::2])]
-            m[i] = m[i] + terms[0]
-            if i == p:
-                m[i] = m[i] - jnp.where(on, 2.0, 0.0)
-    if panel_range[-1] < panels - 1:
-        for i in range(panels):
-            out_ref[i * step : (i + 1) * step, :] = m[i]
+            spread_ref[base + k] = jnp.broadcast_to(row[:, at + k : at + k + 1], full)
+        e = {
+            (i, k): jnp.broadcast_to(spread_ref[base + k, i : i + 1, :], full)
+            for i in range(step)
+            for k in range(i + 1)
+        }
+        inside = (lane >= at) & (lane < at + step)
+        known = lane < at + step
+        unit = jnp.where(inside, jnp.where(lane == sub + at, 1.0, 0.0), row)
+        spread_ref[base + step] = unit
+        sweep(e, step)
+        rows_b = [
+            jnp.broadcast_to(spread_ref[base + step, k : k + 1, :], full) for k in range(step)
+        ]
+        q = [
+            tree_sum([e[max(i, k), min(i, k)] * rows_b[k] for k in range(step)])
+            for i in range(step)
+        ]
+        for i in range(p + 1, panels):
+            terms = [
+                jnp.broadcast_to(m[i][:, at + k : at + k + 1], full) * q[k] for k in range(step)
+            ]
+            m[i] = jnp.where(inside, 0.0, m[i]) + tree_sum(terms)
+        solved = q[0]
+        for i in range(1, step):
+            solved = jnp.where(sub == i, q[i], solved)
+        state_ref[at : at + step, :] = jnp.where(known, unit, 0.0)
+        solved_ref[at : at + step, :] = jnp.where(known, -solved, 0.0)
+    if stop < panels:
+        for i in range(stop, panels):
+            state_ref[i * step : (i + 1) * step, :] = m[i]
+        solved_ref[stop * step :, :] = jnp.zeros((size - stop * step, size), jnp.float32)
         return
-    for i in range(0, panels, 2):
-        x = -jnp.concatenate([m[i], m[i + 1]], axis=0)
-        for part in range(PARTS):
-            piece = x.astype(jnp.bfloat16)
-            at = part * size + i * step
-            out_ref[at : at + 2 * step, :] = piece
-            x = x - piece.astype(jnp.float32)
+    x = lax.dot_general(
+        state_ref[...],
+        solved_ref[...],
+        (((0,), (0,)), ((), ())),
+        precision=lax.Precision.HIGHEST,
+        preferred_element_type=jnp.float32,
+    )
+    for part in range(PARTS):
+        piece = x.astype(jnp.bfloat16)
+        out_ref[part * size : (part + 1) * size, :] = piece
+        x = x - piece.astype(jnp.float32)
 
 
 def update_kernel(width, flips, inverse_ref, cross_ref, slab_ref, *refs):
@@ -343,13 +379,18 @@
         compiler_params=room(8),
         name="compact",
     )(order, got)
-    def invert(panel_range, sources, out_shape):
+    square = jax.ShapeDtypeStruct((count, count), jnp.float32)
+
+    def invert(panel_range, sources):
+        first = panel_range[0] == 0
+        parts = jax.ShapeDtypeStruct((PARTS * count, count), jnp.bfloat16)
         return pl.pallas_call(
-            functools.partial(invert_kernel, panel_range),
-            out_shape=out_shape,
+            functools.partial(invert_kernel, panel_range, len(sources)),
+            out_shape=(square, square) if first else parts,
             in_specs=[VMEM] * len(sources),
-            out_specs=VMEM,
-            scratch_shapes=[pltpu.VMEM((count, count), jnp.float32)],
+            out_specs=(VMEM, VMEM) if first else VMEM,
+            scratch_shapes=([] if first else [pltpu.VMEM((count, count), jnp.float32)] * 2)
+            + [pltpu.VMEM((18, 8, count), jnp.float32)],
             cost_estimate=pl.CostEstimate(
                 flops=200 * len(panel_range) * count**3,
                 bytes_accessed=4 * count * count,
@@ -377,19 +418,13 @@
 
     by = {0: observed, 1: swap(observed, 1)}
     by.update({group: swap(observed, bit) for bit, group in ((2, 2), (4, 4), (8, 6))})
-    panels, early = count // 8, 3 * count // 32
-    midway = invert(
-        range(early),
-        (cross_order, diagonal, *levels),
-        jax.ShapeDtypeStruct((count, count), jnp.float32),
-    )
+    panels, early = count // 8, 12 * count // 128
+    midway = invert(range(early), (cross_order, diagonal, *levels))
     arrived, midway = lax.optimization_barrier(([by[g] for g in (2, 4, 6)], midway))
     for group, piece in zip((2, 4, 6), arrived):
         by[group] = piece
         by[group + 1] = swap(piece, 1)
-    inverse = invert(
-        range(early, panels), (midway,), jax.ShapeDtypeStruct((PARTS * count, count), jnp.bfloat16)
-    )
+    inverse = invert(range(early, panels), tuple(midway))
     flips = tuple(range(PLANE))
     return update(inverse, flips, [by[f] for f in flips], None)
 

time: 35.3 us -> 34.4 us (0.975)
  Pallas kernels: 10.2 us -> 8.6 us
  waiting for transfers between devices: 4.98 us -> 6.18 us
  starting transfers between devices: 19.6 us -> 19.1 us
    pallas_call x2, Pallas kernels: 5.18 us -> 3.57 us  [invert(): pl.pallas_call(functools.partial(invert_kernel, panel_range, len(sources)...]
    ppermute x14, waiting for transfers between devices: 4.33 us -> 5.52 us  [swap(): return lax.ppermute(value, 'rows', [(i, i ^ bit) for i in range(groups)])]
    ppermute x14, starting transfers between devices: 12.3 us -> 11.8 us  [swap(): return lax.ppermute(value, 'rows', [(i, i ^ bit) for i in range(groups)])]
  transfers between devices with their start and end apart: 15 -> 15, of which waited for: 4 -> 7; matrix products, arithmetic and copies ran while one was open for 0% -> 0% of each run, Pallas kernels for 17% -> 13%
where the time goes in v5:
time: 34.4 us; the launch traced here: 34.1 us
  starting transfers between devices  19.1 us (56%)
  Pallas kernels  8.6 us (25%)
  waiting for transfers between devices  6.18 us (18%)
    ppermute x14, starting transfers between devices, swap(): return lax.ppermute(value, 'rows', [(i, i ^ bit) for i in range(groups)])  11.8 us
    all_to_all x1, starting transfers between devices, plane_body(): lax.all_to_all(packed.reshape(groups, SLOTS, -1), 'rows', split_axis=0, c...  7.3 us
    ppermute x14, waiting for transfers between devices, swap(): return lax.ppermute(value, 'rows', [(i, i ^ bit) for i in range(groups)])  5.52 us
    pallas_call x2, Pallas kernels, invert(): pl.pallas_call(functools.partial(invert_kernel, panel_range, len(sources)...  3.57 us
    pallas_call x1, Pallas kernels, plane_body(): pl.pallas_call(functools.partial(pick_kernel, groups, width), out_shape=(...  2.34 us
    pallas_call x1, Pallas kernels, update(): pl.pallas_call(functools.partial(update_kernel, width, flips), out_shape=...  1.78 us
  transfers between devices with their start and end apart: 15, of which 7 were waited for; matrix products, arithmetic and copies ran while one was open for 0% of the time, Pallas kernels for 13%

profile of v5, /device:TPU:0, one launch (start us, length us, event | category | flops | bytes accessed | tf_op | source)
XLA Modules:
  0.0 34.1 jit_solution(17042652306775823187)
XLA Ops:
  0.0 2.3 %pick.1 = (bf16[512,384]{1,0:T(8,128)(2,1)}, bf16[16,128]{1,0:T(8,128)(2,1)}) custom-call(s32[1,128]{1,0:T(1,128)} %bitcast.5, bf16[128,4096]{1,0:T(8,128)(2,1)} %slab_ref.1, bf16[128,128]{1,0:T(8,128)(2,1)} %cross_ref.1), custom_call_target="tpu_custom_call" | custom-call | tf_op jit(solution)/shard_map/pick/pallas_call | solution.py:329
  2.4 7.3 %all-to-all-start = ((bf16[32,16,384]{2,1,0:T(8,128)(2,1)}), bf16[32,16,384]{2,1,0:T(8,128)(2,1)S(1)}, u32[]{:S(2)}, u32[]{:S(2)}) async-start(bf16[32,16,384]{2,1,0:T(8,128)(2,1)} %bitcast.8), calls=%async_computation | async-start | bytes 786432 | tf_op jit(solution)/shard_map/all_to_all | solution.py:368
  9.7 0.3 collective-permute-start.3
  10.0 0.9 %collective-permute-done.3 = bf16[16,128]{1,0:T(8,128)(2,1)S(1)} collective-permute-done((bf16[16,128]{1,0:T(8,128)(2,1)S(1)}, bf16[16,128]{1,0:T(8,128)(2,1)S(1)}, u32[]{:S(2)}, u32[]{:S(2)}) %collective-permute-start.3) | collective-permute-done | bytes 4128 | tf_op jit(solution)/shard_map/ppermute | solution.py:366
  10.9 1.8 %collective-permute-start.4 = (bf16[32,128]{1,0:T(8,128)(2,1)S(1)}, bf16[32,128]{1,0:T(8,128)(2,1)S(1)}, u32[]{:S(2)}, u32[]{:S(2)}) collective-permute-start(bf16[32,128]{1,0:T(8,128)(2,1)S(1)} %get-tuple-element.29), channel_id=1, source_target_pairs={{0,2},{1,3},{2,0},{3,1},{4,6},{5,7},{6,4},{7,5},{8,10},{9,11},{10,... | collective-permute-start | bytes 24584 | tf_op jit(solution)/shard_map/ppermute | solution.py:366
  12.7 1.5 %collective-permute-start.6 = (bf16[32,128]{1,0:T(8,128)(2,1)S(1)}, bf16[32,128]{1,0:T(8,128)(2,1)S(1)}, u32[]{:S(2)}, u32[]{:S(2)}) collective-permute-start(bf16[32,128]{1,0:T(8,128)(2,1)S(1)} %get-tuple-element.29), channel_id=1, source_target_pairs={{0,6},{1,7},{2,4},{3,5},{4,2},{5,3},{6,0},{7,1},{8,14},{9,15},{10,... | collective-permute-start | bytes 24584 | tf_op jit(solution)/shard_map/ppermute | solution.py:366
  14.1 0.3 collective-permute-start.5
  14.4 0.2 collective-permute-done.4
  14.6 3.2 %collective-permute-done.5 = bf16[32,128]{1,0:T(8,128)(2,1)S(1)} collective-permute-done((bf16[32,128]{1,0:T(8,128)(2,1)S(1)}, bf16[32,128]{1,0:T(8,128)(2,1)S(1)}, u32[]{:S(2)}, u32[]{:S(2)}) %collective-permute-start.5) | collective-permute-done | bytes 8224 | tf_op jit(solution)/shard_map/ppermute | solution.py:366
  17.8 0.0 copy-start.3
  17.8 3.5 %collective-permute-start.9 = (bf16[128,128]{1,0:T(8,128)(2,1)S(1)}, bf16[128,128]{1,0:T(8,128)(2,1)S(1)}, u32[]{:S(2)}, u32[]{:S(2)}) collective-permute-start(bf16[128,128]{1,0:T(8,128)(2,1)S(1)} %constant_dynamic-update-slice_fusion.2.refs_2_), channel_id=1, source_target_pairs={{0,24},{1,25},{2,26},{3,27},{4,28},{5,29},{6,30},{7,31},{8,16},{9,... | collective-permute-start | bytes 98312 | tf_op jit(solution)/shard_map/ppermute | solution.py:366
  21.3 0.0 collective-permute-start.8
  21.3 1.0 %collective-permute-start.7 = (bf16[128,128]{1,0:T(8,128)(2,1)S(1)}, bf16[128,128]{1,0:T(8,128)(2,1)S(1)}, u32[]{:S(2)}, u32[]{:S(2)}) collective-permute-start(bf16[128,128]{1,0:T(8,128)(2,1)S(1)} %constant_dynamic-update-slice_fusion.2.refs_2_), channel_id=1, source_target_pairs={{0,8},{1,9},{2,10},{3,11},{4,12},{5,13},{6,14},{7,15},{8,0},{9,1},... | collective-permute-start | bytes 98312 | tf_op jit(solution)/shard_map/ppermute | solution.py:366
  22.3 0.6 %order.1 = (bf16[512,512]{1,0:T(8,128)(2,1)S(1)}, bf16[128,512]{1,0:T(8,128)(2,1)S(1)}, f32[128,128]{1,0:T(8,128)S(1)}) custom-call(s32[1,128]{1,0:T(1,128)S(1)} %bitcast.6, f32[1,128]{1,0:T(1,128)S(1)} %bitcast.7), custom_call_target="tpu_custom_call" | custom-call | flops 2097152000 | bytes 65536 | tf_op jit(solution)/shard_map/order/pallas_call | solution.py:349
  22.9 0.7 %all-to-all-done = bf16[32,16,384]{2,1,0:T(8,128)(2,1)S(1)} async-done(((bf16[32,16,384]{2,1,0:T(8,128)(2,1)}), bf16[32,16,384]{2,1,0:T(8,128)(2,1)S(1)}, u32[]{:S(2)}, u32[]{:S(2)}) %all-to-all-start) | async-done | bytes 393248 | tf_op jit(solution)/shard_map/all_to_all | solution.py:368
  23.5 0.3 compact.1.refs_0_
  23.9 1.2 %collective-permute-start.2 = (bf16[128,512]{1,0:T(8,128)(2,1)S(1)}, bf16[128,512]{1,0:T(8,128)(2,1)S(1)}, u32[]{:S(2)}, u32[]{:S(2)}) collective-permute-start(bf16[128,512]{1,0:T(8,128)(2,1)S(1)} %compact.1.refs_0_), channel_id=1, source_target_pairs={{0,8},{1,9},{2,10},{3,11},{4,12},{5,13},{6,14},{7,15},{8,0},{9,1},... | collective-permute-start | bytes 393224 | tf_op jit(solution)/shard_map/ppermute | solution.py:366
  25.0 0.4 %collective-permute-start.1 = (bf16[128,512]{1,0:T(8,128)(2,1)S(1)}, bf16[128,512]{1,0:T(8,128)(2,1)S(1)}, u32[]{:S(2)}, u32[]{:S(2)}) collective-permute-start(bf16[128,512]{1,0:T(8,128)(2,1)S(1)} %compact.1.refs_0_), channel_id=1, source_target_pairs={{0,4},{1,5},{2,6},{3,7},{4,0},{5,1},{6,2},{7,3},{8,12},{9,13},{10,... | collective-permute-start | bytes 393224 | tf_op jit(solution)/shard_map/ppermute | solution.py:366
  25.5 0.0 collective-permute-done.9.refs_5_
  25.5 1.3 %collective-permute-start = (bf16[128,512]{1,0:T(8,128)(2,1)S(1)}, bf16[128,512]{1,0:T(8,128)(2,1)S(1)}, u32[]{:S(2)}, u32[]{:S(2)}) collective-permute-start(bf16[128,512]{1,0:T(8,128)(2,1)S(1)} %compact.1.refs_0_), channel_id=1, source_target_pairs={{0,2},{1,3},{2,0},{3,1},{4,6},{5,7},{6,4},{7,5},{8,10},{9,11},{10,... | collective-permute-start | bytes 393224 | tf_op jit(solution)/shard_map/ppermute | solution.py:366
  26.8 2.6 %invert.2 = (f32[128,128]{1,0:T(8,128)S(1)}, f32[128,128]{1,0:T(8,128)S(1)}) custom-call(bf16[128,512]{1,0:T(8,128)(2,1)S(1)} %get-tuple-element.19.refs_0_, f32[128,128]{1,0:T(8,128)S(1)} %get-tuple-element.20.refs_1_, bf16[128,128]{1,0:T(8,128)(2,1)S(1)} %constant_dynamic-update-slice_fusion.2.refs_2_, ...), custom_call_target="tpu_custom_call" | custom-call | flops 5033164800 | bytes 65536 | tf_op jit(solution)/shard_map/invert/pallas_call | solution.py:387
  29.5 0.1 collective-permute-start.10
  29.5 0.0 collective-permute-done.2.refs_6_
  29.6 0.7 %collective-permute-done.1.refs_4_ = bf16[128,512]{1,0:T(8,128)(2,1)S(1)} collective-permute-done((bf16[128,512]{1,0:T(8,128)(2,1)S(1)}, bf16[128,512]{1,0:T(8,128)(2,1)S(1)}, u32[]{:S(2)}, u32[]{:S(2)}) %collective-permute-start.1) | collective-permute-done | bytes 131104 | tf_op jit(solution)/shard_map/ppermute | solution.py:366
  30.2 0.2 collective-permute-done.refs_2_
  30.5 0.0 collective-permute-start.11
  30.5 0.5 %collective-permute-start.12 = (bf16[128,512]{1,0:T(8,128)(2,1)S(1)}, bf16[128,512]{1,0:T(8,128)(2,1)S(1)}, u32[]{:S(2)}, u32[]{:S(2)}) collective-permute-start(bf16[128,512]{1,0:T(8,128)(2,1)S(1)} %collective-permute-done.1.refs_4_), channel_id=1, source_target_pairs={{0,1},{1,0},{2,3},{3,2},{4,5},{5,4},{6,7},{7,6},{8,9},{9,8},{10,11... | collective-permute-start | bytes 393224 | tf_op jit(solution)/shard_map/ppermute | solution.py:366
  31.0 0.1 collective-permute-start.13
  31.0 0.9 %invert.3.inverse_ref = bf16[384,128]{1,0:T(8,128)(2,1)S(1)} custom-call(f32[128,128]{1,0:T(8,128)S(1)} %get-tuple-element.24.refs_0_, f32[128,128]{1,0:T(8,128)S(1)} %get-tuple-element.25.refs_1_), custom_call_target="tpu_custom_call" | custom-call | flops 1677721600 | bytes 65536 | tf_op jit(solution)/shard_map/invert/pallas_call | solution.py:387
  32.0 0.0 collective-permute-done.11.refs_3_
  32.0 0.3 collective-permute-done.13.refs_7_
  32.3 1.8 %update.1 = bf16[128,4096]{1,0:T(8,128)(2,1)} custom-call(bf16[384,128]{1,0:T(8,128)(2,1)S(1)} %invert.3.inverse_ref, bf16[128,128]{1,0:T(8,128)(2,1)S(1)} %copy-done.1, bf16[128,4096]{1,0:T(8,128)(2,1)S(1)} %copy-done, bf16[128,512]{1,0:T(8,128)(2,1)S(1)} %compact.1.refs_0_, bf16[128,512]{1,0:T(8,128)(2,1)S(1)} %collective-permute-done.10.refs_1_, ...), custom_call_target="tpu_custom_call" | custom-call | tf_op jit(solution)/shard_map/update/pallas_call | solution.py:405
  (19 shorter events, 0.1 us)
Async XLA Ops:
  2.3 7.3 %copy-start.4 = (bf16[16,128]{1,0:T(8,128)(2,1)S(1)}, bf16[16,128]{1,0:T(8,128)(2,1)}, u32[]{:S(2)}) copy-start(bf16[16,128]{1,0:T(8,128)(2,1)} %get-tuple-element.21) | copy-start | bytes 12292
  2.4 21.2 %all-to-all-start = ((bf16[32,16,384]{2,1,0:T(8,128)(2,1)}), bf16[32,16,384]{2,1,0:T(8,128)(2,1)S(1)}, u32[]{:S(2)}, u32[]{:S(2)}) async-start(bf16[32,16,384]{2,1,0:T(8,128)(2,1)} %bitcast.8), calls=%async_computation | async-start | bytes 786432 | tf_op jit(solution)/shard_map/all_to_all | solution.py:368
  9.7 1.2 %collective-permute-start.3 = (bf16[16,128]{1,0:T(8,128)(2,1)S(1)}, bf16[16,128]{1,0:T(8,128)(2,1)S(1)}, u32[]{:S(2)}, u32[]{:S(2)}) collective-permute-start(bf16[16,128]{1,0:T(8,128)(2,1)S(1)} %copy-done.4), channel_id=1, source_target_pairs={{0,1},{1,0},{2,3},{3,2},{4,5},{5,4},{6,7},{7,6},{8,9},{9,8},{10,11... | collective-permute-start | bytes 12296 | tf_op jit(solution)/shard_map/ppermute | solution.py:366
  10.9 3.7 %collective-permute-start.4 = (bf16[32,128]{1,0:T(8,128)(2,1)S(1)}, bf16[32,128]{1,0:T(8,128)(2,1)S(1)}, u32[]{:S(2)}, u32[]{:S(2)}) collective-permute-start(bf16[32,128]{1,0:T(8,128)(2,1)S(1)} %get-tuple-element.29), channel_id=1, source_target_pairs={{0,2},{1,3},{2,0},{3,1},{4,6},{5,7},{6,4},{7,5},{8,10},{9,11},{10,... | collective-permute-start | bytes 24584 | tf_op jit(solution)/shard_map/ppermute | solution.py:366
  12.7 5.1 %collective-permute-start.6 = (bf16[32,128]{1,0:T(8,128)(2,1)S(1)}, bf16[32,128]{1,0:T(8,128)(2,1)S(1)}, u32[]{:S(2)}, u32[]{:S(2)}) collective-permute-start(bf16[32,128]{1,0:T(8,128)(2,1)S(1)} %get-tuple-element.29), channel_id=1, source_target_pairs={{0,6},{1,7},{2,4},{3,5},{4,2},{5,3},{6,0},{7,1},{8,14},{9,15},{10,... | collective-permute-start | bytes 24584 | tf_op jit(solution)/shard_map/ppermute | solution.py:366
  14.1 3.7 %collective-permute-start.5 = (bf16[32,128]{1,0:T(8,128)(2,1)S(1)}, bf16[32,128]{1,0:T(8,128)(2,1)S(1)}, u32[]{:S(2)}, u32[]{:S(2)}) collective-permute-start(bf16[32,128]{1,0:T(8,128)(2,1)S(1)} %get-tuple-element.29), channel_id=1, source_target_pairs={{0,4},{1,5},{2,6},{3,7},{4,0},{5,1},{6,2},{7,3},{8,12},{9,13},{10,... | collective-permute-start | bytes 24584 | tf_op jit(solution)/shard_map/ppermute | solution.py:366
  17.8 4.5 %copy-start.2 = (s32[128]{0:T(128)S(1)}, s32[128]{0:T(128)}, u32[]{:S(2)}) copy-start(s32[128]{0:T(128)} %param.6) | copy-start | bytes 1540
  17.8 4.5 %copy-start.3 = (f32[128]{0:T(128)S(1)}, f32[128]{0:T(128)}, u32[]{:S(2)}) copy-start(f32[128]{0:T(128)} %param.7) | copy-start | bytes 1540
  17.8 7.6 %collective-permute-start.9 = (bf16[128,128]{1,0:T(8,128)(2,1)S(1)}, bf16[128,128]{1,0:T(8,128)(2,1)S(1)}, u32[]{:S(2)}, u32[]{:S(2)}) collective-permute-start(bf16[128,128]{1,0:T(8,128)(2,1)S(1)} %constant_dynamic-update-slice_fusion.2.refs_2_), channel_id=1, source_target_pairs={{0,24},{1,25},{2,26},{3,27},{4,28},{5,29},{6,30},{7,31},{8,16},{9,... | collective-permute-start | bytes 98312 | tf_op jit(solution)/shard_map/ppermute | solution.py:366
  21.3 5.5 %collective-permute-start.8 = (bf16[128,128]{1,0:T(8,128)(2,1)S(1)}, bf16[128,128]{1,0:T(8,128)(2,1)S(1)}, u32[]{:S(2)}, u32[]{:S(2)}) collective-permute-start(bf16[128,128]{1,0:T(8,128)(2,1)S(1)} %constant_dynamic-update-slice_fusion.2.refs_2_), channel_id=1, source_target_pairs={{0,16},{1,17},{2,18},{3,19},{4,20},{5,21},{6,22},{7,23},{8,24},{9,... | collective-permute-start | bytes 98312 | tf_op jit(solution)/shard_map/ppermute | solution.py:366
  21.3 5.5 %collective-permute-start.7 = (bf16[128,128]{1,0:T(8,128)(2,1)S(1)}, bf16[128,128]{1,0:T(8,128)(2,1)S(1)}, u32[]{:S(2)}, u32[]{:S(2)}) collective-permute-start(bf16[128,128]{1,0:T(8,128)(2,1)S(1)} %constant_dynamic-update-slice_fusion.2.refs_2_), channel_id=1, source_target_pairs={{0,8},{1,9},{2,10},{3,11},{4,12},{5,13},{6,14},{7,15},{8,0},{9,1},... | collective-permute-start | bytes 98312 | tf_op jit(solution)/shard_map/ppermute | solution.py:366
  23.9 5.7 %collective-permute-start.2 = (bf16[128,512]{1,0:T(8,128)(2,1)S(1)}, bf16[128,512]{1,0:T(8,128)(2,1)S(1)}, u32[]{:S(2)}, u32[]{:S(2)}) collective-permute-start(bf16[128,512]{1,0:T(8,128)(2,1)S(1)} %compact.1.refs_0_), channel_id=1, source_target_pairs={{0,8},{1,9},{2,10},{3,11},{4,12},{5,13},{6,14},{7,15},{8,0},{9,1},... | collective-permute-start | bytes 393224 | tf_op jit(solution)/shard_map/ppermute | solution.py:366
  25.0 5.2 %collective-permute-start.1 = (bf16[128,512]{1,0:T(8,128)(2,1)S(1)}, bf16[128,512]{1,0:T(8,128)(2,1)S(1)}, u32[]{:S(2)}, u32[]{:S(2)}) collective-permute-start(bf16[128,512]{1,0:T(8,128)(2,1)S(1)} %compact.1.refs_0_), channel_id=1, source_target_pairs={{0,4},{1,5},{2,6},{3,7},{4,0},{5,1},{6,2},{7,3},{8,12},{9,13},{10,... | collective-permute-start | bytes 393224 | tf_op jit(solution)/shard_map/ppermute | solution.py:366
  25.5 5.0 %collective-permute-start = (bf16[128,512]{1,0:T(8,128)(2,1)S(1)}, bf16[128,512]{1,0:T(8,128)(2,1)S(1)}, u32[]{:S(2)}, u32[]{:S(2)}) collective-permute-start(bf16[128,512]{1,0:T(8,128)(2,1)S(1)} %compact.1.refs_0_), channel_id=1, source_target_pairs={{0,2},{1,3},{2,0},{3,1},{4,6},{5,7},{6,4},{7,5},{8,10},{9,11},{10,... | collective-permute-start | bytes 393224 | tf_op jit(solution)/shard_map/ppermute | solution.py:366
  29.5 2.5 %collective-permute-start.10 = (bf16[128,512]{1,0:T(8,128)(2,1)S(1)}, bf16[128,512]{1,0:T(8,128)(2,1)S(1)}, u32[]{:S(2)}, u32[]{:S(2)}) collective-permute-start(bf16[128,512]{1,0:T(8,128)(2,1)S(1)} %compact.1.refs_0_), channel_id=1, source_target_pairs={{0,1},{1,0},{2,3},{3,2},{4,5},{5,4},{6,7},{7,6},{8,9},{9,8},{10,11... | collective-permute-start | bytes 393224 | tf_op jit(solution)/shard_map/ppermute | solution.py:366
  30.5 1.9 %copy-start = (bf16[128,4096]{1,0:T(8,128)(2,1)S(1)}, bf16[128,4096]{1,0:T(8,128)(2,1)}, u32[]{:S(2)}) copy-start(bf16[128,4096]{1,0:T(8,128)(2,1)} %slab_ref.1) | copy-start | bytes 3145732
  30.5 1.9 %copy-start.1 = (bf16[128,128]{1,0:T(8,128)(2,1)S(1)}, bf16[128,128]{1,0:T(8,128)(2,1)}, u32[]{:S(2)}) copy-start(bf16[128,128]{1,0:T(8,128)(2,1)} %cross_ref.1) | copy-start | bytes 98308
  30.5 1.5 %collective-permute-start.11 = (bf16[128,512]{1,0:T(8,128)(2,1)S(1)}, bf16[128,512]{1,0:T(8,128)(2,1)S(1)}, u32[]{:S(2)}, u32[]{:S(2)}) collective-permute-start(bf16[128,512]{1,0:T(8,128)(2,1)S(1)} %collective-permute-done.refs_2_), channel_id=1, source_target_pairs={{0,1},{1,0},{2,3},{3,2},{4,5},{5,4},{6,7},{7,6},{8,9},{9,8},{10,11... | collective-permute-start | bytes 393224 | tf_op jit(solution)/shard_map/ppermute | solution.py:366
  30.5 1.5 %collective-permute-start.12 = (bf16[128,512]{1,0:T(8,128)(2,1)S(1)}, bf16[128,512]{1,0:T(8,128)(2,1)S(1)}, u32[]{:S(2)}, u32[]{:S(2)}) collective-permute-start(bf16[128,512]{1,0:T(8,128)(2,1)S(1)} %collective-permute-done.1.refs_4_), channel_id=1, source_target_pairs={{0,1},{1,0},{2,3},{3,2},{4,5},{5,4},{6,7},{7,6},{8,9},{9,8},{10,11... | collective-permute-start | bytes 393224 | tf_op jit(solution)/shard_map/ppermute | solution.py:366
  31.0 1.3 %collective-permute-start.13 = (bf16[128,512]{1,0:T(8,128)(2,1)S(1)}, bf16[128,512]{1,0:T(8,128)(2,1)S(1)}, u32[]{:S(2)}, u32[]{:S(2)}) collective-permute-start(bf16[128,512]{1,0:T(8,128)(2,1)S(1)} %collective-permute-done.2.refs_6_), channel_id=1, source_target_pairs={{0,1},{1,0},{2,3},{3,2},{4,5},{5,4},{6,7},{7,6},{8,9},{9,8},{10,11... | collective-permute-start | bytes 393224 | tf_op jit(solution)/shard_map/ppermute | solution.py:366

commit v6 on v5

--- a/solution.py
+++ b/solution.py
@@ -223,6 +223,10 @@
         e[k, k], e[k + 1, k], e[k + 1, k + 1] = -pa, -pb, -pc
 
 
+def gain_of(inverse_parts, observed):
+    return dot32(inverse_parts, jnp.concatenate([observed] * PARTS, axis=0)).astype(jnp.bfloat16)
+
+
 def invert_kernel(panel_range, sources, *refs):
     inputs, outputs, (spread_ref,) = refs[:sources], refs[sources:-1], refs[-1:]
     step = 8
@@ -234,8 +238,8 @@
         state_ref[...] = inn
         given = state_ref
     else:
-        given, solved_before = inputs
-        out_ref, state_ref, solved_ref = outputs
+        given, solved_before = inputs[:2]
+        out_ref, gain_ref, state_ref, solved_ref = outputs
         size = given.shape[0]
         done = first * step
         state_ref[:done, :] = given[:done, :]
@@ -288,26 +292,30 @@
         precision=lax.Precision.HIGHEST,
         preferred_element_type=jnp.float32,
     )
+    parts = []
     for part in range(PARTS):
         piece = x.astype(jnp.bfloat16)
         out_ref[part * size : (part + 1) * size, :] = piece
         x = x - piece.astype(jnp.float32)
-
-
-def update_kernel(width, flips, inverse_ref, cross_ref, slab_ref, *refs):
-    pieces, (out_ref, held, sem) = refs[: len(flips)], refs[-3:]
+        parts.append(piece)
+    for index, piece in enumerate(inputs[2:]):
+        gain_ref[index] = gain_of(jnp.concatenate(parts, axis=1), piece[...])
+
+
+def update_kernel(width, flips, inverse_ref, gain_ref, cross_ref, slab_ref, *refs):
+    pieces, (out_ref, held, sem) = refs[:-3], refs[-3:]
     place = column_group(lax.axis_index("rows"))
     cross = cross_ref[...]
     size = cross.shape[1]
     inverse = jnp.concatenate(
         [inverse_ref[t * size : (t + 1) * size] for t in range(PARTS)], axis=1
     )
-    copies, gains = [], []
-    for piece in pieces:
-        gains.append(
-            dot32(inverse, jnp.concatenate([piece[...]] * PARTS, axis=0)).astype(jnp.bfloat16)
-        )
+    copies = []
+    ready = gain_ref.shape[0]
+    gains = [gain_ref[i] for i in range(ready)]
     for index, flip in enumerate(flips):
+        if index == ready:
+            gains += [gain_of(inverse, piece[...]) for piece in pieces]
         at = pl.multiple_of((place ^ flip) * width, width)
         new = slab_ref[:, pl.ds(at, width)].astype(jnp.float32) - dot32(cross, gains[index])
         held[index] = new.astype(jnp.bfloat16)
@@ -384,11 +392,12 @@
     def invert(panel_range, sources):
         first = panel_range[0] == 0
         parts = jax.ShapeDtypeStruct((PARTS * count, count), jnp.bfloat16)
+        gains = jax.ShapeDtypeStruct((len(sources) - 2, count, width), jnp.bfloat16)
         return pl.pallas_call(
             functools.partial(invert_kernel, panel_range, len(sources)),
-            out_shape=(square, square) if first else parts,
+            out_shape=(square, square) if first else (parts, gains),
             in_specs=[VMEM] * len(sources),
-            out_specs=(VMEM, VMEM) if first else VMEM,
+            out_specs=(VMEM, VMEM),
             scratch_shapes=([] if first else [pltpu.VMEM((count, count), jnp.float32)] * 2)
             + [pltpu.VMEM((18, 8, count), jnp.float32)],
             cost_estimate=pl.CostEstimate(
@@ -396,37 +405,32 @@
                 bytes_accessed=4 * count * count,
                 transcendentals=count,
             ),
-            compiler_params=room(4),
+            compiler_params=room(6),
             name="invert",
         )(*sources)
 
-    def update(inverse, flips, pieces, before):
-        more = () if before is None else (before,)
-        return pl.pallas_call(
-            functools.partial(update_kernel, width, flips),
-            out_shape=jax.ShapeDtypeStruct(slab.shape, jnp.bfloat16),
-            in_specs=[VMEM] * (3 + len(pieces)) + [HBM] * len(more),
-            out_specs=HBM,
-            scratch_shapes=[
-                pltpu.VMEM((len(flips), rows, width), jnp.bfloat16),
-                pltpu.SemaphoreType.DMA((len(flips),)),
-            ],
-            input_output_aliases={3 + len(pieces): 0} if more else {},
-            compiler_params=room(12),
-            name="update",
-        )(inverse, cross, slab, *pieces, *more)
-
     by = {0: observed, 1: swap(observed, 1)}
     by.update({group: swap(observed, bit) for bit, group in ((2, 2), (4, 4), (8, 6))})
-    panels, early = count // 8, 12 * count // 128
+    panels, early = count // 8, 13 * count // 128
     midway = invert(range(early), (cross_order, diagonal, *levels))
     arrived, midway = lax.optimization_barrier(([by[g] for g in (2, 4, 6)], midway))
     for group, piece in zip((2, 4, 6), arrived):
         by[group] = piece
         by[group + 1] = swap(piece, 1)
-    inverse = invert(range(early, panels), tuple(midway))
-    flips = tuple(range(PLANE))
-    return update(inverse, flips, [by[f] for f in flips], None)
+    inverse, gains = invert(range(early, panels), (*midway, *(by[g] for g in (0, 2, 4, 6))))
+    flips = (0, 2, 4, 6, 1, 3, 5, 7)
+    return pl.pallas_call(
+        functools.partial(update_kernel, width, flips),
+        out_shape=jax.ShapeDtypeStruct(slab.shape, jnp.bfloat16),
+        in_specs=[VMEM] * 8,
+        out_specs=HBM,
+        scratch_shapes=[
+            pltpu.VMEM((len(flips), rows, width), jnp.bfloat16),
+            pltpu.SemaphoreType.DMA((len(flips),)),
+        ],
+        compiler_params=room(12),
+        name="update",
+    )(inverse, gains, cross, slab, *(by[g] for g in (1, 3, 5, 7)))
 
 
 def solution(mesh):

time: 34.4 us -> 34 us (0.988)
  waiting for transfers between devices: 6.18 us -> 5.72 us
    ppermute x14, waiting for transfers between devices: 5.52 us -> 5.07 us  [swap(): return lax.ppermute(value, 'rows', [(i, i ^ bit) for i in range(groups)])]
    pallas_call x2, Pallas kernels: 3.57 us -> 4.02 us  [invert(): pl.pallas_call(functools.partial(invert_kernel, panel_range, len(sources)...]
  transfers between devices with their start and end apart: 15 -> 15, of which waited for: 7 -> 6; matrix products, arithmetic and copies ran while one was open for 0% -> 0% of each run, Pallas kernels for 13% -> 15%
where the time goes in v6:
time: 34 us; the launch traced here: 33.8 us
  starting transfers between devices  19.1 us (56%)
  Pallas kernels  8.73 us (26%)
  waiting for transfers between devices  5.72 us (17%)
    ppermute x14, starting transfers between devices, swap(): return lax.ppermute(value, 'rows', [(i, i ^ bit) for i in range(groups)])  11.8 us
    all_to_all x1, starting transfers between devices, plane_body(): lax.all_to_all(packed.reshape(groups, SLOTS, -1), 'rows', split_axis=0, c...  7.3 us
    ppermute x14, waiting for transfers between devices, swap(): return lax.ppermute(value, 'rows', [(i, i ^ bit) for i in range(groups)])  5.07 us
    pallas_call x2, Pallas kernels, invert(): pl.pallas_call(functools.partial(invert_kernel, panel_range, len(sources)...  4.02 us
    pallas_call x1, Pallas kernels, plane_body(): pl.pallas_call(functools.partial(pick_kernel, groups, width), out_shape=(...  2.34 us
    pallas_call x1, Pallas kernels, plane_body(): pl.pallas_call(functools.partial(update_kernel, width, flips), out_shape=...  1.45 us
  transfers between devices with their start and end apart: 15, of which 6 were waited for; matrix products, arithmetic and copies ran while one was open for 0% of the time, Pallas kernels for 15%

profile of v6, /device:TPU:0, one launch (start us, length us, event | category | flops | bytes accessed | tf_op | source)
XLA Modules:
  0.0 33.8 jit_solution(7617223676587391076)
XLA Ops:
  0.0 2.3 %pick.1 = (bf16[512,384]{1,0:T(8,128)(2,1)}, bf16[16,128]{1,0:T(8,128)(2,1)}) custom-call(s32[1,128]{1,0:T(1,128)} %bitcast.5, bf16[128,4096]{1,0:T(8,128)(2,1)} %slab_ref.1, bf16[128,128]{1,0:T(8,128)(2,1)} %cross_ref.1), custom_call_target="tpu_custom_call" | custom-call | tf_op jit(solution)/shard_map/pick/pallas_call | solution.py:337
  2.4 7.3 %all-to-all-start = ((bf16[32,16,384]{2,1,0:T(8,128)(2,1)}), bf16[32,16,384]{2,1,0:T(8,128)(2,1)S(1)}, u32[]{:S(2)}, u32[]{:S(2)}) async-start(bf16[32,16,384]{2,1,0:T(8,128)(2,1)} %bitcast.8), calls=%async_computation | async-start | bytes 786432 | tf_op jit(solution)/shard_map/all_to_all | solution.py:376
  9.7 0.3 collective-permute-start.3
  10.0 0.9 %collective-permute-done.3 = bf16[16,128]{1,0:T(8,128)(2,1)S(1)} collective-permute-done((bf16[16,128]{1,0:T(8,128)(2,1)S(1)}, bf16[16,128]{1,0:T(8,128)(2,1)S(1)}, u32[]{:S(2)}, u32[]{:S(2)}) %collective-permute-start.3) | collective-permute-done | bytes 4128 | tf_op jit(solution)/shard_map/ppermute | solution.py:374
  10.9 1.8 %collective-permute-start.4 = (bf16[32,128]{1,0:T(8,128)(2,1)S(1)}, bf16[32,128]{1,0:T(8,128)(2,1)S(1)}, u32[]{:S(2)}, u32[]{:S(2)}) collective-permute-start(bf16[32,128]{1,0:T(8,128)(2,1)S(1)} %get-tuple-element.33), channel_id=1, source_target_pairs={{0,2},{1,3},{2,0},{3,1},{4,6},{5,7},{6,4},{7,5},{8,10},{9,11},{10,... | collective-permute-start | bytes 24584 | tf_op jit(solution)/shard_map/ppermute | solution.py:374
  12.7 1.5 %collective-permute-start.6 = (bf16[32,128]{1,0:T(8,128)(2,1)S(1)}, bf16[32,128]{1,0:T(8,128)(2,1)S(1)}, u32[]{:S(2)}, u32[]{:S(2)}) collective-permute-start(bf16[32,128]{1,0:T(8,128)(2,1)S(1)} %get-tuple-element.33), channel_id=1, source_target_pairs={{0,6},{1,7},{2,4},{3,5},{4,2},{5,3},{6,0},{7,1},{8,14},{9,15},{10,... | collective-permute-start | bytes 24584 | tf_op jit(solution)/shard_map/ppermute | solution.py:374
  14.1 0.3 collective-permute-start.5
  14.4 0.2 collective-permute-done.4
  14.6 3.2 %collective-permute-done.5 = bf16[32,128]{1,0:T(8,128)(2,1)S(1)} collective-permute-done((bf16[32,128]{1,0:T(8,128)(2,1)S(1)}, bf16[32,128]{1,0:T(8,128)(2,1)S(1)}, u32[]{:S(2)}, u32[]{:S(2)}) %collective-permute-start.5) | collective-permute-done | bytes 8224 | tf_op jit(solution)/shard_map/ppermute | solution.py:374
  17.8 0.0 collective-permute-done.6
  17.8 0.0 copy-start.3
  17.8 3.5 %collective-permute-start.9 = (bf16[128,128]{1,0:T(8,128)(2,1)S(1)}, bf16[128,128]{1,0:T(8,128)(2,1)S(1)}, u32[]{:S(2)}, u32[]{:S(2)}) collective-permute-start(bf16[128,128]{1,0:T(8,128)(2,1)S(1)} %constant_dynamic-update-slice_fusion.2.refs_2_), channel_id=1, source_target_pairs={{0,24},{1,25},{2,26},{3,27},{4,28},{5,29},{6,30},{7,31},{8,16},{9,... | collective-permute-start | bytes 98312 | tf_op jit(solution)/shard_map/ppermute | solution.py:374
  21.3 0.0 collective-permute-start.8
  21.3 1.0 %collective-permute-start.7 = (bf16[128,128]{1,0:T(8,128)(2,1)S(1)}, bf16[128,128]{1,0:T(8,128)(2,1)S(1)}, u32[]{:S(2)}, u32[]{:S(2)}) collective-permute-start(bf16[128,128]{1,0:T(8,128)(2,1)S(1)} %constant_dynamic-update-slice_fusion.2.refs_2_), channel_id=1, source_target_pairs={{0,8},{1,9},{2,10},{3,11},{4,12},{5,13},{6,14},{7,15},{8,0},{9,1},... | collective-permute-start | bytes 98312 | tf_op jit(solution)/shard_map/ppermute | solution.py:374
  22.3 0.6 %order.1 = (bf16[512,512]{1,0:T(8,128)(2,1)S(1)}, bf16[128,512]{1,0:T(8,128)(2,1)S(1)}, f32[128,128]{1,0:T(8,128)S(1)}) custom-call(s32[1,128]{1,0:T(1,128)S(1)} %bitcast.6, f32[1,128]{1,0:T(1,128)S(1)} %bitcast.7), custom_call_target="tpu_custom_call" | custom-call | flops 2097152000 | bytes 65536 | tf_op jit(solution)/shard_map/order/pallas_call | solution.py:357
  22.9 0.7 %all-to-all-done = bf16[32,16,384]{2,1,0:T(8,128)(2,1)S(1)} async-done(((bf16[32,16,384]{2,1,0:T(8,128)(2,1)}), bf16[32,16,384]{2,1,0:T(8,128)(2,1)S(1)}, u32[]{:S(2)}, u32[]{:S(2)}) %all-to-all-start) | async-done | bytes 393248 | tf_op jit(solution)/shard_map/all_to_all | solution.py:376
  23.5 0.3 compact.1.refs_2_
  23.9 1.2 %collective-permute-start.2 = (bf16[128,512]{1,0:T(8,128)(2,1)S(1)}, bf16[128,512]{1,0:T(8,128)(2,1)S(1)}, u32[]{:S(2)}, u32[]{:S(2)}) collective-permute-start(bf16[128,512]{1,0:T(8,128)(2,1)S(1)} %compact.1.refs_2_), channel_id=1, source_target_pairs={{0,8},{1,9},{2,10},{3,11},{4,12},{5,13},{6,14},{7,15},{8,0},{9,1},... | collective-permute-start | bytes 393224 | tf_op jit(solution)/shard_map/ppermute | solution.py:374
  25.0 0.4 %collective-permute-start.1 = (bf16[128,512]{1,0:T(8,128)(2,1)S(1)}, bf16[128,512]{1,0:T(8,128)(2,1)S(1)}, u32[]{:S(2)}, u32[]{:S(2)}) collective-permute-start(bf16[128,512]{1,0:T(8,128)(2,1)S(1)} %compact.1.refs_2_), channel_id=1, source_target_pairs={{0,4},{1,5},{2,6},{3,7},{4,0},{5,1},{6,2},{7,3},{8,12},{9,13},{10,... | collective-permute-start | bytes 393224 | tf_op jit(solution)/shard_map/ppermute | solution.py:374
  25.5 1.3 %collective-permute-start = (bf16[128,512]{1,0:T(8,128)(2,1)S(1)}, bf16[128,512]{1,0:T(8,128)(2,1)S(1)}, u32[]{:S(2)}, u32[]{:S(2)}) collective-permute-start(bf16[128,512]{1,0:T(8,128)(2,1)S(1)} %compact.1.refs_2_), channel_id=1, source_target_pairs={{0,2},{1,3},{2,0},{3,1},{4,6},{5,7},{6,4},{7,5},{8,10},{9,11},{10,... | collective-permute-start | bytes 393224 | tf_op jit(solution)/shard_map/ppermute | solution.py:374
  26.8 0.0 collective-permute-done.8.refs_4_
  26.8 0.0 collective-permute-done.7.refs_3_
  26.8 2.8 %invert.2 = (f32[128,128]{1,0:T(8,128)S(1)}, f32[128,128]{1,0:T(8,128)S(1)}) custom-call(bf16[128,512]{1,0:T(8,128)(2,1)S(1)} %get-tuple-element.21.refs_0_, f32[128,128]{1,0:T(8,128)S(1)} %get-tuple-element.22.refs_1_, bf16[128,128]{1,0:T(8,128)(2,1)S(1)} %constant_dynamic-update-slice_fusion.2.refs_2_, ...), custom_call_target="tpu_custom_call" | custom-call | flops 5452595200 | bytes 65536 | tf_op jit(solution)/shard_map/invert/pallas_call | solution.py:396
  29.7 0.1 collective-permute-start.10
  29.7 0.5 %collective-permute-done.1.refs_4_ = bf16[128,512]{1,0:T(8,128)(2,1)S(1)} collective-permute-done((bf16[128,512]{1,0:T(8,128)(2,1)S(1)}, bf16[128,512]{1,0:T(8,128)(2,1)S(1)}, u32[]{:S(2)}, u32[]{:S(2)}) %collective-permute-start.1) | collective-permute-done | bytes 131104 | tf_op jit(solution)/shard_map/ppermute | solution.py:374
  30.2 0.2 collective-permute-done.refs_3_
  30.5 0.0 collective-permute-start.11
  30.5 0.5 %collective-permute-start.12 = (bf16[128,512]{1,0:T(8,128)(2,1)S(1)}, bf16[128,512]{1,0:T(8,128)(2,1)S(1)}, u32[]{:S(2)}, u32[]{:S(2)}) collective-permute-start(bf16[128,512]{1,0:T(8,128)(2,1)S(1)} %collective-permute-done.1.refs_4_), channel_id=1, source_target_pairs={{0,1},{1,0},{2,3},{3,2},{4,5},{5,4},{6,7},{7,6},{8,9},{9,8},{10,11... | collective-permute-start | bytes 393224 | tf_op jit(solution)/shard_map/ppermute | solution.py:374
  31.0 0.1 collective-permute-start.13
  31.0 1.2 %invert.3 = (bf16[384,128]{1,0:T(8,128)(2,1)S(1)}, bf16[4,128,512]{2,1,0:T(8,128)(2,1)S(1)}) custom-call(f32[128,128]{1,0:T(8,128)S(1)} %get-tuple-element.26.refs_0_, f32[128,128]{1,0:T(8,128)S(1)} %get-tuple-element.27.refs_1_, bf16[128,512]{1,0:T(8,128)(2,1)S(1)} %compact.1.refs_2_, bf16[128,512]{1,0:T(8,128)(2,1)S(1)} %collective-permute-done.refs_3_, ...), custom_call_target="tpu_custom_call" | custom-call | flops 1258291200 | bytes 65536 | tf_op jit(solution)/shard_map/invert/pallas_call | solution.py:396
  32.3 0.0 collective-permute-done.13.refs_3_
  32.3 1.5 %update.1 = bf16[128,4096]{1,0:T(8,128)(2,1)} custom-call(bf16[384,128]{1,0:T(8,128)(2,1)S(1)} %get-tuple-element.31.inverse_ref, bf16[4,128,512]{2,1,0:T(8,128)(2,1)S(1)} %get-tuple-element.32.gain_ref, bf16[128,128]{1,0:T(8,128)(2,1)S(1)} %copy-done.1, bf16[128,4096]{1,0:T(8,128)(2,1)S(1)} %copy-done, ...), custom_call_target="tpu_custom_call" | custom-call | tf_op jit(solution)/shard_map/update/pallas_call | solution.py:422
  (19 shorter events, 0.1 us)
Async XLA Ops:
  2.3 7.3 %copy-start.4 = (bf16[16,128]{1,0:T(8,128)(2,1)S(1)}, bf16[16,128]{1,0:T(8,128)(2,1)}, u32[]{:S(2)}) copy-start(bf16[16,128]{1,0:T(8,128)(2,1)} %get-tuple-element.23) | copy-start | bytes 12292
  2.4 21.2 %all-to-all-start = ((bf16[32,16,384]{2,1,0:T(8,128)(2,1)}), bf16[32,16,384]{2,1,0:T(8,128)(2,1)S(1)}, u32[]{:S(2)}, u32[]{:S(2)}) async-start(bf16[32,16,384]{2,1,0:T(8,128)(2,1)} %bitcast.8), calls=%async_computation | async-start | bytes 786432 | tf_op jit(solution)/shard_map/all_to_all | solution.py:376
  9.7 1.2 %collective-permute-start.3 = (bf16[16,128]{1,0:T(8,128)(2,1)S(1)}, bf16[16,128]{1,0:T(8,128)(2,1)S(1)}, u32[]{:S(2)}, u32[]{:S(2)}) collective-permute-start(bf16[16,128]{1,0:T(8,128)(2,1)S(1)} %copy-done.4), channel_id=1, source_target_pairs={{0,1},{1,0},{2,3},{3,2},{4,5},{5,4},{6,7},{7,6},{8,9},{9,8},{10,11... | collective-permute-start | bytes 12296 | tf_op jit(solution)/shard_map/ppermute | solution.py:374
  10.9 3.7 %collective-permute-start.4 = (bf16[32,128]{1,0:T(8,128)(2,1)S(1)}, bf16[32,128]{1,0:T(8,128)(2,1)S(1)}, u32[]{:S(2)}, u32[]{:S(2)}) collective-permute-start(bf16[32,128]{1,0:T(8,128)(2,1)S(1)} %get-tuple-element.33), channel_id=1, source_target_pairs={{0,2},{1,3},{2,0},{3,1},{4,6},{5,7},{6,4},{7,5},{8,10},{9,11},{10,... | collective-permute-start | bytes 24584 | tf_op jit(solution)/shard_map/ppermute | solution.py:374
  12.7 5.1 %collective-permute-start.6 = (bf16[32,128]{1,0:T(8,128)(2,1)S(1)}, bf16[32,128]{1,0:T(8,128)(2,1)S(1)}, u32[]{:S(2)}, u32[]{:S(2)}) collective-permute-start(bf16[32,128]{1,0:T(8,128)(2,1)S(1)} %get-tuple-element.33), channel_id=1, source_target_pairs={{0,6},{1,7},{2,4},{3,5},{4,2},{5,3},{6,0},{7,1},{8,14},{9,15},{10,... | collective-permute-start | bytes 24584 | tf_op jit(solution)/shard_map/ppermute | solution.py:374
  14.1 3.7 %collective-permute-start.5 = (bf16[32,128]{1,0:T(8,128)(2,1)S(1)}, bf16[32,128]{1,0:T(8,128)(2,1)S(1)}, u32[]{:S(2)}, u32[]{:S(2)}) collective-permute-start(bf16[32,128]{1,0:T(8,128)(2,1)S(1)} %get-tuple-element.33), channel_id=1, source_target_pairs={{0,4},{1,5},{2,6},{3,7},{4,0},{5,1},{6,2},{7,3},{8,12},{9,13},{10,... | collective-permute-start | bytes 24584 | tf_op jit(solution)/shard_map/ppermute | solution.py:374
  17.8 4.5 %copy-start.2 = (s32[128]{0:T(128)S(1)}, s32[128]{0:T(128)}, u32[]{:S(2)}) copy-start(s32[128]{0:T(128)} %param.6) | copy-start | bytes 1540
  17.8 4.5 %copy-start.3 = (f32[128]{0:T(128)S(1)}, f32[128]{0:T(128)}, u32[]{:S(2)}) copy-start(f32[128]{0:T(128)} %param.7) | copy-start | bytes 1540
  17.8 7.6 %collective-permute-start.9 = (bf16[128,128]{1,0:T(8,128)(2,1)S(1)}, bf16[128,128]{1,0:T(8,128)(2,1)S(1)}, u32[]{:S(2)}, u32[]{:S(2)}) collective-permute-start(bf16[128,128]{1,0:T(8,128)(2,1)S(1)} %constant_dynamic-update-slice_fusion.2.refs_2_), channel_id=1, source_target_pairs={{0,24},{1,25},{2,26},{3,27},{4,28},{5,29},{6,30},{7,31},{8,16},{9,... | collective-permute-start | bytes 98312 | tf_op jit(solution)/shard_map/ppermute | solution.py:374
  21.3 5.5 %collective-permute-start.8 = (bf16[128,128]{1,0:T(8,128)(2,1)S(1)}, bf16[128,128]{1,0:T(8,128)(2,1)S(1)}, u32[]{:S(2)}, u32[]{:S(2)}) collective-permute-start(bf16[128,128]{1,0:T(8,128)(2,1)S(1)} %constant_dynamic-update-slice_fusion.2.refs_2_), channel_id=1, source_target_pairs={{0,16},{1,17},{2,18},{3,19},{4,20},{5,21},{6,22},{7,23},{8,24},{9,... | collective-permute-start | bytes 98312 | tf_op jit(solution)/shard_map/ppermute | solution.py:374
  21.3 5.5 %collective-permute-start.7 = (bf16[128,128]{1,0:T(8,128)(2,1)S(1)}, bf16[128,128]{1,0:T(8,128)(2,1)S(1)}, u32[]{:S(2)}, u32[]{:S(2)}) collective-permute-start(bf16[128,128]{1,0:T(8,128)(2,1)S(1)} %constant_dynamic-update-slice_fusion.2.refs_2_), channel_id=1, source_target_pairs={{0,8},{1,9},{2,10},{3,11},{4,12},{5,13},{6,14},{7,15},{8,0},{9,1},... | collective-permute-start | bytes 98312 | tf_op jit(solution)/shard_map/ppermute | solution.py:374
  23.9 5.9 %collective-permute-start.2 = (bf16[128,512]{1,0:T(8,128)(2,1)S(1)}, bf16[128,512]{1,0:T(8,128)(2,1)S(1)}, u32[]{:S(2)}, u32[]{:S(2)}) collective-permute-start(bf16[128,512]{1,0:T(8,128)(2,1)S(1)} %compact.1.refs_2_), channel_id=1, source_target_pairs={{0,8},{1,9},{2,10},{3,11},{4,12},{5,13},{6,14},{7,15},{8,0},{9,1},... | collective-permute-start | bytes 393224 | tf_op jit(solution)/shard_map/ppermute | solution.py:374
  25.0 5.2 %collective-permute-start.1 = (bf16[128,512]{1,0:T(8,128)(2,1)S(1)}, bf16[128,512]{1,0:T(8,128)(2,1)S(1)}, u32[]{:S(2)}, u32[]{:S(2)}) collective-permute-start(bf16[128,512]{1,0:T(8,128)(2,1)S(1)} %compact.1.refs_2_), channel_id=1, source_target_pairs={{0,4},{1,5},{2,6},{3,7},{4,0},{5,1},{6,2},{7,3},{8,12},{9,13},{10,... | collective-permute-start | bytes 393224 | tf_op jit(solution)/shard_map/ppermute | solution.py:374
  25.5 5.0 %collective-permute-start = (bf16[128,512]{1,0:T(8,128)(2,1)S(1)}, bf16[128,512]{1,0:T(8,128)(2,1)S(1)}, u32[]{:S(2)}, u32[]{:S(2)}) collective-permute-start(bf16[128,512]{1,0:T(8,128)(2,1)S(1)} %compact.1.refs_2_), channel_id=1, source_target_pairs={{0,2},{1,3},{2,0},{3,1},{4,6},{5,7},{6,4},{7,5},{8,10},{9,11},{10,... | collective-permute-start | bytes 393224 | tf_op jit(solution)/shard_map/ppermute | solution.py:374
  29.7 2.6 %collective-permute-start.10 = (bf16[128,512]{1,0:T(8,128)(2,1)S(1)}, bf16[128,512]{1,0:T(8,128)(2,1)S(1)}, u32[]{:S(2)}, u32[]{:S(2)}) collective-permute-start(bf16[128,512]{1,0:T(8,128)(2,1)S(1)} %compact.1.refs_2_), channel_id=1, source_target_pairs={{0,1},{1,0},{2,3},{3,2},{4,5},{5,4},{6,7},{7,6},{8,9},{9,8},{10,11... | collective-permute-start | bytes 393224 | tf_op jit(solution)/shard_map/ppermute | solution.py:374
  30.5 1.9 %copy-start = (bf16[128,4096]{1,0:T(8,128)(2,1)S(1)}, bf16[128,4096]{1,0:T(8,128)(2,1)}, u32[]{:S(2)}) copy-start(bf16[128,4096]{1,0:T(8,128)(2,1)} %slab_ref.1) | copy-start | bytes 3145732
  30.5 1.9 %copy-start.1 = (bf16[128,128]{1,0:T(8,128)(2,1)S(1)}, bf16[128,128]{1,0:T(8,128)(2,1)}, u32[]{:S(2)}) copy-start(bf16[128,128]{1,0:T(8,128)(2,1)} %cross_ref.1) | copy-start | bytes 98308
  30.5 1.8 %collective-permute-start.11 = (bf16[128,512]{1,0:T(8,128)(2,1)S(1)}, bf16[128,512]{1,0:T(8,128)(2,1)S(1)}, u32[]{:S(2)}, u32[]{:S(2)}) collective-permute-start(bf16[128,512]{1,0:T(8,128)(2,1)S(1)} %collective-permute-done.refs_3_), channel_id=1, source_target_pairs={{0,1},{1,0},{2,3},{3,2},{4,5},{5,4},{6,7},{7,6},{8,9},{9,8},{10,11... | collective-permute-start | bytes 393224 | tf_op jit(solution)/shard_map/ppermute | solution.py:374
  30.5 1.8 %collective-permute-start.12 = (bf16[128,512]{1,0:T(8,128)(2,1)S(1)}, bf16[128,512]{1,0:T(8,128)(2,1)S(1)}, u32[]{:S(2)}, u32[]{:S(2)}) collective-permute-start(bf16[128,512]{1,0:T(8,128)(2,1)S(1)} %collective-permute-done.1.refs_4_), channel_id=1, source_target_pairs={{0,1},{1,0},{2,3},{3,2},{4,5},{5,4},{6,7},{7,6},{8,9},{9,8},{10,11... | collective-permute-start | bytes 393224 | tf_op jit(solution)/shard_map/ppermute | solution.py:374
  31.0 1.3 %collective-permute-start.13 = (bf16[128,512]{1,0:T(8,128)(2,1)S(1)}, bf16[128,512]{1,0:T(8,128)(2,1)S(1)}, u32[]{:S(2)}, u32[]{:S(2)}) collective-permute-start(bf16[128,512]{1,0:T(8,128)(2,1)S(1)} %collective-permute-done.2.refs_5_), channel_id=1, source_target_pairs={{0,1},{1,0},{2,3},{3,2},{4,5},{5,4},{6,7},{7,6},{8,9},{9,8},{10,11... | collective-permute-start | bytes 393224 | tf_op jit(solution)/shard_map/ppermute | solution.py:374

commit v7 on v6

--- a/solution.py
+++ b/solution.py
@@ -417,12 +417,12 @@
     for group, piece in zip((2, 4, 6), arrived):
         by[group] = piece
         by[group + 1] = swap(piece, 1)
-    inverse, gains = invert(range(early, panels), (*midway, *(by[g] for g in (0, 2, 4, 6))))
-    flips = (0, 2, 4, 6, 1, 3, 5, 7)
+    inverse, gains = invert(range(early, panels), (*midway, *(by[g] for g in (0, 1, 2, 4, 6))))
+    flips = (0, 1, 2, 4, 6, 3, 5, 7)
     return pl.pallas_call(
         functools.partial(update_kernel, width, flips),
         out_shape=jax.ShapeDtypeStruct(slab.shape, jnp.bfloat16),
-        in_specs=[VMEM] * 8,
+        in_specs=[VMEM] * 7,
         out_specs=HBM,
         scratch_shapes=[
             pltpu.VMEM((len(flips), rows, width), jnp.bfloat16),
@@ -430,7 +430,7 @@
         ],
         compiler_params=room(12),
         name="update",
-    )(inverse, gains, cross, slab, *(by[g] for g in (1, 3, 5, 7)))
+    )(inverse, gains, cross, slab, *(by[g] for g in (3, 5, 7)))
 
 
 def solution(mesh):

time: 34 us -> 34.7 us (1.021)
  waiting for transfers between devices: 5.72 us -> 6.25 us
    ppermute x14, waiting for transfers between devices: 5.07 us -> 5.6 us  [swap(): return lax.ppermute(value, 'rows', [(i, i ^ bit) for i in range(groups)])]
  transfers between devices with their start and end apart: 15 -> 15, of which waited for: 6 -> 7; matrix products, arithmetic and copies ran while one was open for 0% -> 0% of each run, Pallas kernels for 15% -> 15%
where the time goes in v7:
time: 34.7 us; the launch traced here: 34.4 us
  starting transfers between devices  19.2 us (55%)
  Pallas kernels  8.74 us (25%)
  waiting for transfers between devices  6.25 us (18%)
    ppermute x14, starting transfers between devices, swap(): return lax.ppermute(value, 'rows', [(i, i ^ bit) for i in range(groups)])  11.9 us
    all_to_all x1, starting transfers between devices, plane_body(): lax.all_to_all(packed.reshape(groups, SLOTS, -1), 'rows', split_axis=0, c...  7.3 us
    ppermute x14, waiting for transfers between devices, swap(): return lax.ppermute(value, 'rows', [(i, i ^ bit) for i in range(groups)])  5.6 us
    pallas_call x2, Pallas kernels, invert(): pl.pallas_call(functools.partial(invert_kernel, panel_range, len(sources)...  4.08 us
    pallas_call x1, Pallas kernels, plane_body(): pl.pallas_call(functools.partial(pick_kernel, groups, width), out_shape=(...  2.34 us
    pallas_call x1, Pallas kernels, plane_body(): pl.pallas_call(functools.partial(update_kernel, width, flips), out_shape=...  1.41 us
  transfers between devices with their start and end apart: 15, of which 7 were waited for; matrix products, arithmetic and copies ran while one was open for 0% of the time, Pallas kernels for 15%

profile of v7, /device:TPU:0, one launch (start us, length us, event | category | flops | bytes accessed | tf_op | source)
XLA Modules:
  0.0 34.4 jit_solution(15211566178905225479)
XLA Ops:
  0.0 2.3 %pick.1 = (bf16[512,384]{1,0:T(8,128)(2,1)}, bf16[16,128]{1,0:T(8,128)(2,1)}) custom-call(s32[1,128]{1,0:T(1,128)} %bitcast.5, bf16[128,4096]{1,0:T(8,128)(2,1)} %slab_ref.1, bf16[128,128]{1,0:T(8,128)(2,1)} %cross_ref.1), custom_call_target="tpu_custom_call" | custom-call | tf_op jit(solution)/shard_map/pick/pallas_call | solution.py:337
  2.4 7.3 %all-to-all-start = ((bf16[32,16,384]{2,1,0:T(8,128)(2,1)}), bf16[32,16,384]{2,1,0:T(8,128)(2,1)S(1)}, u32[]{:S(2)}, u32[]{:S(2)}) async-start(bf16[32,16,384]{2,1,0:T(8,128)(2,1)} %bitcast.8), calls=%async_computation | async-start | bytes 786432 | tf_op jit(solution)/shard_map/all_to_all | solution.py:376
  9.7 0.3 collective-permute-start.3
  10.0 0.9 %collective-permute-done.3 = bf16[16,128]{1,0:T(8,128)(2,1)S(1)} collective-permute-done((bf16[16,128]{1,0:T(8,128)(2,1)S(1)}, bf16[16,128]{1,0:T(8,128)(2,1)S(1)}, u32[]{:S(2)}, u32[]{:S(2)}) %collective-permute-start.3) | collective-permute-done | bytes 4128 | tf_op jit(solution)/shard_map/ppermute | solution.py:374
  10.9 1.8 %collective-permute-start.4 = (bf16[32,128]{1,0:T(8,128)(2,1)S(1)}, bf16[32,128]{1,0:T(8,128)(2,1)S(1)}, u32[]{:S(2)}, u32[]{:S(2)}) collective-permute-start(bf16[32,128]{1,0:T(8,128)(2,1)S(1)} %get-tuple-element.33), channel_id=1, source_target_pairs={{0,2},{1,3},{2,0},{3,1},{4,6},{5,7},{6,4},{7,5},{8,10},{9,11},{10,... | collective-permute-start | bytes 24584 | tf_op jit(solution)/shard_map/ppermute | solution.py:374
  12.7 1.5 %collective-permute-start.6 = (bf16[32,128]{1,0:T(8,128)(2,1)S(1)}, bf16[32,128]{1,0:T(8,128)(2,1)S(1)}, u32[]{:S(2)}, u32[]{:S(2)}) collective-permute-start(bf16[32,128]{1,0:T(8,128)(2,1)S(1)} %get-tuple-element.33), channel_id=1, source_target_pairs={{0,6},{1,7},{2,4},{3,5},{4,2},{5,3},{6,0},{7,1},{8,14},{9,15},{10,... | collective-permute-start | bytes 24584 | tf_op jit(solution)/shard_map/ppermute | solution.py:374
  14.1 0.3 collective-permute-start.5
  14.4 0.2 collective-permute-done.4
  14.6 3.2 %collective-permute-done.5 = bf16[32,128]{1,0:T(8,128)(2,1)S(1)} collective-permute-done((bf16[32,128]{1,0:T(8,128)(2,1)S(1)}, bf16[32,128]{1,0:T(8,128)(2,1)S(1)}, u32[]{:S(2)}, u32[]{:S(2)}) %collective-permute-start.5) | collective-permute-done | bytes 8224 | tf_op jit(solution)/shard_map/ppermute | solution.py:374
  17.8 0.0 collective-permute-done.6
  17.8 0.0 copy-start.3
  17.8 3.5 %collective-permute-start.9 = (bf16[128,128]{1,0:T(8,128)(2,1)S(1)}, bf16[128,128]{1,0:T(8,128)(2,1)S(1)}, u32[]{:S(2)}, u32[]{:S(2)}) collective-permute-start(bf16[128,128]{1,0:T(8,128)(2,1)S(1)} %constant_dynamic-update-slice_fusion.2.refs_2_), channel_id=1, source_target_pairs={{0,24},{1,25},{2,26},{3,27},{4,28},{5,29},{6,30},{7,31},{8,16},{9,... | collective-permute-start | bytes 98312 | tf_op jit(solution)/shard_map/ppermute | solution.py:374
  21.3 0.0 collective-permute-start.8
  21.3 1.0 %collective-permute-start.7 = (bf16[128,128]{1,0:T(8,128)(2,1)S(1)}, bf16[128,128]{1,0:T(8,128)(2,1)S(1)}, u32[]{:S(2)}, u32[]{:S(2)}) collective-permute-start(bf16[128,128]{1,0:T(8,128)(2,1)S(1)} %constant_dynamic-update-slice_fusion.2.refs_2_), channel_id=1, source_target_pairs={{0,8},{1,9},{2,10},{3,11},{4,12},{5,13},{6,14},{7,15},{8,0},{9,1},... | collective-permute-start | bytes 98312 | tf_op jit(solution)/shard_map/ppermute | solution.py:374
  22.3 0.6 %order.1 = (bf16[512,512]{1,0:T(8,128)(2,1)S(1)}, bf16[128,512]{1,0:T(8,128)(2,1)S(1)}, f32[128,128]{1,0:T(8,128)S(1)}) custom-call(s32[1,128]{1,0:T(1,128)S(1)} %bitcast.6, f32[1,128]{1,0:T(1,128)S(1)} %bitcast.7), custom_call_target="tpu_custom_call" | custom-call | flops 2097152000 | bytes 65536 | tf_op jit(solution)/shard_map/order/pallas_call | solution.py:357
  22.9 0.7 %all-to-all-done = bf16[32,16,384]{2,1,0:T(8,128)(2,1)S(1)} async-done(((bf16[32,16,384]{2,1,0:T(8,128)(2,1)}), bf16[32,16,384]{2,1,0:T(8,128)(2,1)S(1)}, u32[]{:S(2)}, u32[]{:S(2)}) %all-to-all-start) | async-done | bytes 393248 | tf_op jit(solution)/shard_map/all_to_all | solution.py:376
  23.5 0.3 compact.1.refs_2_
  23.9 0.1 collective-permute-start.10
  24.0 1.2 %collective-permute-start.2 = (bf16[128,512]{1,0:T(8,128)(2,1)S(1)}, bf16[128,512]{1,0:T(8,128)(2,1)S(1)}, u32[]{:S(2)}, u32[]{:S(2)}) collective-permute-start(bf16[128,512]{1,0:T(8,128)(2,1)S(1)} %compact.1.refs_2_), channel_id=1, source_target_pairs={{0,8},{1,9},{2,10},{3,11},{4,12},{5,13},{6,14},{7,15},{8,0},{9,1},... | collective-permute-start | bytes 393224 | tf_op jit(solution)/shard_map/ppermute | solution.py:374
  25.1 0.4 %collective-permute-start.1 = (bf16[128,512]{1,0:T(8,128)(2,1)S(1)}, bf16[128,512]{1,0:T(8,128)(2,1)S(1)}, u32[]{:S(2)}, u32[]{:S(2)}) collective-permute-start(bf16[128,512]{1,0:T(8,128)(2,1)S(1)} %compact.1.refs_2_), channel_id=1, source_target_pairs={{0,4},{1,5},{2,6},{3,7},{4,0},{5,1},{6,2},{7,3},{8,12},{9,13},{10,... | collective-permute-start | bytes 393224 | tf_op jit(solution)/shard_map/ppermute | solution.py:374
  25.6 0.6 %collective-permute-done.8.refs_4_ = bf16[128,128]{1,0:T(8,128)(2,1)S(1)} collective-permute-done((bf16[128,128]{1,0:T(8,128)(2,1)S(1)}, bf16[128,128]{1,0:T(8,128)(2,1)S(1)}, u32[]{:S(2)}, u32[]{:S(2)}) %collective-permute-start.8) | collective-permute-done | bytes 32800 | tf_op jit(solution)/shard_map/ppermute | solution.py:374
  26.1 1.4 %collective-permute-start = (bf16[128,512]{1,0:T(8,128)(2,1)S(1)}, bf16[128,512]{1,0:T(8,128)(2,1)S(1)}, u32[]{:S(2)}, u32[]{:S(2)}) collective-permute-start(bf16[128,512]{1,0:T(8,128)(2,1)S(1)} %compact.1.refs_2_), channel_id=1, source_target_pairs={{0,2},{1,3},{2,0},{3,1},{4,6},{5,7},{6,4},{7,5},{8,10},{9,11},{10,... | collective-permute-start | bytes 393224 | tf_op jit(solution)/shard_map/ppermute | solution.py:374
  27.6 2.8 %invert.2 = (f32[128,128]{1,0:T(8,128)S(1)}, f32[128,128]{1,0:T(8,128)S(1)}) custom-call(bf16[128,512]{1,0:T(8,128)(2,1)S(1)} %get-tuple-element.21.refs_0_, f32[128,128]{1,0:T(8,128)S(1)} %get-tuple-element.22.refs_1_, bf16[128,128]{1,0:T(8,128)(2,1)S(1)} %constant_dynamic-update-slice_fusion.2.refs_2_, ...), custom_call_target="tpu_custom_call" | custom-call | flops 5452595200 | bytes 65536 | tf_op jit(solution)/shard_map/invert/pallas_call | solution.py:396
  30.4 0.0 collective-permute-done.2.refs_6_
  30.4 0.3 collective-permute-done.1.refs_5_
  30.7 0.4 %collective-permute-done.refs_4_ = bf16[128,512]{1,0:T(8,128)(2,1)S(1)} collective-permute-done((bf16[128,512]{1,0:T(8,128)(2,1)S(1)}, bf16[128,512]{1,0:T(8,128)(2,1)S(1)}, u32[]{:S(2)}, u32[]{:S(2)}) %collective-permute-start) | collective-permute-done | bytes 131104 | tf_op jit(solution)/shard_map/ppermute | solution.py:374
  31.1 0.5 %collective-permute-start.12 = (bf16[128,512]{1,0:T(8,128)(2,1)S(1)}, bf16[128,512]{1,0:T(8,128)(2,1)S(1)}, u32[]{:S(2)}, u32[]{:S(2)}) collective-permute-start(bf16[128,512]{1,0:T(8,128)(2,1)S(1)} %collective-permute-done.1.refs_5_), channel_id=1, source_target_pairs={{0,1},{1,0},{2,3},{3,2},{4,5},{5,4},{6,7},{7,6},{8,9},{9,8},{10,11... | collective-permute-start | bytes 393224 | tf_op jit(solution)/shard_map/ppermute | solution.py:374
  31.6 0.1 collective-permute-start.13
  31.7 1.3 %invert.3 = (bf16[384,128]{1,0:T(8,128)(2,1)S(1)}, bf16[5,128,512]{2,1,0:T(8,128)(2,1)S(1)}) custom-call(f32[128,128]{1,0:T(8,128)S(1)} %get-tuple-element.26.refs_0_, f32[128,128]{1,0:T(8,128)S(1)} %get-tuple-element.27.refs_1_, bf16[128,512]{1,0:T(8,128)(2,1)S(1)} %compact.1.refs_2_, bf16[128,512]{1,0:T(8,128)(2,1)S(1)} %collective-permute-done.10.refs_3_, ...), custom_call_target="tpu_custom_call" | custom-call | flops 1258291200 | bytes 65536 | tf_op jit(solution)/shard_map/invert/pallas_call | solution.py:396
  33.0 0.0 collective-permute-done.12.refs_1_
  33.0 0.0 collective-permute-done.13.refs_2_
  33.0 1.4 %update.1 = bf16[128,4096]{1,0:T(8,128)(2,1)} custom-call(bf16[384,128]{1,0:T(8,128)(2,1)S(1)} %get-tuple-element.31.inverse_ref, bf16[5,128,512]{2,1,0:T(8,128)(2,1)S(1)} %get-tuple-element.32.gain_ref, bf16[128,128]{1,0:T(8,128)(2,1)S(1)} %copy-done.1, bf16[128,4096]{1,0:T(8,128)(2,1)S(1)} %copy-done, ...), custom_call_target="tpu_custom_call" | custom-call | tf_op jit(solution)/shard_map/update/pallas_call | solution.py:422
  (19 shorter events, 0.1 us)
Async XLA Ops:
  2.3 7.3 %copy-start.4 = (bf16[16,128]{1,0:T(8,128)(2,1)S(1)}, bf16[16,128]{1,0:T(8,128)(2,1)}, u32[]{:S(2)}) copy-start(bf16[16,128]{1,0:T(8,128)(2,1)} %get-tuple-element.23) | copy-start | bytes 12292
  2.4 21.2 %all-to-all-start = ((bf16[32,16,384]{2,1,0:T(8,128)(2,1)}), bf16[32,16,384]{2,1,0:T(8,128)(2,1)S(1)}, u32[]{:S(2)}, u32[]{:S(2)}) async-start(bf16[32,16,384]{2,1,0:T(8,128)(2,1)} %bitcast.8), calls=%async_computation | async-start | bytes 786432 | tf_op jit(solution)/shard_map/all_to_all | solution.py:376
  9.7 1.2 %collective-permute-start.3 = (bf16[16,128]{1,0:T(8,128)(2,1)S(1)}, bf16[16,128]{1,0:T(8,128)(2,1)S(1)}, u32[]{:S(2)}, u32[]{:S(2)}) collective-permute-start(bf16[16,128]{1,0:T(8,128)(2,1)S(1)} %copy-done.4), channel_id=1, source_target_pairs={{0,1},{1,0},{2,3},{3,2},{4,5},{5,4},{6,7},{7,6},{8,9},{9,8},{10,11... | collective-permute-start | bytes 12296 | tf_op jit(solution)/shard_map/ppermute | solution.py:374
  10.9 3.7 %collective-permute-start.4 = (bf16[32,128]{1,0:T(8,128)(2,1)S(1)}, bf16[32,128]{1,0:T(8,128)(2,1)S(1)}, u32[]{:S(2)}, u32[]{:S(2)}) collective-permute-start(bf16[32,128]{1,0:T(8,128)(2,1)S(1)} %get-tuple-element.33), channel_id=1, source_target_pairs={{0,2},{1,3},{2,0},{3,1},{4,6},{5,7},{6,4},{7,5},{8,10},{9,11},{10,... | collective-permute-start | bytes 24584 | tf_op jit(solution)/shard_map/ppermute | solution.py:374
  12.7 5.1 %collective-permute-start.6 = (bf16[32,128]{1,0:T(8,128)(2,1)S(1)}, bf16[32,128]{1,0:T(8,128)(2,1)S(1)}, u32[]{:S(2)}, u32[]{:S(2)}) collective-permute-start(bf16[32,128]{1,0:T(8,128)(2,1)S(1)} %get-tuple-element.33), channel_id=1, source_target_pairs={{0,6},{1,7},{2,4},{3,5},{4,2},{5,3},{6,0},{7,1},{8,14},{9,15},{10,... | collective-permute-start | bytes 24584 | tf_op jit(solution)/shard_map/ppermute | solution.py:374
  14.1 3.7 %collective-permute-start.5 = (bf16[32,128]{1,0:T(8,128)(2,1)S(1)}, bf16[32,128]{1,0:T(8,128)(2,1)S(1)}, u32[]{:S(2)}, u32[]{:S(2)}) collective-permute-start(bf16[32,128]{1,0:T(8,128)(2,1)S(1)} %get-tuple-element.33), channel_id=1, source_target_pairs={{0,4},{1,5},{2,6},{3,7},{4,0},{5,1},{6,2},{7,3},{8,12},{9,13},{10,... | collective-permute-start | bytes 24584 | tf_op jit(solution)/shard_map/ppermute | solution.py:374
  17.8 4.5 %copy-start.2 = (s32[128]{0:T(128)S(1)}, s32[128]{0:T(128)}, u32[]{:S(2)}) copy-start(s32[128]{0:T(128)} %param.6) | copy-start | bytes 1540
  17.8 4.5 %copy-start.3 = (f32[128]{0:T(128)S(1)}, f32[128]{0:T(128)}, u32[]{:S(2)}) copy-start(f32[128]{0:T(128)} %param.7) | copy-start | bytes 1540
  17.8 7.3 %collective-permute-start.9 = (bf16[128,128]{1,0:T(8,128)(2,1)S(1)}, bf16[128,128]{1,0:T(8,128)(2,1)S(1)}, u32[]{:S(2)}, u32[]{:S(2)}) collective-permute-start(bf16[128,128]{1,0:T(8,128)(2,1)S(1)} %constant_dynamic-update-slice_fusion.2.refs_2_), channel_id=1, source_target_pairs={{0,24},{1,25},{2,26},{3,27},{4,28},{5,29},{6,30},{7,31},{8,16},{9,... | collective-permute-start | bytes 98312 | tf_op jit(solution)/shard_map/ppermute | solution.py:374
  21.3 4.8 %collective-permute-start.8 = (bf16[128,128]{1,0:T(8,128)(2,1)S(1)}, bf16[128,128]{1,0:T(8,128)(2,1)S(1)}, u32[]{:S(2)}, u32[]{:S(2)}) collective-permute-start(bf16[128,128]{1,0:T(8,128)(2,1)S(1)} %constant_dynamic-update-slice_fusion.2.refs_2_), channel_id=1, source_target_pairs={{0,16},{1,17},{2,18},{3,19},{4,20},{5,21},{6,22},{7,23},{8,24},{9,... | collective-permute-start | bytes 98312 | tf_op jit(solution)/shard_map/ppermute | solution.py:374
  21.3 6.2 %collective-permute-start.7 = (bf16[128,128]{1,0:T(8,128)(2,1)S(1)}, bf16[128,128]{1,0:T(8,128)(2,1)S(1)}, u32[]{:S(2)}, u32[]{:S(2)}) collective-permute-start(bf16[128,128]{1,0:T(8,128)(2,1)S(1)} %constant_dynamic-update-slice_fusion.2.refs_2_), channel_id=1, source_target_pairs={{0,8},{1,9},{2,10},{3,11},{4,12},{5,13},{6,14},{7,15},{8,0},{9,1},... | collective-permute-start | bytes 98312 | tf_op jit(solution)/shard_map/ppermute | solution.py:374
  23.9 7.8 %collective-permute-start.10 = (bf16[128,512]{1,0:T(8,128)(2,1)S(1)}, bf16[128,512]{1,0:T(8,128)(2,1)S(1)}, u32[]{:S(2)}, u32[]{:S(2)}) collective-permute-start(bf16[128,512]{1,0:T(8,128)(2,1)S(1)} %compact.1.refs_2_), channel_id=1, source_target_pairs={{0,1},{1,0},{2,3},{3,2},{4,5},{5,4},{6,7},{7,6},{8,9},{9,8},{10,11... | collective-permute-start | bytes 393224 | tf_op jit(solution)/shard_map/ppermute | solution.py:374
  24.0 6.4 %collective-permute-start.2 = (bf16[128,512]{1,0:T(8,128)(2,1)S(1)}, bf16[128,512]{1,0:T(8,128)(2,1)S(1)}, u32[]{:S(2)}, u32[]{:S(2)}) collective-permute-start(bf16[128,512]{1,0:T(8,128)(2,1)S(1)} %compact.1.refs_2_), channel_id=1, source_target_pairs={{0,8},{1,9},{2,10},{3,11},{4,12},{5,13},{6,14},{7,15},{8,0},{9,1},... | collective-permute-start | bytes 393224 | tf_op jit(solution)/shard_map/ppermute | solution.py:374
  25.1 5.6 %collective-permute-start.1 = (bf16[128,512]{1,0:T(8,128)(2,1)S(1)}, bf16[128,512]{1,0:T(8,128)(2,1)S(1)}, u32[]{:S(2)}, u32[]{:S(2)}) collective-permute-start(bf16[128,512]{1,0:T(8,128)(2,1)S(1)} %compact.1.refs_2_), channel_id=1, source_target_pairs={{0,4},{1,5},{2,6},{3,7},{4,0},{5,1},{6,2},{7,3},{8,12},{9,13},{10,... | collective-permute-start | bytes 393224 | tf_op jit(solution)/shard_map/ppermute | solution.py:374
  26.1 5.0 %collective-permute-start = (bf16[128,512]{1,0:T(8,128)(2,1)S(1)}, bf16[128,512]{1,0:T(8,128)(2,1)S(1)}, u32[]{:S(2)}, u32[]{:S(2)}) collective-permute-start(bf16[128,512]{1,0:T(8,128)(2,1)S(1)} %compact.1.refs_2_), channel_id=1, source_target_pairs={{0,2},{1,3},{2,0},{3,1},{4,6},{5,7},{6,4},{7,5},{8,10},{9,11},{10,... | collective-permute-start | bytes 393224 | tf_op jit(solution)/shard_map/ppermute | solution.py:374
  31.1 1.9 %copy-start = (bf16[128,4096]{1,0:T(8,128)(2,1)S(1)}, bf16[128,4096]{1,0:T(8,128)(2,1)}, u32[]{:S(2)}) copy-start(bf16[128,4096]{1,0:T(8,128)(2,1)} %slab_ref.1) | copy-start | bytes 3145732
  31.1 1.9 %copy-start.1 = (bf16[128,128]{1,0:T(8,128)(2,1)S(1)}, bf16[128,128]{1,0:T(8,128)(2,1)}, u32[]{:S(2)}) copy-start(bf16[128,128]{1,0:T(8,128)(2,1)} %cross_ref.1) | copy-start | bytes 98308
  31.1 1.9 %collective-permute-start.11 = (bf16[128,512]{1,0:T(8,128)(2,1)S(1)}, bf16[128,512]{1,0:T(8,128)(2,1)S(1)}, u32[]{:S(2)}, u32[]{:S(2)}) collective-permute-start(bf16[128,512]{1,0:T(8,128)(2,1)S(1)} %collective-permute-done.refs_4_), channel_id=1, source_target_pairs={{0,1},{1,0},{2,3},{3,2},{4,5},{5,4},{6,7},{7,6},{8,9},{9,8},{10,11... | collective-permute-start | bytes 393224 | tf_op jit(solution)/shard_map/ppermute | solution.py:374
  31.1 1.9 %collective-permute-start.12 = (bf16[128,512]{1,0:T(8,128)(2,1)S(1)}, bf16[128,512]{1,0:T(8,128)(2,1)S(1)}, u32[]{:S(2)}, u32[]{:S(2)}) collective-permute-start(bf16[128,512]{1,0:T(8,128)(2,1)S(1)} %collective-permute-done.1.refs_5_), channel_id=1, source_target_pairs={{0,1},{1,0},{2,3},{3,2},{4,5},{5,4},{6,7},{7,6},{8,9},{9,8},{10,11... | collective-permute-start | bytes 393224 | tf_op jit(solution)/shard_map/ppermute | solution.py:374
  31.6 1.4 %collective-permute-start.13 = (bf16[128,512]{1,0:T(8,128)(2,1)S(1)}, bf16[128,512]{1,0:T(8,128)(2,1)S(1)}, u32[]{:S(2)}, u32[]{:S(2)}) collective-permute-start(bf16[128,512]{1,0:T(8,128)(2,1)S(1)} %collective-permute-done.2.refs_6_), channel_id=1, source_target_pairs={{0,1},{1,0},{2,3},{3,2},{4,5},{5,4},{6,7},{7,6},{8,9},{9,8},{10,11... | collective-permute-start | bytes 393224 | tf_op jit(solution)/shard_map/ppermute | solution.py:374

commit v8 on v6

--- a/solution.py
+++ b/solution.py
@@ -411,7 +411,7 @@
 
     by = {0: observed, 1: swap(observed, 1)}
     by.update({group: swap(observed, bit) for bit, group in ((2, 2), (4, 4), (8, 6))})
-    panels, early = count // 8, 13 * count // 128
+    panels, early = count // 8, 14 * count // 128
     midway = invert(range(early), (cross_order, diagonal, *levels))
     arrived, midway = lax.optimization_barrier(([by[g] for g in (2, 4, 6)], midway))
     for group, piece in zip((2, 4, 6), arrived):

time: 34 us -> 34 us (level)
  transfers between devices with their start and end apart: 15 -> 15, of which waited for: 6 -> 7; matrix products, arithmetic and copies ran while one was open for 0% -> 0% of each run, Pallas kernels for 15% -> 15%
where the time goes in v8:
time: 34 us; the launch traced here: 33.8 us
  starting transfers between devices  19.2 us (56%)
  Pallas kernels  8.76 us (26%)
  waiting for transfers between devices  5.65 us (17%)
    ppermute x14, starting transfers between devices, swap(): return lax.ppermute(value, 'rows', [(i, i ^ bit) for i in range(groups)])  11.9 us
    all_to_all x1, starting transfers between devices, plane_body(): lax.all_to_all(packed.reshape(groups, SLOTS, -1), 'rows', split_axis=0, c...  7.3 us
    ppermute x14, waiting for transfers between devices, swap(): return lax.ppermute(value, 'rows', [(i, i ^ bit) for i in range(groups)])  5 us
    pallas_call x2, Pallas kernels, invert(): pl.pallas_call(functools.partial(invert_kernel, panel_range, len(sources)...  4.05 us
    pallas_call x1, Pallas kernels, plane_body(): pl.pallas_call(functools.partial(pick_kernel, groups, width), out_shape=(...  2.34 us
    pallas_call x1, Pallas kernels, plane_body(): pl.pallas_call(functools.partial(update_kernel, width, flips), out_shape=...  1.45 us
  transfers between devices with their start and end apart: 15, of which 7 were waited for; matrix products, arithmetic and copies ran while one was open for 0% of the time, Pallas kernels for 15%

profile of v8, /device:TPU:0, one launch (start us, length us, event | category | flops | bytes accessed | tf_op | source)
XLA Modules:
  0.0 33.8 jit_solution(6968607298025649546)
XLA Ops:
  0.0 2.3 %pick.1 = (bf16[512,384]{1,0:T(8,128)(2,1)}, bf16[16,128]{1,0:T(8,128)(2,1)}) custom-call(s32[1,128]{1,0:T(1,128)} %bitcast.5, bf16[128,4096]{1,0:T(8,128)(2,1)} %slab_ref.1, bf16[128,128]{1,0:T(8,128)(2,1)} %cross_ref.1), custom_call_target="tpu_custom_call" | custom-call | tf_op jit(solution)/shard_map/pick/pallas_call | solution.py:337
  2.4 7.3 %all-to-all-start = ((bf16[32,16,384]{2,1,0:T(8,128)(2,1)}), bf16[32,16,384]{2,1,0:T(8,128)(2,1)S(1)}, u32[]{:S(2)}, u32[]{:S(2)}) async-start(bf16[32,16,384]{2,1,0:T(8,128)(2,1)} %bitcast.8), calls=%async_computation | async-start | bytes 786432 | tf_op jit(solution)/shard_map/all_to_all | solution.py:376
  9.7 0.3 collective-permute-start.3
  10.0 0.9 %collective-permute-done.3 = bf16[16,128]{1,0:T(8,128)(2,1)S(1)} collective-permute-done((bf16[16,128]{1,0:T(8,128)(2,1)S(1)}, bf16[16,128]{1,0:T(8,128)(2,1)S(1)}, u32[]{:S(2)}, u32[]{:S(2)}) %collective-permute-start.3) | collective-permute-done | bytes 4128 | tf_op jit(solution)/shard_map/ppermute | solution.py:374
  10.9 1.8 %collective-permute-start.4 = (bf16[32,128]{1,0:T(8,128)(2,1)S(1)}, bf16[32,128]{1,0:T(8,128)(2,1)S(1)}, u32[]{:S(2)}, u32[]{:S(2)}) collective-permute-start(bf16[32,128]{1,0:T(8,128)(2,1)S(1)} %get-tuple-element.33), channel_id=1, source_target_pairs={{0,2},{1,3},{2,0},{3,1},{4,6},{5,7},{6,4},{7,5},{8,10},{9,11},{10,... | collective-permute-start | bytes 24584 | tf_op jit(solution)/shard_map/ppermute | solution.py:374
  12.7 1.5 %collective-permute-start.6 = (bf16[32,128]{1,0:T(8,128)(2,1)S(1)}, bf16[32,128]{1,0:T(8,128)(2,1)S(1)}, u32[]{:S(2)}, u32[]{:S(2)}) collective-permute-start(bf16[32,128]{1,0:T(8,128)(2,1)S(1)} %get-tuple-element.33), channel_id=1, source_target_pairs={{0,6},{1,7},{2,4},{3,5},{4,2},{5,3},{6,0},{7,1},{8,14},{9,15},{10,... | collective-permute-start | bytes 24584 | tf_op jit(solution)/shard_map/ppermute | solution.py:374
  14.1 0.3 collective-permute-start.5
  14.4 0.2 collective-permute-done.4
  14.6 3.2 %collective-permute-done.5 = bf16[32,128]{1,0:T(8,128)(2,1)S(1)} collective-permute-done((bf16[32,128]{1,0:T(8,128)(2,1)S(1)}, bf16[32,128]{1,0:T(8,128)(2,1)S(1)}, u32[]{:S(2)}, u32[]{:S(2)}) %collective-permute-start.5) | collective-permute-done | bytes 8224 | tf_op jit(solution)/shard_map/ppermute | solution.py:374
  17.8 0.0 copy-start.3
  17.8 3.5 %collective-permute-start.9 = (bf16[128,128]{1,0:T(8,128)(2,1)S(1)}, bf16[128,128]{1,0:T(8,128)(2,1)S(1)}, u32[]{:S(2)}, u32[]{:S(2)}) collective-permute-start(bf16[128,128]{1,0:T(8,128)(2,1)S(1)} %constant_dynamic-update-slice_fusion.2.refs_2_), channel_id=1, source_target_pairs={{0,24},{1,25},{2,26},{3,27},{4,28},{5,29},{6,30},{7,31},{8,16},{9,... | collective-permute-start | bytes 98312 | tf_op jit(solution)/shard_map/ppermute | solution.py:374
  21.3 0.0 collective-permute-start.8
  21.3 1.0 %collective-permute-start.7 = (bf16[128,128]{1,0:T(8,128)(2,1)S(1)}, bf16[128,128]{1,0:T(8,128)(2,1)S(1)}, u32[]{:S(2)}, u32[]{:S(2)}) collective-permute-start(bf16[128,128]{1,0:T(8,128)(2,1)S(1)} %constant_dynamic-update-slice_fusion.2.refs_2_), channel_id=1, source_target_pairs={{0,8},{1,9},{2,10},{3,11},{4,12},{5,13},{6,14},{7,15},{8,0},{9,1},... | collective-permute-start | bytes 98312 | tf_op jit(solution)/shard_map/ppermute | solution.py:374
  22.3 0.6 %order.1 = (bf16[512,512]{1,0:T(8,128)(2,1)S(1)}, bf16[128,512]{1,0:T(8,128)(2,1)S(1)}, f32[128,128]{1,0:T(8,128)S(1)}) custom-call(s32[1,128]{1,0:T(1,128)S(1)} %bitcast.6, f32[1,128]{1,0:T(1,128)S(1)} %bitcast.7), custom_call_target="tpu_custom_call" | custom-call | flops 2097152000 | bytes 65536 | tf_op jit(solution)/shard_map/order/pallas_call | solution.py:357
  22.9 0.7 %all-to-all-done = bf16[32,16,384]{2,1,0:T(8,128)(2,1)S(1)} async-done(((bf16[32,16,384]{2,1,0:T(8,128)(2,1)}), bf16[32,16,384]{2,1,0:T(8,128)(2,1)S(1)}, u32[]{:S(2)}, u32[]{:S(2)}) %all-to-all-start) | async-done | bytes 393248 | tf_op jit(solution)/shard_map/all_to_all | solution.py:376
  23.5 0.3 compact.1.refs_2_
  23.9 1.2 %collective-permute-start.2 = (bf16[128,512]{1,0:T(8,128)(2,1)S(1)}, bf16[128,512]{1,0:T(8,128)(2,1)S(1)}, u32[]{:S(2)}, u32[]{:S(2)}) collective-permute-start(bf16[128,512]{1,0:T(8,128)(2,1)S(1)} %compact.1.refs_2_), channel_id=1, source_target_pairs={{0,8},{1,9},{2,10},{3,11},{4,12},{5,13},{6,14},{7,15},{8,0},{9,1},... | collective-permute-start | bytes 393224 | tf_op jit(solution)/shard_map/ppermute | solution.py:374
  25.0 0.4 %collective-permute-start.1 = (bf16[128,512]{1,0:T(8,128)(2,1)S(1)}, bf16[128,512]{1,0:T(8,128)(2,1)S(1)}, u32[]{:S(2)}, u32[]{:S(2)}) collective-permute-start(bf16[128,512]{1,0:T(8,128)(2,1)S(1)} %compact.1.refs_2_), channel_id=1, source_target_pairs={{0,4},{1,5},{2,6},{3,7},{4,0},{5,1},{6,2},{7,3},{8,12},{9,13},{10,... | collective-permute-start | bytes 393224 | tf_op jit(solution)/shard_map/ppermute | solution.py:374
  25.5 0.0 collective-permute-done.9.refs_5_
  25.5 1.3 %collective-permute-start = (bf16[128,512]{1,0:T(8,128)(2,1)S(1)}, bf16[128,512]{1,0:T(8,128)(2,1)S(1)}, u32[]{:S(2)}, u32[]{:S(2)}) collective-permute-start(bf16[128,512]{1,0:T(8,128)(2,1)S(1)} %compact.1.refs_2_), channel_id=1, source_target_pairs={{0,2},{1,3},{2,0},{3,1},{4,6},{5,7},{6,4},{7,5},{8,10},{9,11},{10,... | collective-permute-start | bytes 393224 | tf_op jit(solution)/shard_map/ppermute | solution.py:374
  26.8 3.0 %invert.2 = (f32[128,128]{1,0:T(8,128)S(1)}, f32[128,128]{1,0:T(8,128)S(1)}) custom-call(bf16[128,512]{1,0:T(8,128)(2,1)S(1)} %get-tuple-element.21.refs_0_, f32[128,128]{1,0:T(8,128)S(1)} %get-tuple-element.22.refs_1_, bf16[128,128]{1,0:T(8,128)(2,1)S(1)} %constant_dynamic-update-slice_fusion.2.refs_2_, ...), custom_call_target="tpu_custom_call" | custom-call | flops 5872025600 | bytes 65536 | tf_op jit(solution)/shard_map/invert/pallas_call | solution.py:396
  29.9 0.1 collective-permute-start.10
  30.0 0.0 collective-permute-done.2.refs_5_
  30.0 0.3 collective-permute-done.1.refs_4_
  30.2 0.2 collective-permute-done.refs_3_
  30.5 0.1 collective-permute-start.11
  30.6 0.4 %collective-permute-start.12 = (bf16[128,512]{1,0:T(8,128)(2,1)S(1)}, bf16[128,512]{1,0:T(8,128)(2,1)S(1)}, u32[]{:S(2)}, u32[]{:S(2)}) collective-permute-start(bf16[128,512]{1,0:T(8,128)(2,1)S(1)} %collective-permute-done.1.refs_4_), channel_id=1, source_target_pairs={{0,1},{1,0},{2,3},{3,2},{4,5},{5,4},{6,7},{7,6},{8,9},{9,8},{10,11... | collective-permute-start | bytes 393224 | tf_op jit(solution)/shard_map/ppermute | solution.py:374
  31.0 0.1 collective-permute-start.13
  31.1 1.0 %invert.3 = (bf16[384,128]{1,0:T(8,128)(2,1)S(1)}, bf16[4,128,512]{2,1,0:T(8,128)(2,1)S(1)}) custom-call(f32[128,128]{1,0:T(8,128)S(1)} %get-tuple-element.26.refs_0_, f32[128,128]{1,0:T(8,128)S(1)} %get-tuple-element.27.refs_1_, bf16[128,512]{1,0:T(8,128)(2,1)S(1)} %compact.1.refs_2_, bf16[128,512]{1,0:T(8,128)(2,1)S(1)} %collective-permute-done.refs_3_, ...), custom_call_target="tpu_custom_call" | custom-call | flops 838860800 | bytes 65536 | tf_op jit(solution)/shard_map/invert/pallas_call | solution.py:396
  32.1 0.0 collective-permute-done.10.refs_0_
  32.1 0.2 collective-permute-done.13.refs_3_
  32.3 1.5 %update.1 = bf16[128,4096]{1,0:T(8,128)(2,1)} custom-call(bf16[384,128]{1,0:T(8,128)(2,1)S(1)} %get-tuple-element.31.inverse_ref, bf16[4,128,512]{2,1,0:T(8,128)(2,1)S(1)} %get-tuple-element.32.gain_ref, bf16[128,128]{1,0:T(8,128)(2,1)S(1)} %copy-done.1, bf16[128,4096]{1,0:T(8,128)(2,1)S(1)} %copy-done, ...), custom_call_target="tpu_custom_call" | custom-call | tf_op jit(solution)/shard_map/update/pallas_call | solution.py:422
  (19 shorter events, 0.1 us)
Async XLA Ops:
  2.3 7.3 %copy-start.4 = (bf16[16,128]{1,0:T(8,128)(2,1)S(1)}, bf16[16,128]{1,0:T(8,128)(2,1)}, u32[]{:S(2)}) copy-start(bf16[16,128]{1,0:T(8,128)(2,1)} %get-tuple-element.23) | copy-start | bytes 12292
  2.4 21.2 %all-to-all-start = ((bf16[32,16,384]{2,1,0:T(8,128)(2,1)}), bf16[32,16,384]{2,1,0:T(8,128)(2,1)S(1)}, u32[]{:S(2)}, u32[]{:S(2)}) async-start(bf16[32,16,384]{2,1,0:T(8,128)(2,1)} %bitcast.8), calls=%async_computation | async-start | bytes 786432 | tf_op jit(solution)/shard_map/all_to_all | solution.py:376
  9.7 1.2 %collective-permute-start.3 = (bf16[16,128]{1,0:T(8,128)(2,1)S(1)}, bf16[16,128]{1,0:T(8,128)(2,1)S(1)}, u32[]{:S(2)}, u32[]{:S(2)}) collective-permute-start(bf16[16,128]{1,0:T(8,128)(2,1)S(1)} %copy-done.4), channel_id=1, source_target_pairs={{0,1},{1,0},{2,3},{3,2},{4,5},{5,4},{6,7},{7,6},{8,9},{9,8},{10,11... | collective-permute-start | bytes 12296 | tf_op jit(solution)/shard_map/ppermute | solution.py:374
  10.9 3.7 %collective-permute-start.4 = (bf16[32,128]{1,0:T(8,128)(2,1)S(1)}, bf16[32,128]{1,0:T(8,128)(2,1)S(1)}, u32[]{:S(2)}, u32[]{:S(2)}) collective-permute-start(bf16[32,128]{1,0:T(8,128)(2,1)S(1)} %get-tuple-element.33), channel_id=1, source_target_pairs={{0,2},{1,3},{2,0},{3,1},{4,6},{5,7},{6,4},{7,5},{8,10},{9,11},{10,... | collective-permute-start | bytes 24584 | tf_op jit(solution)/shard_map/ppermute | solution.py:374
  12.7 5.1 %collective-permute-start.6 = (bf16[32,128]{1,0:T(8,128)(2,1)S(1)}, bf16[32,128]{1,0:T(8,128)(2,1)S(1)}, u32[]{:S(2)}, u32[]{:S(2)}) collective-permute-start(bf16[32,128]{1,0:T(8,128)(2,1)S(1)} %get-tuple-element.33), channel_id=1, source_target_pairs={{0,6},{1,7},{2,4},{3,5},{4,2},{5,3},{6,0},{7,1},{8,14},{9,15},{10,... | collective-permute-start | bytes 24584 | tf_op jit(solution)/shard_map/ppermute | solution.py:374
  14.1 3.7 %collective-permute-start.5 = (bf16[32,128]{1,0:T(8,128)(2,1)S(1)}, bf16[32,128]{1,0:T(8,128)(2,1)S(1)}, u32[]{:S(2)}, u32[]{:S(2)}) collective-permute-start(bf16[32,128]{1,0:T(8,128)(2,1)S(1)} %get-tuple-element.33), channel_id=1, source_target_pairs={{0,4},{1,5},{2,6},{3,7},{4,0},{5,1},{6,2},{7,3},{8,12},{9,13},{10,... | collective-permute-start | bytes 24584 | tf_op jit(solution)/shard_map/ppermute | solution.py:374
  17.8 4.5 %copy-start.2 = (s32[128]{0:T(128)S(1)}, s32[128]{0:T(128)}, u32[]{:S(2)}) copy-start(s32[128]{0:T(128)} %param.6) | copy-start | bytes 1540
  17.8 4.5 %copy-start.3 = (f32[128]{0:T(128)S(1)}, f32[128]{0:T(128)}, u32[]{:S(2)}) copy-start(f32[128]{0:T(128)} %param.7) | copy-start | bytes 1540
  17.8 7.6 %collective-permute-start.9 = (bf16[128,128]{1,0:T(8,128)(2,1)S(1)}, bf16[128,128]{1,0:T(8,128)(2,1)S(1)}, u32[]{:S(2)}, u32[]{:S(2)}) collective-permute-start(bf16[128,128]{1,0:T(8,128)(2,1)S(1)} %constant_dynamic-update-slice_fusion.2.refs_2_), channel_id=1, source_target_pairs={{0,24},{1,25},{2,26},{3,27},{4,28},{5,29},{6,30},{7,31},{8,16},{9,... | collective-permute-start | bytes 98312 | tf_op jit(solution)/shard_map/ppermute | solution.py:374
  21.3 5.5 %collective-permute-start.8 = (bf16[128,128]{1,0:T(8,128)(2,1)S(1)}, bf16[128,128]{1,0:T(8,128)(2,1)S(1)}, u32[]{:S(2)}, u32[]{:S(2)}) collective-permute-start(bf16[128,128]{1,0:T(8,128)(2,1)S(1)} %constant_dynamic-update-slice_fusion.2.refs_2_), channel_id=1, source_target_pairs={{0,16},{1,17},{2,18},{3,19},{4,20},{5,21},{6,22},{7,23},{8,24},{9,... | collective-permute-start | bytes 98312 | tf_op jit(solution)/shard_map/ppermute | solution.py:374
  21.3 5.5 %collective-permute-start.7 = (bf16[128,128]{1,0:T(8,128)(2,1)S(1)}, bf16[128,128]{1,0:T(8,128)(2,1)S(1)}, u32[]{:S(2)}, u32[]{:S(2)}) collective-permute-start(bf16[128,128]{1,0:T(8,128)(2,1)S(1)} %constant_dynamic-update-slice_fusion.2.refs_2_), channel_id=1, source_target_pairs={{0,8},{1,9},{2,10},{3,11},{4,12},{5,13},{6,14},{7,15},{8,0},{9,1},... | collective-permute-start | bytes 98312 | tf_op jit(solution)/shard_map/ppermute | solution.py:374
  23.9 6.1 %collective-permute-start.2 = (bf16[128,512]{1,0:T(8,128)(2,1)S(1)}, bf16[128,512]{1,0:T(8,128)(2,1)S(1)}, u32[]{:S(2)}, u32[]{:S(2)}) collective-permute-start(bf16[128,512]{1,0:T(8,128)(2,1)S(1)} %compact.1.refs_2_), channel_id=1, source_target_pairs={{0,8},{1,9},{2,10},{3,11},{4,12},{5,13},{6,14},{7,15},{8,0},{9,1},... | collective-permute-start | bytes 393224 | tf_op jit(solution)/shard_map/ppermute | solution.py:374
  25.0 5.2 %collective-permute-start.1 = (bf16[128,512]{1,0:T(8,128)(2,1)S(1)}, bf16[128,512]{1,0:T(8,128)(2,1)S(1)}, u32[]{:S(2)}, u32[]{:S(2)}) collective-permute-start(bf16[128,512]{1,0:T(8,128)(2,1)S(1)} %compact.1.refs_2_), channel_id=1, source_target_pairs={{0,4},{1,5},{2,6},{3,7},{4,0},{5,1},{6,2},{7,3},{8,12},{9,13},{10,... | collective-permute-start | bytes 393224 | tf_op jit(solution)/shard_map/ppermute | solution.py:374
  25.5 5.0 %collective-permute-start = (bf16[128,512]{1,0:T(8,128)(2,1)S(1)}, bf16[128,512]{1,0:T(8,128)(2,1)S(1)}, u32[]{:S(2)}, u32[]{:S(2)}) collective-permute-start(bf16[128,512]{1,0:T(8,128)(2,1)S(1)} %compact.1.refs_2_), channel_id=1, source_target_pairs={{0,2},{1,3},{2,0},{3,1},{4,6},{5,7},{6,4},{7,5},{8,10},{9,11},{10,... | collective-permute-start | bytes 393224 | tf_op jit(solution)/shard_map/ppermute | solution.py:374
  29.9 2.2 %collective-permute-start.10 = (bf16[128,512]{1,0:T(8,128)(2,1)S(1)}, bf16[128,512]{1,0:T(8,128)(2,1)S(1)}, u32[]{:S(2)}, u32[]{:S(2)}) collective-permute-start(bf16[128,512]{1,0:T(8,128)(2,1)S(1)} %compact.1.refs_2_), channel_id=1, source_target_pairs={{0,1},{1,0},{2,3},{3,2},{4,5},{5,4},{6,7},{7,6},{8,9},{9,8},{10,11... | collective-permute-start | bytes 393224 | tf_op jit(solution)/shard_map/ppermute | solution.py:374
  30.5 1.9 %copy-start = (bf16[128,4096]{1,0:T(8,128)(2,1)S(1)}, bf16[128,4096]{1,0:T(8,128)(2,1)}, u32[]{:S(2)}) copy-start(bf16[128,4096]{1,0:T(8,128)(2,1)} %slab_ref.1) | copy-start | bytes 3145732
  30.5 1.9 %copy-start.1 = (bf16[128,128]{1,0:T(8,128)(2,1)S(1)}, bf16[128,128]{1,0:T(8,128)(2,1)}, u32[]{:S(2)}) copy-start(bf16[128,128]{1,0:T(8,128)(2,1)} %cross_ref.1) | copy-start | bytes 98308
  30.5 1.6 %collective-permute-start.11 = (bf16[128,512]{1,0:T(8,128)(2,1)S(1)}, bf16[128,512]{1,0:T(8,128)(2,1)S(1)}, u32[]{:S(2)}, u32[]{:S(2)}) collective-permute-start(bf16[128,512]{1,0:T(8,128)(2,1)S(1)} %collective-permute-done.refs_3_), channel_id=1, source_target_pairs={{0,1},{1,0},{2,3},{3,2},{4,5},{5,4},{6,7},{7,6},{8,9},{9,8},{10,11... | collective-permute-start | bytes 393224 | tf_op jit(solution)/shard_map/ppermute | solution.py:374
  30.6 1.6 %collective-permute-start.12 = (bf16[128,512]{1,0:T(8,128)(2,1)S(1)}, bf16[128,512]{1,0:T(8,128)(2,1)S(1)}, u32[]{:S(2)}, u32[]{:S(2)}) collective-permute-start(bf16[128,512]{1,0:T(8,128)(2,1)S(1)} %collective-permute-done.1.refs_4_), channel_id=1, source_target_pairs={{0,1},{1,0},{2,3},{3,2},{4,5},{5,4},{6,7},{7,6},{8,9},{9,8},{10,11... | collective-permute-start | bytes 393224 | tf_op jit(solution)/shard_map/ppermute | solution.py:374
  31.0 1.3 %collective-permute-start.13 = (bf16[128,512]{1,0:T(8,128)(2,1)S(1)}, bf16[128,512]{1,0:T(8,128)(2,1)S(1)}, u32[]{:S(2)}, u32[]{:S(2)}) collective-permute-start(bf16[128,512]{1,0:T(8,128)(2,1)S(1)} %collective-permute-done.2.refs_5_), channel_id=1, source_target_pairs={{0,1},{1,0},{2,3},{3,2},{4,5},{5,4},{6,7},{7,6},{8,9},{9,8},{10,11... | collective-permute-start | bytes 393224 | tf_op jit(solution)/shard_map/ppermute | solution.py:374
